TPU v7x, 256 devices: a whole 4x4x8 slice. The times are simulated.
256 devices in a mesh: tm: 32 (over z, x), dp: 8 (over y, core).
Axes of the slice: x: 4, y: 4, z: 8, core: 2. Of those that a mesh axis runs over, the one named last changes fastest.
Arguments:
- frames: bfloat16 [8, 4096, 1024], P('dp', 'tm'), may hold values from -6 to 6
- grad_frames: bfloat16 [8, 4096, 1024], P('dp', 'tm'), may hold values from -6 to 6
- w_qkv: bfloat16 [1024, 2304], replicated, may hold values from -0.1875 to 0.1875
- w_out: bfloat16 [1024, 768], replicated, may hold values from -0.21875 to 0.21875
Outputs:
- grad_input: bfloat16 [8, 4096, 1024], P('dp', 'tm')
- grad_qkv: float32 [1024, 2304], P('tm')
- grad_out: float32 [1024, 768], P('tm')
All inputs are finite; a program needn't handle non-finite values.
Results may differ from a plain program's by a relative error of at most 0.014.
Values sent between devices are 32-bit elements; how exact they have to be, the bound alone decides.
No kernel may reach another device: no remote copies, remote signals or barrier semaphores. Data moves between devices by JAX's collectives and lax.ppermute only.
A program may use at most 64 MiB of HBM per device.

v0:
```python
import jax
import jax.numpy as jnp
from jax import lax
from jax.sharding import Mesh
from jax.sharding import PartitionSpec as P

HEADS = 12
HEAD = 64
BLOCK = 128
TM = ("tm_0", "tm_1")


def filled_with(value, identity):
    return jax.tree.map(
        lambda part, zero: jnp.zeros_like(part) + jnp.asarray(zero, part.dtype), value, identity
    )


def carried_in(value, axes, combine, identity, reverse):
    before = start = filled_with(value, identity)
    running = value
    for axis in reversed(axes):
        peers, here = (lax.axis_size(axis), lax.axis_index(axis))
        pieces = jax.tree.map(lambda part: lax.all_gather(part, axis), running)
        inside, running = (start, start)
        for k in reversed(range(peers)) if reverse else range(peers):
            passed = k > here if reverse else k < here
            running = combine(running, jax.tree.map(lambda part: part[k], pieces))
            inside = jax.tree.map(lambda new, old: jnp.where(passed, new, old), running, inside)
        before = combine(inside, before)
    return before


def summed_rows(running, axes):
    for axis in axes:
        running = lax.psum_scatter(running, axis, scatter_dimension=0, tiled=True)
    return running


def over_pieces(value, axis):
    return lax.all_gather(value, axis).sum(0)


def features(a):
    return jnp.where(a > 0, a + 1.0, jnp.exp(jnp.minimum(a, 0.0)))


def slope(a):
    return jnp.where(a > 0, 1.0, jnp.exp(jnp.minimum(a, 0.0)))


def add_pairs(earlier, later):
    return (earlier[0] + later[0], earlier[1] + later[1])


def per_device(frames, grad_frames, w_qkv, w_out):
    f32 = jnp.float32
    bf = jnp.bfloat16
    x = frames[0]
    dy = grad_frames[0]
    rows = x.shape[0]
    inner = HEADS * HEAD
    qkv = jnp.dot(x, w_qkv, preferred_element_type=f32).astype(bf)
    q = qkv[:, :inner].astype(f32)
    k = qkv[:, inner : 2 * inner].astype(f32)
    fq = features(q).astype(bf)
    fk = features(k).astype(bf)
    v = qkv[:, 2 * inner :]
    g = jnp.dot(dy, w_out, preferred_element_type=f32).astype(bf)
    nblk = rows // BLOCK
    shape4 = (nblk, BLOCK, HEADS, HEAD)
    fqb, fkb, vb, gb = (
        fq.reshape(shape4),
        fk.reshape(shape4),
        v.reshape(shape4),
        g.reshape(shape4),
    )
    mask = jnp.tril(jnp.ones((BLOCK, BLOCK), bool))
    state_add = jnp.einsum("nshd,nshe->nhde", fkb, vb, preferred_element_type=f32)
    norm_add = jnp.sum(fkb.astype(f32), 1)
    zeros_state = jnp.zeros((HEADS, HEAD, HEAD), f32)
    zeros_norm = jnp.zeros((HEADS, HEAD), f32)
    state_pre, norm_pre = carried_in(
        (jnp.sum(state_add, 0), jnp.sum(norm_add, 0)),
        TM,
        add_pairs,
        (zeros_state, zeros_norm),
        False,
    )

    def forward(carry, item_list):
        running_state, running_norm = carry
        (
            query_feature_map,
            value_rows,
            output_gradient_rows,
            state_increment,
            norm_increment,
            key_feature_map,
        ) = item_list
        fq32 = query_feature_map.astype(f32)
        g32 = output_gradient_rows.astype(f32)
        block_state = running_state.astype(bf)
        scores = jnp.where(
            mask,
            jnp.einsum(
                "thd,shd->hts", query_feature_map, key_feature_map, preferred_element_type=f32
            ),
            0.0,
        )
        den = scores.sum(-1).T + jnp.sum(fq32 * running_norm[None], -1)
        weights = scores.astype(bf)
        num = jnp.einsum(
            "hts,she->the", weights, value_rows, preferred_element_type=f32
        ) + jnp.einsum("thd,hde->the", query_feature_map, block_state, preferred_element_type=f32)
        ratio = num / den[..., None]
        attention_block = ratio.astype(bf)
        numerator_gradient = (g32 / den[..., None]).astype(bf)
        denominator_gradient = -jnp.sum(g32 * ratio, -1) / den
        block_score_gradient = jnp.einsum(
            "thd,the->hde", query_feature_map, numerator_gradient, preferred_element_type=f32
        )
        block_normalizer_gradient = jnp.sum(denominator_gradient[..., None] * fq32, 0)
        return (
            (running_state + state_increment, running_norm + norm_increment),
            (
                attention_block,
                block_state,
                running_norm,
                numerator_gradient,
                denominator_gradient,
                block_score_gradient,
                block_normalizer_gradient,
            ),
        )

    _, outs = lax.scan(forward, (state_pre, norm_pre), (fqb, vb, gb, state_add, norm_add, fkb))
    (
        attention_block,
        block_state,
        running_norm,
        numerator_gradient,
        denominator_gradient,
        block_score_gradient,
        block_normalizer_gradient,
    ) = outs
    dstate_suf, dnorm_suf = carried_in(
        (jnp.sum(block_score_gradient, 0), jnp.sum(block_normalizer_gradient, 0)),
        TM,
        add_pairs,
        (zeros_state, zeros_norm),
        True,
    )

    def backward(carry, item_list):
        dstate, dnorm = carry
        query_feature_map, key_feature_map, value_rows, sb, nz, dn, dd, dsb, dzb = item_list
        dstate_b = dstate.astype(bf)
        scores = jnp.where(
            mask,
            jnp.einsum(
                "thd,shd->hts", query_feature_map, key_feature_map, preferred_element_type=f32
            ),
            0.0,
        )
        weights = scores.astype(bf)
        dscore = (
            jnp.einsum("the,she->hts", dn, value_rows, preferred_element_type=f32)
            + dd.T[:, :, None]
        )
        dscore = jnp.where(mask, dscore, 0.0).astype(bf)
        dfq = (
            jnp.einsum("hts,shd->thd", dscore, key_feature_map, preferred_element_type=f32)
            + jnp.einsum("the,hde->thd", dn, sb, preferred_element_type=f32)
            + dd[..., None] * nz[None]
        )
        dfk = (
            jnp.einsum("hts,thd->shd", dscore, query_feature_map, preferred_element_type=f32)
            + jnp.einsum("she,hde->shd", value_rows, dstate_b, preferred_element_type=f32)
            + dnorm[None]
        )
        dv = jnp.einsum("hts,the->she", weights, dn, preferred_element_type=f32) + jnp.einsum(
            "shd,hde->she", key_feature_map, dstate_b, preferred_element_type=f32
        )
        return ((dstate + dsb, dnorm + dzb), (dfq, dfk, dv))

    _, grads = lax.scan(
        backward,
        (dstate_suf, dnorm_suf),
        (
            fqb,
            fkb,
            vb,
            block_state,
            running_norm,
            numerator_gradient,
            denominator_gradient,
            block_score_gradient,
            block_normalizer_gradient,
        ),
        reverse=True,
    )
    dfq, dfk, dv = grads
    dq = dfq.reshape(rows, inner) * slope(q)
    dk = dfk.reshape(rows, inner) * slope(k)
    dqkv = jnp.concatenate([dq, dk, dv.reshape(rows, inner)], axis=1).astype(bf)
    dx = lax.dot_general(dqkv, w_qkv, (((1,), (1,)), ((), ())), preferred_element_type=f32).astype(
        bf
    )
    attn_rows = attention_block.reshape(rows, inner)
    part_qkv = lax.dot_general(x, dqkv, (((0,), (0,)), ((), ())), preferred_element_type=f32)
    part_out = lax.dot_general(dy, attn_rows, (((0,), (0,)), ((), ())), preferred_element_type=f32)
    summed = summed_rows(jnp.concatenate([part_qkv, part_out], axis=1), TM)
    summed = over_pieces(summed, "dp")
    return (dx[None], summed[:, : 3 * inner], summed[:, 3 * inner :])


def solution(mesh):
    torus = Mesh(mesh.devices.reshape(8, 4, mesh.shape["dp"]), ("tm_0", "tm_1", "dp"))
    placed = (P("dp", TM, None), P("dp", TM, None), P(), P())
    return jax.shard_map(
        per_device,
        mesh=torus,
        in_specs=placed,
        out_specs=(P("dp", TM, None), P(TM, None), P(TM, None)),
        check_vma=False,
    )
```

profile of v0, /device:TPU:1, one launch (start us, length us, event | category | flops | bytes accessed | tf_op | source)
XLA Modules:
  0.0 379.9 jit_solution(11483968225486463115)
XLA Ops:
  7.2 3.3 convolution_convert_fusion
  13.5 17.2 %all-gather = f32[48,64,64]{2,1,0:T(8,128)S(1)} all-gather(f32[12,64,64]{2,1,0:T(8,128)S(1)} %fusion.54), channel_id=2, replica_groups=mesh['tm_0'=8,'tm_1'=4,'dp'=8] {'tm_1'}, dimensions={0}, use_global_device_ids=true | all-gather | bytes 983040 | tf_op jit(solution)/shard_map/all_gather | solution.py:24
  31.7 2.1 fusion.8
  33.8 1.9 copy.50
  35.7 1.1 copy.51
  36.8 9.0 %all_gather.38 = f32[4,12,64]{2,1,0:T(8,128)S(1)} all-gather(f32[1,12,64]{2,1,0:T(8,128)S(1)} %reduce_sum.80), channel_id=1, replica_groups=mesh['tm_0'=8,'tm_1'=4,'dp'=8] {'tm_1'}, dimensions={0}, use_global_device_ids=true | all-gather | bytes 15360 | tf_op jit(solution)/shard_map/all_gather | solution.py:24
  45.9 24.2 %all_gather.39 = f32[8,12,64]{2,1,0:T(8,128)S(1)} all-gather(f32[1,12,64]{2,1,0:T(8,128)S(1)} %slice_add_fusion.37), channel_id=1, replica_groups=mesh['tm_0'=8,'tm_1'=4,'dp'=8] {'tm_0'}, dimensions={0}, use_global_device_ids=true | all-gather | bytes 27648 | tf_op jit(solution)/shard_map/all_gather | solution.py:24
  70.3 1.3 fusion.53
  73.8 7.1 %all-gather.7.cloned.1.call-done = f32[8,12,64,64]{3,2,1,0:T(8,128)} async-done(((f32[1,12,64,64]{3,2,1,0:T(8,128)}), f32[8,12,64,64]{3,2,1,0:T(8,128)}) %all-gather.7.cloned.1.call-update) | async-done | bytes 1572880 | tf_op jit(solution)/shard_map/all_gather | solution.py:24
  80.9 2.4 fusion.28
  83.4 1.6 fusion.52
  85.8 16.5 %all-gather.1 = f32[48,64,64]{2,1,0:T(8,128)S(1)} all-gather(f32[12,64,64]{2,1,0:T(8,128)S(1)} %fusion.57), channel_id=3, replica_groups=mesh['tm_0'=8,'tm_1'=4,'dp'=8] {'tm_1'}, dimensions={0}, use_global_device_ids=true | all-gather | bytes 983040 | tf_op jit(solution)/shard_map/all_gather | solution.py:24
  104.8 1.3 fusion.1
  106.1 1.3 fusion.55
  108.3 1.9 copy.57
  111.0 1.9 copy.59
  112.9 2.1 fusion.21
  115.1 9.9 %all_gather.44 = f32[4,12,64]{2,1,0:T(8,128)S(1)} all-gather(f32[1,12,64]{2,1,0:T(8,128)S(1)} %broadcast_in_dim.84), channel_id=1, replica_groups=mesh['tm_0'=8,'tm_1'=4,'dp'=8] {'tm_1'}, dimensions={0}, use_global_device_ids=true | all-gather | bytes 15360 | tf_op jit(solution)/shard_map/all_gather | solution.py:24
  125.0 20.9 %all_gather.45 = f32[8,12,64]{2,1,0:T(8,128)S(1)} all-gather(f32[1,12,64]{2,1,0:T(8,128)S(1)} %slice_add_fusion.27), channel_id=1, replica_groups=mesh['tm_0'=8,'tm_1'=4,'dp'=8] {'tm_0'}, dimensions={0}, use_global_device_ids=true | all-gather | bytes 27648 | tf_op jit(solution)/shard_map/all_gather | solution.py:24
  145.9 2.2 fusion.38
  148.1 2.1 fusion.56
  150.2 2.2 convolution_bitcast_fusion.1
  152.5 2.5 fusion.24
  155.6 1.0 fusion.15
  156.9 1.4 convolution_bitcast_fusion
  158.7 7.0 %pad_maximum_fusion = f32[1024,3072]{0,1:T(8,128)} fusion(f32[1024,768]{0,1:T(8,128)S(1)} %copy-done.1, f32[1024,2304]{0,1:T(8,128)S(1)} %convolution_bitcast_fusion), kind=kLoop, calls=%fused_computation | loop fusion | flops 3145728 | bytes 25165824 | tf_op jit(solution)/shard_map/concatenate | solution.py:213
  165.9 141.6 %reduce-scatter.5.cloned.1.call-done = f32[128,3072]{0,1:T(8,128)} async-done(((f32[1024,3072]{0,1:T(8,128)}), f32[128,3072]{0,1:T(8,128)}) %reduce-scatter.5.cloned.1.call-update) | async-done | bytes 1572880 | tf_op jit(solution)/shard_map/reduce_scatter | solution.py:36
  307.5 3.0 copy.72
  310.6 26.0 %reduce-scatter.7.cloned.1.call-done = f32[32,3072]{1,0:T(8,128)} async-done(((f32[128,3072]{1,0:T(8,128)}), f32[32,3072]{1,0:T(8,128)}) %reduce-scatter.7.cloned.1.call-update) | async-done | bytes 393232 | tf_op jit(solution)/shard_map/reduce_scatter | solution.py:36
  336.7 4.7 %fusion.9 = bf16[1,128,1024]{2,1,0:T(8,128)(2,1)} fusion(bf16[1024,2304]{1,0:T(8,128)(2,1)} %param.6, bf16[128,768]{1,0:T(8,128)(2,1)S(1)} %copy.63, bf16[128,768]{1,0:T(8,128)(2,1)S(1)} %fusion.15, bf16[128,768]{1,0:T(8,128)(2,1)S(1)} %copy-done.13), kind=kOutput, calls=%fused_computation.21 | convolution fusion | flops 605880320 | bytes 5570560 | tf_op jit(solution)/shard_map/dot_general | solution.py:207
  341.3 28.5 %all-gather.11.cloned.1.call-done = f32[256,3072]{1,0:T(8,128)} async-done(((f32[32,3072]{1,0:T(8,128)}), f32[256,3072]{1,0:T(8,128)}) %all-gather.11.cloned.1.call-update) | async-done | bytes 3145744 | tf_op jit(solution)/shard_map/all_gather | solution.py:41
  369.9 2.1 reduce_sum.85
  (85 shorter events, 14.3 us)
Async XLA Ops:
  7.2 24.5 %copy-start = (bf16[1024,768]{1,0:T(8,128)(2,1)S(1)}, bf16[1024,768]{1,0:T(8,128)(2,1)}, u32[]{:S(2)}) copy-start(bf16[1024,768]{1,0:T(8,128)(2,1)} %param.7) | copy-start | bytes 4718596
  7.2 73.7 %all-gather.7.cloned.1.call-start = ((), (), s32[]{:S(2)}) async-start(), calls=%async_computation.2 | async-start | bytes 3538944 | tf_op jit(solution)/shard_map/all_gather | solution.py:24
  10.5 0.8 copy-start.2
  12.6 0.7 copy-start.3
  31.6 120.9 %all-gather.9.cloned.1.call-start = ((), (), s32[]{:S(2)}) async-start(), calls=%async_computation.3 | async-start | bytes 3538944 | tf_op jit(solution)/shard_map/all_gather | solution.py:24
  70.1 2.7 copy-start.22
  70.3 13.0 %copy-start.19 = (f32[128,12]{0,1:T(8,128)}, f32[128,12]{0,1:T(8,128)S(1)}, u32[]{:S(2)}) copy-start(f32[128,12]{0,1:T(8,128)S(1)} %multiply_reduce_fusion.2) | copy-start | bytes 18436
  71.6 0.6 copy-start.21
  71.6 1.2 copy-start.7
  80.9 2.5 copy-start.16
  80.9 2.5 copy-start.17
  80.9 2.5 copy-start.20
  83.3 1.6 copy-start.14
  84.9 0.7 copy-start.5
  103.2 204.3 %reduce-scatter.5.cloned.1.call-start = ((), (), s32[]{:S(2)}) async-start(), calls=%async_computation.4 | async-start | bytes 14155776 | tf_op jit(solution)/shard_map/reduce_scatter | solution.py:36
  103.3 4.1 %copy-start.6 = (bf16[128,12,64]{0,2,1:T(8,128)(2,1)S(1)}, bf16[128,12,64]{0,2,1:T(8,128)(2,1)}, u32[]{:S(2)}) copy-start(bf16[128,12,64]{0,2,1:T(8,128)(2,1)} %copy-done.5) | copy-start | bytes 589828
  103.3 4.1 %copy-start.15 = (bf16[1,12,64,64]{3,2,1,0:T(8,128)(2,1)S(1)}, bf16[1,12,64,64]{3,2,1,0:T(8,128)(2,1)}, u32[]{:S(2)}) copy-start(bf16[1,12,64,64]{3,2,1,0:T(8,128)(2,1)} %copy-done.14) | copy-start | bytes 294916
  106.0 2.3 copy-start.8
  115.1 35.1 %copy-start.12 = (bf16[1,128,1024]{2,1,0:T(8,128)(2,1)S(1)}, bf16[1,128,1024]{2,1,0:T(8,128)(2,1)}, u32[]{:S(2)}) copy-start(bf16[1,128,1024]{2,1,0:T(8,128)(2,1)} %param.5) | copy-start | bytes 786436
  115.1 35.1 %copy-start.18 = (bf16[128,12,64]{0,2,1:T(8,128)(2,1)S(1)}, bf16[128,12,64]{0,2,1:T(8,128)(2,1)}, u32[]{:S(2)}) copy-start(bf16[128,12,64]{0,2,1:T(8,128)(2,1)} %get-tuple-element.75) | copy-start | bytes 589828
  152.5 2.5 copy-start.4
  152.5 2.5 copy-start.10
  152.5 2.8 copy-start.9
  155.2 1.6 copy-start.11
  155.3 1.6 copy-start.13
  156.8 1.9 copy-start.1
  165.8 170.8 %reduce-scatter.7.cloned.1.call-start = ((), (), s32[]{:S(2)}) async-start(), calls=%async_computation.6 | async-start | bytes 1966080 | tf_op jit(solution)/shard_map/reduce_scatter | solution.py:36
  310.5 59.3 %all-gather.11.cloned.1.call-start = ((), (), s32[]{:S(2)}) async-start(), calls=%async_computation.5 | async-start | bytes 3538944 | tf_op jit(solution)/shard_map/all_gather | solution.py:41
Sparse Core Ops, SparseCore 0:
  31.7 49.1 all-gather.6
  103.3 46.4 all-gather.8
  165.9 141.4 reduce-scatter.4
  310.7 25.9 reduce-scatter.6
  338.3 31.5 all-gather.10
where the time goes:
time: 381 us; the launch traced here: 380 us
  waiting for transfers between devices  203 us (53%)
  blocking collectives  97.7 us (26%)
  matrix products  26.3 us (7%)
  other arithmetic  22 us (6%)
  local copies, waits for them, and re-layouts  16.1 us (4%)
  between operations  14.2 us (4%)
    reduce_scatter x2, waiting for transfers between devices, summed_rows(): running = lax.psum_scatter(running, axis, scatter_dimension=0, tiled=True)  168 us
    all_gather x6, blocking collectives, carried_in(): pieces = jax.tree.map(lambda part: lax.all_gather(part, axis), running)  97.7 us
    all_gather x1, waiting for transfers between devices, over_pieces(): return lax.all_gather(value, axis).sum(0)  28.5 us
  transfers between devices with their start and end apart: 5, of which 4 were waited for; matrix products, arithmetic and copies ran while one was open for 8% of the time, Pallas kernels for 0%

commit v1 on v0

v1 whole, which is shorter than its diff:
```python
import functools

import jax
import jax.numpy as jnp
from jax import lax
from jax.experimental import pallas as pl
from jax.experimental.pallas import tpu as pltpu
from jax.sharding import Mesh
from jax.sharding import PartitionSpec as P

HEADS = 12
HEAD = 64
BLOCK = 128
PAIRS = HEADS // 2
INNER = HEADS * HEAD
TM = ("z", "x")
DP = ("y", "c")
F32 = jnp.float32
BF16 = jnp.bfloat16
VMEM_LIMIT = 40 * 1024 * 1024


def features(a):
    return jnp.where(a > 0, a + 1.0, jnp.exp(jnp.minimum(a, 0.0)))


def slope(a):
    return jnp.where(a > 0, 1.0, jnp.exp(jnp.minimum(a, 0.0)))


def low_lanes(shape):
    return lax.broadcasted_iota(jnp.int32, shape, len(shape) - 1) < HEAD


def split_pair(a):
    low = low_lanes(a.shape)
    zero = jnp.zeros_like(a)
    return jnp.where(low, a, zero), jnp.where(low, zero, a)


def block_diagonal(packed):
    first, second = split_pair(packed)
    return jnp.concatenate([first, second], axis=0)


def diagonal_blocks(m):
    return jnp.where(low_lanes((HEAD, 2 * HEAD)), m[:HEAD], m[HEAD:])


def mm(a, b):
    return lax.dot_general(a, b, (((1,), (0,)), ((), ())), preferred_element_type=F32)


def mm_bt(a, b):
    return lax.dot_general(a, b, (((1,), (1,)), ((), ())), preferred_element_type=F32)


def mm_at(a, b):
    return lax.dot_general(a, b, (((0,), (0,)), ((), ())), preferred_element_type=F32)


def causal():
    rows = lax.broadcasted_iota(jnp.int32, (BLOCK, BLOCK), 0)
    columns = lax.broadcasted_iota(jnp.int32, (BLOCK, BLOCK), 1)
    return columns <= rows


def project_kernel(x_ref, dy_ref, wq_ref, wk_ref, wv_ref, wo_ref, q_ref, k_ref, v_ref, g_ref, send_ref):
    step = pl.program_id(0)

    @pl.when(step == 0)
    def _():
        send_ref[...] = jnp.zeros_like(send_ref)

    x = x_ref[...]
    q_ref[...] = mm(x, wq_ref[...]).astype(BF16)
    k = mm(x, wk_ref[...]).astype(BF16)
    k_ref[...] = k
    v = mm(x, wv_ref[...]).astype(BF16)
    v_ref[...] = v
    g_ref[...] = mm(dy_ref[...], wo_ref[...]).astype(BF16)
    fk = features(k.astype(F32)).astype(BF16)
    for i in range(2):
        lanes = slice(128 * i, 128 * i + 128)
        state = diagonal_blocks(mm_at(fk[:, lanes], v[:, lanes]))
        norm = jnp.sum(fk[:, lanes].astype(F32), axis=0, keepdims=True)
        pair = 2 * step + i
        send_ref[pl.ds(4 * pair, 4), 0:16, :] = state.reshape(4, 16, 128)
        for t in range(32):
            send_ref[t, pl.ds(16 + pair, 1), :] = norm


def project(x, dy, w_qkv, w_out):
    rows, width = x.shape
    whole = pl.BlockSpec((rows, width), lambda i: (0, 0))
    column = lambda first: pl.BlockSpec((width, 256), lambda i: (0, first + i))
    out = pl.BlockSpec((rows, 256), lambda i: (0, i))
    return pl.pallas_call(
        project_kernel,
        grid=(3,),
        in_specs=[whole, whole, column(0), column(3), column(6), column(0)],
        out_specs=[out] * 4 + [pl.BlockSpec((32, 24, 128), lambda i: (0, 0, 0))],
        out_shape=[jax.ShapeDtypeStruct((rows, INNER), BF16)] * 4
        + [jax.ShapeDtypeStruct((32, 24, 128), F32)],
        compiler_params=pltpu.CompilerParams(vmem_limit_bytes=VMEM_LIMIT),
        name="project",
    )(x, dy, w_qkv, w_qkv, w_qkv, w_out)


def denominators_kernel(me_ref, got_ref, q_ref, k_ref, g_ref, send_ref, den_ref, norm_ref, w_ref):
    me = me_ref[0]
    carry = jnp.zeros((16, 128), F32)
    norms = jnp.zeros((8, 128), F32)
    for t in range(32):
        send_ref[t, 0:16, :] = carry
        carry = carry + got_ref[t, 0:16, :]
        norms = norms + jnp.where(t < me, got_ref[t, 16:24, :], 0.0)
    norm_ref[...] = norms
    mask = causal()
    for p in range(PAIRS):
        lanes = slice(128 * p, 128 * p + 128)
        fq32 = features(q_ref[:, lanes].astype(F32))
        fq = fq32.astype(BF16)
        fk = features(k_ref[:, lanes].astype(F32)).astype(BF16)
        fq_norm = fq.astype(F32) * norms[p : p + 1, :]
        sums = []
        for half, (rows, extra) in enumerate(zip(split_pair(fq), split_pair(fq_norm))):
            scores = jnp.where(mask, mm_bt(rows, fk), 0.0)
            w_ref[p, :, 128 * half : 128 * half + 128] = scores.astype(BF16)
            sums.append(jnp.sum(scores + extra, axis=1, keepdims=True))
        den = jnp.where(low_lanes((BLOCK, 128)), sums[0], sums[1])
        den_ref[:, lanes] = den
        dnum = (g_ref[:, lanes].astype(F32) / den).astype(BF16)
        dstate = diagonal_blocks(mm_at(fq, dnum))
        send_ref[4 * p : 4 * p + 4, 16:32, :] = dstate.reshape(4, 16, 128)
    send_ref[24:32, 16:32, :] = jnp.zeros((8, 16, 128), F32)


def in_vmem(n):
    return [pl.BlockSpec(memory_space=pltpu.VMEM)] * n


SCALARS = pl.BlockSpec(memory_space=pltpu.SMEM)


def denominators(me, got, q, k, g):
    return pl.pallas_call(
        denominators_kernel,
        in_specs=[SCALARS] + in_vmem(4),
        out_specs=in_vmem(4),
        out_shape=[
            jax.ShapeDtypeStruct((32, 32, 128), F32),
            jax.ShapeDtypeStruct((BLOCK, INNER), F32),
            jax.ShapeDtypeStruct((8, 128), F32),
            jax.ShapeDtypeStruct((PAIRS, BLOCK, 256), BF16),
        ],
        compiler_params=pltpu.CompilerParams(vmem_limit_bytes=VMEM_LIMIT),
        name="denominators",
    )(me, got, q, k, g)


def forward_kernel(
    got_ref, q_ref, k_ref, v_ref, g_ref, den_ref, norm_ref, w_ref, send_ref, out_ref, dq_ref, ds_ref
):
    carry = jnp.zeros((16, 128), F32)
    for t in reversed(range(32)):
        send_ref[t, 0:16, :] = carry
        carry = carry + got_ref[t, 16:32, :]
    mask = causal()
    low = low_lanes((BLOCK, 128))
    dnorms = []
    for p in range(PAIRS):
        lanes = slice(128 * p, 128 * p + 128)
        block, part = p // 3, slice(128 * (p % 3), 128 * (p % 3) + 128)
        q = q_ref[:, lanes].astype(F32)
        fq = features(q).astype(BF16)
        fk = features(k_ref[:, lanes].astype(F32)).astype(BF16)
        v = v_ref[:, lanes]
        g = g_ref[:, lanes].astype(F32)
        inverse = 1.0 / den_ref[:, lanes]
        state = block_diagonal(got_ref[4 * p : 4 * p + 4, 0:16, :].reshape(64, 128).astype(BF16))
        v_halves = jnp.concatenate(split_pair(v), axis=0)
        ratio = (mm(w_ref[p], v_halves) + mm(fq, state)) * inverse
        out_ref[2 + block, :, part] = ratio.astype(BF16).astype(F32)
        dnum = (g * inverse).astype(BF16)
        sums = [jnp.sum(a, axis=1, keepdims=True) for a in split_pair(g * ratio)]
        dden = -jnp.where(low, sums[0], sums[1]) * inverse
        ddens = (dden[:, 0:1], dden[:, 127:128])
        dnorms.append(jnp.sum(dden * fq.astype(F32), axis=0, keepdims=True))
        ds = [
            jnp.where(mask, mm_bt(rows, v) + column, 0.0).astype(BF16)
            for rows, column in zip(split_pair(dnum), ddens)
        ]
        ds_ref[p] = jnp.concatenate(ds, axis=0)
        dfq = (
            mm(jnp.concatenate(ds, axis=1), jnp.concatenate(split_pair(fk), axis=0))
            + mm_bt(dnum, state)
            + dden * norm_ref[p : p + 1, :]
        )
        dq = (dfq * slope(q)).astype(BF16)
        dq_ref[:, lanes] = dq
        out_ref[block, :, part] = dq.astype(F32)
    dnorm = jnp.concatenate(dnorms + [jnp.zeros((2, 128), F32)], axis=0)
    for t in range(32):
        send_ref[t, 16:24, :] = dnorm


def forward(got, q, k, v, g, den, norm, w):
    return pl.pallas_call(
        forward_kernel,
        in_specs=in_vmem(8),
        out_specs=in_vmem(4),
        out_shape=[
            jax.ShapeDtypeStruct((32, 24, 128), F32),
            jax.ShapeDtypeStruct((4, BLOCK, 384), F32),
            jax.ShapeDtypeStruct((BLOCK, INNER), BF16),
            jax.ShapeDtypeStruct((PAIRS, 256, 128), BF16),
        ],
        compiler_params=pltpu.CompilerParams(vmem_limit_bytes=VMEM_LIMIT),
        name="forward",
    )(got, q, k, v, g, den, norm, w)


def backward_kernel(
    me_ref, got_ref, q_ref, k_ref, v_ref, g_ref, den_ref, w_ref, ds_ref, out_ref, dkv_ref
):
    me = me_ref[0]
    dnorms = jnp.zeros((8, 128), F32)
    for t in range(32):
        dnorms = dnorms + jnp.where(t > me, got_ref[t, 16:24, :], 0.0)
    for p in range(PAIRS):
        lanes = slice(128 * p, 128 * p + 128)
        block, part = p // 3, slice(128 * (p % 3), 128 * (p % 3) + 128)
        fq = features(q_ref[:, lanes].astype(F32)).astype(BF16)
        k = k_ref[:, lanes].astype(F32)
        fk = features(k).astype(BF16)
        v = v_ref[:, lanes]
        dnum = (g_ref[:, lanes].astype(F32) * (1.0 / den_ref[:, lanes])).astype(BF16)
        dstate = block_diagonal(got_ref[4 * p : 4 * p + 4, 0:16, :].reshape(64, 128).astype(BF16))
        dfk = (
            mm_at(ds_ref[p], jnp.concatenate(split_pair(fq), axis=0))
            + mm_bt(v, dstate)
            + dnorms[p : p + 1, :]
        )
        dk = (dfk * slope(k)).astype(BF16)
        w = jnp.concatenate([w_ref[p, :, 0:128], w_ref[p, :, 128:256]], axis=0)
        dv = (mm_at(w, jnp.concatenate(split_pair(dnum), axis=0)) + mm(fk, dstate)).astype(BF16)
        out_ref[block, :, part] = dk.astype(F32)
        out_ref[2 + block, :, part] = dv.astype(F32)
        dkv_ref[:, lanes] = dk
        dkv_ref[:, slice(INNER + 128 * p, INNER + 128 * p + 128)] = dv


def backward(me, got, q, k, v, g, den, w, ds):
    return pl.pallas_call(
        backward_kernel,
        in_specs=[SCALARS] + in_vmem(8),
        out_specs=in_vmem(2),
        out_shape=[
            jax.ShapeDtypeStruct((4, BLOCK, 384), F32),
            jax.ShapeDtypeStruct((BLOCK, 2 * INNER), BF16),
        ],
        compiler_params=pltpu.CompilerParams(vmem_limit_bytes=VMEM_LIMIT),
        name="backward",
    )(me, got, q, k, v, g, den, w, ds)


def weights_kernel(y_ref, xdy_ref, first_ref, second_ref, out_ref):
    y = y_ref[0]
    columns = xdy_ref.shape[-1]
    x = xdy_ref[:, 0].reshape(4 * BLOCK, columns).astype(BF16)
    other = xdy_ref[:, y // 2].reshape(4 * BLOCK, columns).astype(BF16)
    first = mm_at(other, first_ref[...].reshape(4 * BLOCK, 384).astype(BF16))
    second = mm_at(x, second_ref[...].reshape(4 * BLOCK, 384).astype(BF16))
    blocks = columns // 32
    first = first.reshape(blocks, 2, 16, 384)
    second = second.reshape(blocks, 2, 16, 384)
    for c in range(2):
        out_ref[c, :, :, 0:384] = first[:, c]
        out_ref[c, :, :, 384:768] = second[:, c]


def weights(y, xdy, first, second):
    blocks = pl.BlockSpec((4, BLOCK, 384), lambda i: (0, 0, 0))
    return pl.pallas_call(
        weights_kernel,
        grid=(4,),
        in_specs=[
            SCALARS,
            pl.BlockSpec((4, 2, BLOCK, 256), lambda i: (0, 0, 0, i)),
            blocks,
            blocks,
        ],
        out_specs=pl.BlockSpec((2, 8, 16, 768), lambda i: (0, i, 0, 0)),
        out_shape=jax.ShapeDtypeStruct((2, 32, 16, 768), F32),
        compiler_params=pltpu.CompilerParams(vmem_limit_bytes=VMEM_LIMIT),
        name="weights",
    )(y, xdy, first, second)


def swap(a, axes):
    return lax.all_to_all(a, axes, 0, 0, tiled=True)


def per_device(frames, grad_frames, w_qkv, w_out):
    x = frames[0]
    dy = grad_frames[0]
    me = lax.axis_index(TM).reshape(1).astype(jnp.int32)
    y = lax.axis_index("y").reshape(1).astype(jnp.int32)
    xdy = lax.all_gather(jnp.stack([x.astype(F32), dy.astype(F32)]), "y")
    q, k, v, g, send = project(x, dy, w_qkv, w_out)
    got = swap(send, TM)
    send, den, norm, w = denominators(me, got, q, k, g)
    got = swap(send, TM)
    send, first, dq, ds = forward(got, q, k, v, g, den, norm, w)
    got = swap(send, TM)
    second, dkv = backward(me, got, q, k, v, g, den, w, ds)
    dqkv = jnp.concatenate([dq, dkv], axis=1)
    dx = lax.dot_general(dqkv, w_qkv, (((1,), (1,)), ((), ())), preferred_element_type=F32).astype(BF16)
    first = swap(first, "y")
    second = swap(second, "y")
    part = swap(weights(y, xdy, first, second), "c")
    part = part[0] + part[1]
    total = jnp.sum(swap(part, TM), axis=0)
    pieces = swap(jnp.broadcast_to(total[None], (8,) + total.shape), DP)
    pieces = pieces.reshape(4, 32, 768)
    half = 384
    grad_qkv = jnp.concatenate(
        [pieces[0, :, :half], pieces[1, :, :half]] + [pieces[i, :, half:] for i in range(4)], axis=1
    )
    grad_out = jnp.concatenate([pieces[2, :, :half], pieces[3, :, :half]], axis=1)
    return dx[None], grad_qkv, grad_out


def solution(mesh):
    torus = Mesh(mesh.devices.reshape(8, 4, 4, 2), TM + DP)
    rows = P(DP, TM, None)
    return jax.shard_map(
        per_device,
        mesh=torus,
        in_specs=(rows, rows, P(), P()),
        out_specs=(rows, P(TM, None), P(TM, None)),
        check_vma=False,
    )
```

time: 381 us -> 194 us (0.51)
  waiting for transfers between devices: 203 us -> 32.5 us
  starting transfers between devices: 0.2 us -> 25.3 us
  matrix products: 26.3 us -> 4.67 us
  other arithmetic: 22 us -> 3.18 us
  Pallas kernels: 0 us -> 11.9 us
  local copies, waits for them, and re-layouts: 16.1 us -> 5.41 us
    reduce_scatter x2 -> x0, waiting for transfers between devices: 168 us -> none  [summed_rows(): running = lax.psum_scatter(running, axis, scatter_dimension=0, tiled=True)]
    all_gather x6 -> x0, blocking collectives: 97.7 us -> none  [carried_in(): pieces = jax.tree.map(lambda part: lax.all_gather(part, axis), running)]
    all_to_all x0 -> x4, blocking collectives: none -> 96.3 us  [swap(): return lax.all_to_all(a, axes, 0, 0, tiled=True)]
    all_gather x3 -> x1, waiting for transfers between devices: 35.6 us -> 0.01 us  [per_device(): xdy = lax.all_gather(jnp.stack([x.astype(F32), dy.astype(F32)]), 'y')]
    all_to_all x0 -> x4, waiting for transfers between devices: none -> 32.5 us  [swap(): return lax.all_to_all(a, axes, 0, 0, tiled=True)]
    all_to_all x0 -> x4, starting transfers between devices: none -> 25.2 us  [swap(): return lax.all_to_all(a, axes, 0, 0, tiled=True)]
    dot_general x16 -> x0, matrix products: 21.7 us -> none  [the longest x1 3.31 us: per_device(): qkv = jnp.dot(x, w_qkv, preferred_element_type=f32).astype(bf)]
    pallas_call x0 -> x5, Pallas kernels: none -> 11.9 us  [the longest x1 3.18 us: project(): pl.pallas_call(project_kernel, grid=(3,), in_specs=[whole, whole, column(...]
  transfers between devices with their start and end apart: 5 -> 5, of which waited for: 4 -> 4; matrix products, arithmetic and copies ran while one was open for 8% -> 2% of each run, Pallas kernels for 0% -> 5%
where the time goes in v1:
time: 194 us; the launch traced here: 193 us
  blocking collectives  96.3 us (50%)
  waiting for transfers between devices  32.5 us (17%)
  starting transfers between devices  25.3 us (13%)
  between operations  14.2 us (7%)
  Pallas kernels  11.9 us (6%)
  local copies, waits for them, and re-layouts  5.41 us (3%)
  matrix products  4.67 us (2%)
  other arithmetic  3.18 us (2%)
    all_to_all x4, blocking collectives, swap(): return lax.all_to_all(a, axes, 0, 0, tiled=True)  96.3 us
    all_to_all x4, waiting for transfers between devices, swap(): return lax.all_to_all(a, axes, 0, 0, tiled=True)  32.5 us
    all_to_all x4, starting transfers between devices, swap(): return lax.all_to_all(a, axes, 0, 0, tiled=True)  25.2 us
    dot_general x1, matrix products, per_device(): lax.dot_general(dqkv, w_qkv, (((1,), (1,)), ((), ())), preferred_element_...  4.67 us
    unnamed x21, local copies, waits for them, and re-layouts  4.62 us
  transfers between devices with their start and end apart: 5, of which 4 were waited for; matrix products, arithmetic and copies ran while one was open for 2% of the time, Pallas kernels for 5%

profile of v1, /device:TPU:1, one launch (start us, length us, event | category | flops | bytes accessed | tf_op | source)
XLA Modules:
  0.0 193.5 jit_solution(10063164441275389075)
XLA Ops:
  7.2 0.0 all-gather.3.cloned.1.call-start
  7.2 2.2 %maximum_convert_fusion = f32[2,128,1024]{2,1,0:T(8,128)} fusion(bf16[1,128,1024]{2,1,0:T(8,128)(2,1)} %param.5, bf16[1,128,1024]{2,1,0:T(8,128)(2,1)} %param.4), kind=kLoop, calls=%fused_computation.7 | loop fusion | flops 524288 | bytes 1572864 | tf_op jit(solution)/shard_map/all_gather | solution.py:310
  9.5 0.0 all-gather.3.cloned.1.call-update
  9.5 0.0 copy-done.4
  9.5 0.0 copy-done.3
  9.5 0.0 copy-start
  9.5 2.3 %copy-done = bf16[1024,2304]{1,0:T(8,128)(2,1)S(1)} copy-done((bf16[1024,2304]{1,0:T(8,128)(2,1)S(1)}, bf16[1024,2304]{1,0:T(8,128)(2,1)}, u32[]{:S(2)}) %copy-start) | copy-done | bytes 4718616
  11.8 3.2 %project.1 = (bf16[128,768]{1,0:T(8,128)(2,1)S(1)}, bf16[128,768]{1,0:T(8,128)(2,1)S(1)}, bf16[128,768]{1,0:T(8,128)(2,1)S(1)}, bf16[128,768]{1,0:T(8,128)(2,1)S(1)}, f32[32,24,128]{2,1,0:T(8,128)}) custom-call(bf16[128,1024]{1,0:T(8,128)(2,1)S(1)} %bitcast.40, bf16[128,1024]{1,0:T(8,128)(2,1)S(1)} %bitcast.41, bf16[1024,2304]{1,0:T(8,128)(2,1)S(1)} %copy-done, ...), custom_call_target="tpu_custom_call" | custom-call | tf_op jit(solution)/shard_map/project/pallas_call | solution.py:98
  15.0 11.9 %all-to-all-start = ((f32[32,24,128]{2,1,0:T(8,128)}), f32[32,24,128]{2,1,0:T(8,128)S(1)}, u32[]{:S(2)}, u32[]{:S(2)}) async-start(f32[32,24,128]{2,1,0:T(8,128)} %get-tuple-element.18), calls=%async_computation | async-start | bytes 786432 | tf_op jit(solution)/shard_map/all_to_all | solution.py:302
  26.9 13.8 %all-to-all-done.got_ref = f32[32,24,128]{2,1,0:T(8,128)S(1)} async-done(((f32[32,24,128]{2,1,0:T(8,128)}), f32[32,24,128]{2,1,0:T(8,128)S(1)}, u32[]{:S(2)}, u32[]{:S(2)}) %all-to-all-start) | async-done | bytes 393248 | tf_op jit(solution)/shard_map/all_to_all | solution.py:302
  40.7 1.7 denominators.1
  42.5 20.1 %all_to_all.40.got_ref = f32[32,32,128]{2,1,0:T(8,128)S(1)} all-to-all(f32[32,32,128]{2,1,0:T(8,128)S(1)} %get-tuple-element.22), channel_id=1, replica_groups=mesh['z'=8,'x'=4,'y'=4,'c'=2] {'z','x'}, dimensions={0} | all-to-all | bytes 1048576 | tf_op jit(solution)/shard_map/all_to_all | solution.py:302
  62.5 3.1 %forward.1 = (f32[32,24,128]{2,1,0:T(8,128)S(1)}, f32[4,128,384]{2,1,0:T(8,128)}, bf16[128,768]{1,0:T(8,128)(2,1)S(1)}, bf16[6,256,128]{2,1,0:T(8,128)(2,1)S(1)}) custom-call(f32[32,32,128]{2,1,0:T(8,128)S(1)} %all_to_all.40.got_ref, bf16[128,768]{1,0:T(8,128)(2,1)S(1)} %get-tuple-element.19.q_ref, bf16[128,768]{1,0:T(8,128)(2,1)S(1)} %get-tuple-element.20.k_ref, ...), custom_call_target="tpu_custom_call" | custom-call | tf_op jit(solution)/shard_map/forward/pallas_call | solution.py:209
  65.6 18.9 %all_to_all.41.got_ref = f32[32,24,128]{2,1,0:T(8,128)S(1)} all-to-all(f32[32,24,128]{2,1,0:T(8,128)S(1)} %get-tuple-element.28), channel_id=1, replica_groups=mesh['z'=8,'x'=4,'y'=4,'c'=2] {'z','x'}, dimensions={0} | all-to-all | bytes 786432 | tf_op jit(solution)/shard_map/all_to_all | solution.py:302
  84.5 4.2 %all-to-all-start.3 = ((f32[4,128,384]{2,1,0:T(8,128)}), f32[4,128,384]{2,1,0:T(8,128)S(1)}, u32[]{:S(2)}, u32[]{:S(2)}) async-start(f32[4,128,384]{2,1,0:T(8,128)} %get-tuple-element.31), calls=%async_computation.3 | async-start | bytes 1572864 | tf_op jit(solution)/shard_map/all_to_all | solution.py:302
  88.7 1.4 backward.1
  90.1 7.0 %all-to-all-done.3.first_ref = f32[4,128,384]{2,1,0:T(8,128)S(1)} async-done(((f32[4,128,384]{2,1,0:T(8,128)}), f32[4,128,384]{2,1,0:T(8,128)S(1)}, u32[]{:S(2)}, u32[]{:S(2)}) %all-to-all-start.3) | async-done | bytes 786464 | tf_op jit(solution)/shard_map/all_to_all | solution.py:302
  97.1 3.5 %all-to-all-start.4 = ((f32[4,128,384]{2,1,0:T(8,128)}), f32[4,128,384]{2,1,0:T(8,128)S(1)}, u32[]{:S(2)}, u32[]{:S(2)}) async-start(f32[4,128,384]{2,1,0:T(8,128)} %get-tuple-element.32), calls=%async_computation.4 | async-start | bytes 1572864 | tf_op jit(solution)/shard_map/all_to_all | solution.py:302
  100.6 8.3 %all-to-all-done.4.second_ref = f32[4,128,384]{2,1,0:T(8,128)S(1)} async-done(((f32[4,128,384]{2,1,0:T(8,128)}), f32[4,128,384]{2,1,0:T(8,128)S(1)}, u32[]{:S(2)}, u32[]{:S(2)}) %all-to-all-start.4) | async-done | bytes 786464 | tf_op jit(solution)/shard_map/all_to_all | solution.py:302
  108.9 2.2 %copy-done.1 = f32[8,128,1024]{2,1,0:T(8,128)S(1)} copy-done((f32[8,128,1024]{2,1,0:T(8,128)S(1)}, f32[8,128,1024]{2,1,0:T(8,128)}, u32[]{:S(2)}) %copy-start.1) | copy-done | bytes 4194328
  111.1 2.5 %weights.1 = f32[2,32,16,768]{3,2,1,0:T(8,128)S(1)} custom-call(s32[1]{0:T(128)} %bitcast.4.y_ref, f32[4,2,128,1024]{3,2,1,0:T(8,128)S(1)} %bitcast.39, f32[4,128,384]{2,1,0:T(8,128)S(1)} %all-to-all-done.3.first_ref, f32[4,128,384]{2,1,0:T(8,128)S(1)} %all-to-all-done.4.second_ref), custom_call_target="tpu_custom_call" | custom-call | tf_op jit(solution)/shard_map/weights/pallas_call | solution.py:285
  113.6 11.9 %all_to_all.42 = f32[2,32,16,768]{3,2,1,0:T(8,128)S(1)} all-to-all(f32[2,32,16,768]{3,2,1,0:T(8,128)S(1)} %weights.1), channel_id=1, replica_groups=mesh['z'=8,'x'=4,'y'=4,'c'=2] {'c'}, dimensions={0} | all-to-all | bytes 6291456 | tf_op jit(solution)/shard_map/all_to_all | solution.py:302
  125.5 0.2 fusion
  125.7 45.5 %all_to_all.43 = f32[32,16,768]{2,1,0:T(8,128)S(1)} all-to-all(f32[32,16,768]{2,1,0:T(8,128)S(1)} %fusion), channel_id=1, replica_groups=mesh['z'=8,'x'=4,'y'=4,'c'=2] {'z','x'}, dimensions={0} | all-to-all | bytes 3145728 | tf_op jit(solution)/shard_map/all_to_all | solution.py:302
  171.2 0.1 reduce_sum.9
  171.2 0.8 broadcast_in_dim.10
  172.0 5.7 %all-to-all-start.7 = ((f32[8,16,768]{2,1,0:T(8,128)}), f32[8,16,768]{2,1,0:T(8,128)S(1)}, u32[]{:S(2)}, u32[]{:S(2)}) async-start(f32[8,16,768]{2,1,0:T(8,128)} %broadcast_in_dim.10), calls=%async_computation.7 | async-start | bytes 786432 | tf_op jit(solution)/shard_map/all_to_all | solution.py:302
  177.7 4.7 %fusion.1 = bf16[1,128,1024]{2,1,0:T(8,128)(2,1)} fusion(bf16[1024,2304]{1,0:T(8,128)(2,1)} %wv_ref.1, bf16[128,1536]{1,0:T(8,128)(2,1)S(1)} %get-tuple-element.30, bf16[128,768]{1,0:T(8,128)(2,1)S(1)} %copy-done.6), kind=kOutput, calls=%fused_computation.3 | convolution fusion | flops 605290496 | bytes 5570560 | tf_op jit(solution)/shard_map/dot_general | solution.py:319
  182.4 3.4 %all-to-all-done.7 = f32[8,16,768]{2,1,0:T(8,128)S(1)} async-done(((f32[8,16,768]{2,1,0:T(8,128)}), f32[8,16,768]{2,1,0:T(8,128)S(1)}, u32[]{:S(2)}, u32[]{:S(2)}) %all-to-all-start.7) | async-done | bytes 393248 | tf_op jit(solution)/shard_map/all_to_all | solution.py:302
  185.9 0.0 copy-start.7
  185.9 0.7 pad_maximum_fusion
  186.6 0.0 copy-done.7
  (17 shorter events, 0.1 us)
Async XLA Ops:
  7.2 2.3 %copy-start.4 = (bf16[1,128,1024]{2,1,0:T(8,128)(2,1)S(1)}, bf16[1,128,1024]{2,1,0:T(8,128)(2,1)}, u32[]{:S(2)}) copy-start(bf16[1,128,1024]{2,1,0:T(8,128)(2,1)} %param.5) | copy-start | bytes 786436
  7.2 2.3 %copy-start.3 = (bf16[1,128,1024]{2,1,0:T(8,128)(2,1)S(1)}, bf16[1,128,1024]{2,1,0:T(8,128)(2,1)}, u32[]{:S(2)}) copy-start(bf16[1,128,1024]{2,1,0:T(8,128)(2,1)} %param.4) | copy-start | bytes 786436
  7.2 2.3 %copy-start.2 = (bf16[1024,768]{1,0:T(8,128)(2,1)S(1)}, bf16[1024,768]{1,0:T(8,128)(2,1)}, u32[]{:S(2)}) copy-start(bf16[1024,768]{1,0:T(8,128)(2,1)} %wo_ref.1) | copy-start | bytes 4718596
  7.2 101.7 %all-gather.3.cloned.1.call-start = ((), (), s32[]{:S(2)}) async-start(), calls=%async_computation.8 | async-start | bytes 5242880 | tf_op jit(solution)/shard_map/all_gather | solution.py:310
  9.5 2.3 %copy-start = (bf16[1024,2304]{1,0:T(8,128)(2,1)S(1)}, bf16[1024,2304]{1,0:T(8,128)(2,1)}, u32[]{:S(2)}) copy-start(bf16[1024,2304]{1,0:T(8,128)(2,1)} %wv_ref.1) | copy-start | bytes 14155780
  15.0 25.7 %all-to-all-start = ((f32[32,24,128]{2,1,0:T(8,128)}), f32[32,24,128]{2,1,0:T(8,128)S(1)}, u32[]{:S(2)}, u32[]{:S(2)}) async-start(f32[32,24,128]{2,1,0:T(8,128)} %get-tuple-element.18), calls=%async_computation | async-start | bytes 786432 | tf_op jit(solution)/shard_map/all_to_all | solution.py:302
  65.6 18.9 %copy-start.5 = (bf16[128,768]{1,0:T(8,128)(2,1)}, bf16[128,768]{1,0:T(8,128)(2,1)S(1)}, u32[]{:S(2)}) copy-start(bf16[128,768]{1,0:T(8,128)(2,1)S(1)} %get-tuple-element.27) | copy-start | bytes 589828
  84.5 12.6 %all-to-all-start.3 = ((f32[4,128,384]{2,1,0:T(8,128)}), f32[4,128,384]{2,1,0:T(8,128)S(1)}, u32[]{:S(2)}, u32[]{:S(2)}) async-start(f32[4,128,384]{2,1,0:T(8,128)} %get-tuple-element.31), calls=%async_computation.3 | async-start | bytes 1572864 | tf_op jit(solution)/shard_map/all_to_all | solution.py:302
  97.1 11.8 %all-to-all-start.4 = ((f32[4,128,384]{2,1,0:T(8,128)}), f32[4,128,384]{2,1,0:T(8,128)S(1)}, u32[]{:S(2)}, u32[]{:S(2)}) async-start(f32[4,128,384]{2,1,0:T(8,128)} %get-tuple-element.32), calls=%async_computation.4 | async-start | bytes 1572864 | tf_op jit(solution)/shard_map/all_to_all | solution.py:302
  108.9 2.2 %copy-start.1 = (f32[8,128,1024]{2,1,0:T(8,128)S(1)}, f32[8,128,1024]{2,1,0:T(8,128)}, u32[]{:S(2)}) copy-start(f32[8,128,1024]{2,1,0:T(8,128)} %all-gather.3.cloned.1.call-done) | copy-start | bytes 12582916
  171.2 6.6 %copy-start.6 = (bf16[128,768]{1,0:T(8,128)(2,1)S(1)}, bf16[128,768]{1,0:T(8,128)(2,1)}, u32[]{:S(2)}) copy-start(bf16[128,768]{1,0:T(8,128)(2,1)} %copy-done.5) | copy-start | bytes 589828
  172.0 13.8 %all-to-all-start.7 = ((f32[8,16,768]{2,1,0:T(8,128)}), f32[8,16,768]{2,1,0:T(8,128)S(1)}, u32[]{:S(2)}, u32[]{:S(2)}) async-start(f32[8,16,768]{2,1,0:T(8,128)} %broadcast_in_dim.10), calls=%async_computation.7 | async-start | bytes 786432 | tf_op jit(solution)/shard_map/all_to_all | solution.py:302
  185.9 0.7 copy-start.7
Sparse Core Ops, SparseCore 0:
  9.8 54.6 all-gather.2

commit v2 on v1

--- a/solution.py
+++ b/solution.py
@@ -17,7 +17,9 @@
 DP = ("y", "c")
 F32 = jnp.float32
 BF16 = jnp.bfloat16
-VMEM_LIMIT = 40 * 1024 * 1024
+VMEM_LIMIT = 32 * 1024 * 1024
+PROJECT_VMEM = 52000 * 1024
+WEIGHTS_VMEM = 52000 * 1024
 
 
 def features(a):
@@ -65,46 +67,90 @@
     return columns <= rows
 
 
-def project_kernel(x_ref, dy_ref, wq_ref, wk_ref, wv_ref, wo_ref, q_ref, k_ref, v_ref, g_ref, send_ref):
-    step = pl.program_id(0)
-
-    @pl.when(step == 0)
-    def _():
-        send_ref[...] = jnp.zeros_like(send_ref)
-
+def in_vmem(n):
+    return [pl.BlockSpec(memory_space=pltpu.VMEM)] * n
+
+
+def in_hbm(n):
+    return [pl.BlockSpec(memory_space=pltpu.HBM)] * n
+
+
+SCALARS = pl.BlockSpec(memory_space=pltpu.SMEM)
+
+
+def project_kernel(
+    x_hbm, dy_hbm, w_hbm, wo_hbm, q_ref, k_ref, v_ref, g_ref, send_ref, xdy_ref,
+    x_ref, dy_ref, w_ref, wo_ref, frame_sem, weight_sem,
+):
+    frames = [
+        pltpu.make_async_copy(x_hbm, x_ref, frame_sem.at[0]),
+        pltpu.make_async_copy(dy_hbm, dy_ref, frame_sem.at[1]),
+    ]
+    for copy in frames:
+        copy.start()
+    copies = []
+    for step in range(3):
+        lanes = pl.ds(256 * step, 256)
+        row = []
+        for kind, first in ((1, INNER), (2, 2 * INNER), (0, 0)):
+            columns = pl.ds(first + 256 * step, 256)
+            sem = weight_sem.at[step, kind]
+            row.append(pltpu.make_async_copy(w_hbm.at[:, columns], w_ref.at[:, columns], sem))
+        row.append(pltpu.make_async_copy(wo_hbm.at[:, lanes], wo_ref.at[:, lanes], weight_sem.at[step, 3]))
+        for copy in row:
+            copy.start()
+        copies.append(row)
+    send_ref[24:32, 0:16, :] = jnp.zeros((8, 16, 128), F32)
+    send_ref[:, 22:24, :] = jnp.zeros((32, 2, 128), F32)
+    for copy in frames:
+        copy.wait()
     x = x_ref[...]
-    q_ref[...] = mm(x, wq_ref[...]).astype(BF16)
-    k = mm(x, wk_ref[...]).astype(BF16)
-    k_ref[...] = k
-    v = mm(x, wv_ref[...]).astype(BF16)
-    v_ref[...] = v
-    g_ref[...] = mm(dy_ref[...], wo_ref[...]).astype(BF16)
-    fk = features(k.astype(F32)).astype(BF16)
-    for i in range(2):
-        lanes = slice(128 * i, 128 * i + 128)
-        state = diagonal_blocks(mm_at(fk[:, lanes], v[:, lanes]))
-        norm = jnp.sum(fk[:, lanes].astype(F32), axis=0, keepdims=True)
-        pair = 2 * step + i
-        send_ref[pl.ds(4 * pair, 4), 0:16, :] = state.reshape(4, 16, 128)
-        for t in range(32):
-            send_ref[t, pl.ds(16 + pair, 1), :] = norm
+    dy = dy_ref[...]
+    xdy_ref[0] = x.astype(F32)
+    xdy_ref[1] = dy.astype(F32)
+    for step in range(3):
+        k_copy, v_copy, q_copy, g_copy = copies[step]
+        lanes = slice(256 * step, 256 * step + 256)
+        k_copy.wait()
+        k = mm(x, w_ref[:, slice(INNER + 256 * step, INNER + 256 * step + 256)]).astype(BF16)
+        k_ref[:, lanes] = k
+        v_copy.wait()
+        v = mm(x, w_ref[:, slice(2 * INNER + 256 * step, 2 * INNER + 256 * step + 256)]).astype(BF16)
+        v_ref[:, lanes] = v
+        fk = features(k.astype(F32)).astype(BF16)
+        for i in range(2):
+            part = slice(128 * i, 128 * i + 128)
+            state = diagonal_blocks(mm_at(fk[:, part], v[:, part]))
+            norm = jnp.sum(fk[:, part].astype(F32), axis=0, keepdims=True)
+            pair = 2 * step + i
+            send_ref[4 * pair : 4 * pair + 4, 0:16, :] = state.reshape(4, 16, 128)
+            for t in range(32):
+                send_ref[t, 16 + pair : 17 + pair, :] = norm
+        q_copy.wait()
+        q_ref[:, lanes] = mm(x, w_ref[:, lanes]).astype(BF16)
+        g_copy.wait()
+        g_ref[:, lanes] = mm(dy, wo_ref[:, lanes]).astype(BF16)
 
 
 def project(x, dy, w_qkv, w_out):
     rows, width = x.shape
-    whole = pl.BlockSpec((rows, width), lambda i: (0, 0))
-    column = lambda first: pl.BlockSpec((width, 256), lambda i: (0, first + i))
-    out = pl.BlockSpec((rows, 256), lambda i: (0, i))
     return pl.pallas_call(
         project_kernel,
-        grid=(3,),
-        in_specs=[whole, whole, column(0), column(3), column(6), column(0)],
-        out_specs=[out] * 4 + [pl.BlockSpec((32, 24, 128), lambda i: (0, 0, 0))],
+        in_specs=in_hbm(4),
+        out_specs=in_vmem(6),
         out_shape=[jax.ShapeDtypeStruct((rows, INNER), BF16)] * 4
-        + [jax.ShapeDtypeStruct((32, 24, 128), F32)],
-        compiler_params=pltpu.CompilerParams(vmem_limit_bytes=VMEM_LIMIT),
+        + [jax.ShapeDtypeStruct((32, 24, 128), F32), jax.ShapeDtypeStruct((2, rows, width), F32)],
+        scratch_shapes=[
+            pltpu.VMEM(x.shape, BF16),
+            pltpu.VMEM(dy.shape, BF16),
+            pltpu.VMEM(w_qkv.shape, BF16),
+            pltpu.VMEM(w_out.shape, BF16),
+            pltpu.SemaphoreType.DMA((2,)),
+            pltpu.SemaphoreType.DMA((3, 4)),
+        ],
+        compiler_params=pltpu.CompilerParams(vmem_limit_bytes=PROJECT_VMEM),
         name="project",
-    )(x, dy, w_qkv, w_qkv, w_qkv, w_out)
+    )(x, dy, w_qkv, w_out)
 
 
 def denominators_kernel(me_ref, got_ref, q_ref, k_ref, g_ref, send_ref, den_ref, norm_ref, w_ref):
@@ -136,13 +182,6 @@
     send_ref[24:32, 16:32, :] = jnp.zeros((8, 16, 128), F32)
 
 
-def in_vmem(n):
-    return [pl.BlockSpec(memory_space=pltpu.VMEM)] * n
-
-
-SCALARS = pl.BlockSpec(memory_space=pltpu.SMEM)
-
-
 def denominators(me, got, q, k, g):
     return pl.pallas_call(
         denominators_kernel,
@@ -160,8 +199,9 @@
 
 
 def forward_kernel(
-    got_ref, q_ref, k_ref, v_ref, g_ref, den_ref, norm_ref, w_ref, send_ref, out_ref, dq_ref, ds_ref
+    y_ref, got_ref, q_ref, k_ref, v_ref, g_ref, den_ref, norm_ref, w_ref, send_ref, dq_ref, ds_ref, *rest
 ):
+    *block_refs, out_ref = rest
     carry = jnp.zeros((16, 128), F32)
     for t in reversed(range(32)):
         send_ref[t, 0:16, :] = carry
@@ -203,22 +243,25 @@
     dnorm = jnp.concatenate(dnorms + [jnp.zeros((2, 128), F32)], axis=0)
     for t in range(32):
         send_ref[t, 16:24, :] = dnorm
-
-
-def forward(got, q, k, v, g, den, norm, w):
+    for s, block_ref in enumerate(block_refs):
+        block_ref[...] = out_ref[lax.rem(y_ref[0] + s, 4)]
+
+
+def forward(y, got, q, k, v, g, den, norm, w):
     return pl.pallas_call(
         forward_kernel,
-        in_specs=in_vmem(8),
-        out_specs=in_vmem(4),
+        in_specs=[SCALARS] + in_vmem(8),
+        out_specs=in_vmem(7),
         out_shape=[
             jax.ShapeDtypeStruct((32, 24, 128), F32),
-            jax.ShapeDtypeStruct((4, BLOCK, 384), F32),
             jax.ShapeDtypeStruct((BLOCK, INNER), BF16),
             jax.ShapeDtypeStruct((PAIRS, 256, 128), BF16),
-        ],
+        ]
+        + [jax.ShapeDtypeStruct((BLOCK, 384), F32)] * 4,
+        scratch_shapes=[pltpu.VMEM((4, BLOCK, 384), F32)],
         compiler_params=pltpu.CompilerParams(vmem_limit_bytes=VMEM_LIMIT),
         name="forward",
-    )(got, q, k, v, g, den, norm, w)
+    )(y, got, q, k, v, g, den, norm, w)
 
 
 def backward_kernel(
@@ -265,70 +308,163 @@
     )(me, got, q, k, v, g, den, w, ds)
 
 
-def weights_kernel(y_ref, xdy_ref, first_ref, second_ref, out_ref):
-    y = y_ref[0]
-    columns = xdy_ref.shape[-1]
-    x = xdy_ref[:, 0].reshape(4 * BLOCK, columns).astype(BF16)
-    other = xdy_ref[:, y // 2].reshape(4 * BLOCK, columns).astype(BF16)
-    first = mm_at(other, first_ref[...].reshape(4 * BLOCK, 384).astype(BF16))
-    second = mm_at(x, second_ref[...].reshape(4 * BLOCK, 384).astype(BF16))
-    blocks = columns // 32
-    first = first.reshape(blocks, 2, 16, 384)
-    second = second.reshape(blocks, 2, 16, 384)
-    for c in range(2):
-        out_ref[c, :, :, 0:384] = first[:, c]
-        out_ref[c, :, :, 384:768] = second[:, c]
-
-
-def weights(y, xdy, first, second):
-    blocks = pl.BlockSpec((4, BLOCK, 384), lambda i: (0, 0, 0))
-    return pl.pallas_call(
-        weights_kernel,
-        grid=(4,),
-        in_specs=[
-            SCALARS,
-            pl.BlockSpec((4, 2, BLOCK, 256), lambda i: (0, 0, 0, i)),
-            blocks,
-            blocks,
-        ],
-        out_specs=pl.BlockSpec((2, 8, 16, 768), lambda i: (0, i, 0, 0)),
-        out_shape=jax.ShapeDtypeStruct((2, 32, 16, 768), F32),
-        compiler_params=pltpu.CompilerParams(vmem_limit_bytes=VMEM_LIMIT),
+def weights_kernel(where_ref, choice_ref, xdy_hbm, blocks_ref, keep_ref, send_ref, xdy_ref, sems, *, relative):
+    y = where_ref[0]
+    c = where_ref[1]
+    choice = choice_ref[0]
+    copies = []
+    for j in range(4):
+        lanes = pl.ds(256 * j, 256)
+        copies.append(
+            pltpu.make_async_copy(xdy_hbm.at[:, choice, :, lanes], xdy_ref.at[:, :, lanes], sems.at[j])
+        )
+        copies[-1].start()
+    order = [lax.rem(y + 4 - s, 4) if relative else s for s in range(4)]
+    blocks = [r[...] for r in blocks_ref] if relative else [blocks_ref[0][s] for s in range(4)]
+    blocks = jnp.concatenate(blocks, axis=0).astype(BF16)
+    for j in range(4):
+        copies[j].wait()
+        x = jnp.concatenate([xdy_ref[i, :, 256 * j : 256 * j + 256] for i in order], axis=0).astype(BF16)
+        part = mm_at(x, blocks).reshape(2, 4, 2, 16, 384)
+        for i in range(4):
+            first, second = part[:, i, 0], part[:, i, 1]
+            keep_ref[i, 2 * j : 2 * j + 2] = jnp.where(c == 0, first, second)
+            send_ref[i, 2 * j : 2 * j + 2] = jnp.where(c == 0, second, first)
+
+
+def weights(where, choice, xdy, blocks):
+    relative = len(blocks) == 4
+
+    def kernel(*refs):
+        n = len(blocks)
+        weights_kernel(*refs[:3], refs[3 : 3 + n], *refs[3 + n :], relative=relative)
+
+    out = jax.ShapeDtypeStruct((4, 8, 16, 384), F32)
+    return pl.pallas_call(
+        kernel,
+        in_specs=[SCALARS, SCALARS] + in_hbm(1) + in_vmem(len(blocks)),
+        out_specs=in_vmem(2),
+        out_shape=[out, out],
+        scratch_shapes=[pltpu.VMEM((4, BLOCK, 1024), F32), pltpu.SemaphoreType.DMA((4,))],
+        compiler_params=pltpu.CompilerParams(vmem_limit_bytes=WEIGHTS_VMEM),
         name="weights",
-    )(y, xdy, first, second)
+    )(where, choice, xdy, *blocks)
+
+
+def pair_sum_kernel(x_ref, keep_ref, got_ref, *out_refs):
+    for s, out_ref in enumerate(out_refs):
+        i = lax.rem(x_ref[0] + s, 4)
+        out_ref[...] = keep_ref[i] + got_ref[i]
+
+
+def pair_sum(x, keep, got):
+    return pl.pallas_call(
+        pair_sum_kernel,
+        in_specs=[SCALARS] + in_vmem(2),
+        out_specs=in_vmem(4),
+        out_shape=[jax.ShapeDtypeStruct((8, 16, 384), F32)] * 4,
+        compiler_params=pltpu.CompilerParams(vmem_limit_bytes=VMEM_LIMIT),
+        name="pair_sum",
+    )(x, keep, got)
+
+
+def merge_kernel(own_ref, a_ref, b_ref, c_ref, second_ref, out_ref):
+    out_ref[:, :, 0:384] = (own_ref[...] + a_ref[...]) + (b_ref[...] + c_ref[...])
+    out_ref[:, :, 384:768] = (second_ref[0] + second_ref[1]) + (second_ref[2] + second_ref[3])
+
+
+def merge(first, second):
+    return pl.pallas_call(
+        merge_kernel,
+        in_specs=in_vmem(5),
+        out_specs=in_vmem(1)[0],
+        out_shape=jax.ShapeDtypeStruct((8, 16, 768), F32),
+        compiler_params=pltpu.CompilerParams(vmem_limit_bytes=VMEM_LIMIT),
+        name="merge",
+    )(*first, second)
+
+
+def spread_kernel(got_ref, out_ref):
+    total = got_ref[0]
+    for i in range(1, 8):
+        total = total + got_ref[i]
+    for i in range(8):
+        out_ref[i] = total
+
+
+def spread(got):
+    return pl.pallas_call(
+        spread_kernel,
+        in_specs=in_vmem(1),
+        out_specs=in_vmem(1)[0],
+        out_shape=jax.ShapeDtypeStruct(got.shape, F32),
+        compiler_params=pltpu.CompilerParams(vmem_limit_bytes=VMEM_LIMIT),
+        name="spread",
+    )(got)
+
+
+def assemble_kernel(got_ref, qkv_ref, out_ref):
+    for y in range(4):
+        for c in range(2):
+            rows = slice(16 * c, 16 * c + 16)
+            piece = got_ref[2 * y + c]
+            target = qkv_ref if y < 2 else out_ref
+            target[rows, 384 * (y % 2) : 384 * (y % 2) + 384] = piece[:, 0:384]
+            qkv_ref[rows, INNER + 384 * y : INNER + 384 * y + 384] = piece[:, 384:768]
+
+
+def assemble(got):
+    return pl.pallas_call(
+        assemble_kernel,
+        in_specs=in_vmem(1),
+        out_specs=in_vmem(2),
+        out_shape=[jax.ShapeDtypeStruct((32, 3 * INNER), F32), jax.ShapeDtypeStruct((32, INNER), F32)],
+        compiler_params=pltpu.CompilerParams(vmem_limit_bytes=VMEM_LIMIT),
+        name="assemble",
+    )(got)
 
 
 def swap(a, axes):
     return lax.all_to_all(a, axes, 0, 0, tiled=True)
 
 
+def rotate(blocks, axis):
+    n = len(blocks)
+    moved = [lax.ppermute(b, axis, [(i, (i + s) % n) for i in range(n)]) for s, b in enumerate(blocks) if s]
+    return [blocks[0]] + moved
+
+
+def other_core(a):
+    return lax.ppermute(a, "c", [(0, 1), (1, 0)])
+
+
+def scalars(*values):
+    return jnp.stack([jnp.asarray(v, jnp.int32) for v in values])
+
+
 def per_device(frames, grad_frames, w_qkv, w_out):
-    x = frames[0]
-    dy = grad_frames[0]
-    me = lax.axis_index(TM).reshape(1).astype(jnp.int32)
-    y = lax.axis_index("y").reshape(1).astype(jnp.int32)
-    xdy = lax.all_gather(jnp.stack([x.astype(F32), dy.astype(F32)]), "y")
-    q, k, v, g, send = project(x, dy, w_qkv, w_out)
+    me = scalars(lax.axis_index(TM))
+    y, c = lax.axis_index("y"), lax.axis_index("c")
+    where = scalars(y, c)
+    q, k, v, g, send, xdy = project(frames[0], grad_frames[0], w_qkv, w_out)
+    xdy = lax.all_gather(xdy, "y")
     got = swap(send, TM)
     send, den, norm, w = denominators(me, got, q, k, g)
     got = swap(send, TM)
-    send, first, dq, ds = forward(got, q, k, v, g, den, norm, w)
+    send, dq, ds, *first = forward(scalars(y), got, q, k, v, g, den, norm, w)
+    first = rotate(first, "y")
     got = swap(send, TM)
+    keep, give = weights(where, scalars(y // 2), xdy, first)
+    got, give = lax.optimization_barrier((got, give))
     second, dkv = backward(me, got, q, k, v, g, den, w, ds)
     dqkv = jnp.concatenate([dq, dkv], axis=1)
     dx = lax.dot_general(dqkv, w_qkv, (((1,), (1,)), ((), ())), preferred_element_type=F32).astype(BF16)
-    first = swap(first, "y")
-    second = swap(second, "y")
-    part = swap(weights(y, xdy, first, second), "c")
-    part = part[0] + part[1]
-    total = jnp.sum(swap(part, TM), axis=0)
-    pieces = swap(jnp.broadcast_to(total[None], (8,) + total.shape), DP)
-    pieces = pieces.reshape(4, 32, 768)
-    half = 384
-    grad_qkv = jnp.concatenate(
-        [pieces[0, :, :half], pieces[1, :, :half]] + [pieces[i, :, half:] for i in range(4)], axis=1
-    )
-    grad_out = jnp.concatenate([pieces[2, :, :half], pieces[3, :, :half]], axis=1)
+    first = pair_sum(scalars(lax.axis_index("x")), keep, other_core(give))
+    first = rotate(first, "x")
+    second, first = lax.optimization_barrier((swap(second, "y"), first))
+    keep, give = weights(where, scalars(0), xdy, [second])
+    part = merge(first, swap(keep + other_core(give), "x"))
+    grad_qkv, grad_out = assemble(swap(spread(swap(part, "z")), DP))
     return dx[None], grad_qkv, grad_out
 
 

time: 194 us -> 176 us (0.907)
  blocking collectives: 96.3 us -> 32.7 us
  starting transfers between devices: 25.3 us -> 49.1 us
  waiting for transfers between devices: 32.5 us -> 48.3 us
  Pallas kernels: 11.9 us -> 20.4 us
  other arithmetic: 3.18 us -> 0.17 us
    all_to_all x4 -> x2, blocking collectives: 96.3 us -> 32.7 us  [swap(): return lax.all_to_all(a, axes, 0, 0, tiled=True)]
    ppermute x0 -> x8, starting transfers between devices: none -> 13.9 us  [the longest x6 9.94 us: rotate(): lax.ppermute(b, axis, [(i, (i + s) % n) for i in range(n)])]
    all_to_all x4 -> x5, starting transfers between devices: 25.2 us -> 35.2 us  [swap(): return lax.all_to_all(a, axes, 0, 0, tiled=True)]
    ppermute x0 -> x8, waiting for transfers between devices: none -> 8.64 us  [the longest x6 6.73 us: rotate(): lax.ppermute(b, axis, [(i, (i + s) % n) for i in range(n)])]
    pallas_call x3 -> x8, Pallas kernels: 8.74 us -> 16.4 us  [the longest x1 5.93 us: project(): pl.pallas_call(project_kernel, in_specs=in_hbm(4), out_specs=in_vmem(6),...]
    all_to_all x4 -> x5, waiting for transfers between devices: 32.5 us -> 39.6 us  [swap(): return lax.all_to_all(a, axes, 0, 0, tiled=True)]
    all_gather x1 -> x0, other arithmetic: 2.21 us -> none  [per_device(): xdy = lax.all_gather(jnp.stack([x.astype(F32), dy.astype(F32)]), 'y')]
    unnamed x21 -> x18, local copies, waits for them, and re-layouts: 4.62 us -> 5.97 us
  transfers between devices with their start and end apart: 5 -> 14, of which waited for: 4 -> 8; matrix products, arithmetic and copies ran while one was open for 2% -> 3% of each run, Pallas kernels for 5% -> 6%
where the time goes in v2:
time: 176 us
  starting transfers between devices  49.1 us (28%)
  waiting for transfers between devices  48.3 us (27%)
  blocking collectives  32.7 us (19%)
  Pallas kernels  20.4 us (12%)
  between operations  14.2 us (8%)
  local copies, waits for them, and re-layouts  5.97 us (3%)
  matrix products  4.67 us (3%)
    all_to_all x5, waiting for transfers between devices, swap(): return lax.all_to_all(a, axes, 0, 0, tiled=True)  39.6 us
    all_to_all x5, starting transfers between devices, swap(): return lax.all_to_all(a, axes, 0, 0, tiled=True)  35.2 us
    all_to_all x2, blocking collectives, swap(): return lax.all_to_all(a, axes, 0, 0, tiled=True)  32.7 us
    ppermute x6, starting transfers between devices, rotate(): lax.ppermute(b, axis, [(i, (i + s) % n) for i in range(n)])  9.94 us
    ppermute x6, waiting for transfers between devices, rotate(): lax.ppermute(b, axis, [(i, (i + s) % n) for i in range(n)])  6.73 us
    unnamed x18, local copies, waits for them, and re-layouts  5.97 us
    pallas_call x1, Pallas kernels, project(): pl.pallas_call(project_kernel, in_specs=in_hbm(4), out_specs=in_vmem(6),...  5.93 us
    pallas_call x2, Pallas kernels, weights(): pl.pallas_call(kernel, in_specs=[SCALARS, SCALARS] + in_hbm(1) + in_vmem(...  5.93 us
  transfers between devices with their start and end apart: 14, of which 8 were waited for; matrix products, arithmetic and copies ran while one was open for 3% of the time, Pallas kernels for 6%

profile of v2, /device:TPU:1, one launch (start us, length us, event | category | flops | bytes accessed | tf_op | source)
XLA Modules:
  0.0 175.5 jit_solution(14811218695049786565)
XLA Ops:
  7.2 0.9 copy-done.4
  8.2 0.9 copy-done.5
  9.1 5.9 %project.1 = (bf16[128,768]{1,0:T(8,128)(2,1)S(1)}, bf16[128,768]{1,0:T(8,128)(2,1)S(1)}, bf16[128,768]{1,0:T(8,128)(2,1)S(1)}, bf16[128,768]{1,0:T(8,128)(2,1)S...) custom-call(bf16[128,1024]{1,0:T(8,128)(2,1)S(1)} %bitcast.11, bf16[128,1024]{1,0:T(8,128)(2,1)S(1)} %bitcast.12, ...), custom_call_target="tpu_custom_call" | custom-call | tf_op jit(solution)/shard_map/project/pallas_call | solution.py:137
  15.1 11.9 %all-to-all-start = ((f32[32,24,128]{2,1,0:T(8,128)}), f32[32,24,128]{2,1,0:T(8,128)S(1)}, u32[]{:S(2)}, u32[]{:S(2)}) async-start(f32[32,24,128]{2,1,0:T(8,128)} %get-tuple-element.39), calls=%async_computation | async-start | bytes 786432 | tf_op jit(solution)/shard_map/all_to_all | solution.py:428
  27.0 13.8 %all-to-all-done.got_ref = f32[32,24,128]{2,1,0:T(8,128)S(1)} async-done(((f32[32,24,128]{2,1,0:T(8,128)}), f32[32,24,128]{2,1,0:T(8,128)S(1)}, u32[]{:S(2)}, u32[]{:S(2)}) %all-to-all-start) | async-done | bytes 393248 | tf_op jit(solution)/shard_map/all_to_all | solution.py:428
  40.8 2.5 %denominators.1 = (f32[32,32,128]{2,1,0:T(8,128)}, f32[128,768]{1,0:T(8,128)S(1)}, f32[8,128]{1,0:T(8,128)S(1)}, bf16[6,128,256]{2,1,0:T(8,128)(2,1)S(1)}) custom-call(s32[1]{0:T(128)} %bitcast.1.me_ref, f32[32,24,128]{2,1,0:T(8,128)S(1)} %all-to-all-done.got_ref, bf16[128,768]{1,0:T(8,128)(2,1)S(1)} %get-tuple-element.40.q_ref, ...), custom_call_target="tpu_custom_call" | custom-call | tf_op jit(solution)/shard_map/denominators/pallas_call | solution.py:186
  43.3 5.0 %all-to-all-start.1 = ((f32[32,32,128]{2,1,0:T(8,128)}), f32[32,32,128]{2,1,0:T(8,128)S(1)}, u32[]{:S(2)}, u32[]{:S(2)}) async-start(f32[32,32,128]{2,1,0:T(8,128)} %get-tuple-element.43), calls=%async_computation.1 | async-start | bytes 1048576 | tf_op jit(solution)/shard_map/all_to_all | solution.py:428
  48.3 15.3 %all-to-all-done.1.got_ref = f32[32,32,128]{2,1,0:T(8,128)S(1)} async-done(((f32[32,32,128]{2,1,0:T(8,128)}), f32[32,32,128]{2,1,0:T(8,128)S(1)}, u32[]{:S(2)}, u32[]{:S(2)}) %all-to-all-start.1) | async-done | bytes 524320 | tf_op jit(solution)/shard_map/all_to_all | solution.py:428
  63.6 2.9 %forward.1 = (f32[32,24,128]{2,1,0:T(8,128)}, bf16[128,768]{1,0:T(8,128)(2,1)S(1)}, bf16[6,256,128]{2,1,0:T(8,128)(2,1)S(1)}, f32[128,384]{1,0:T(8,128)S(1)}, f3...) custom-call(s32[1]{0:T(128)} %bitcast.y_ref, f32[32,32,128]{2,1,0:T(8,128)S(1)} %all-to-all-done.1.got_ref, ...), custom_call_target="tpu_custom_call" | custom-call | tf_op jit(solution)/shard_map/forward/pallas_call | solution.py:251
  67.9 6.2 %all-to-all-start.2 = ((f32[32,24,128]{2,1,0:T(8,128)}), f32[32,24,128]{2,1,0:T(8,128)S(1)}, u32[]{:S(2)}, u32[]{:S(2)}) async-start(f32[32,24,128]{2,1,0:T(8,128)} %get-tuple-element.49), calls=%async_computation.2 | async-start | bytes 786432 | tf_op jit(solution)/shard_map/all_to_all | solution.py:428
  74.1 1.4 collective-permute-start
  75.5 2.6 %collective-permute-start.1 = (f32[128,384]{1,0:T(8,128)S(1)}, f32[128,384]{1,0:T(8,128)S(1)}, u32[]{:S(2)}, u32[]{:S(2)}) collective-permute-start(f32[128,384]{1,0:T(8,128)S(1)} %get-tuple-element.53), channel_id=1, source_target_pairs={{0,4},{2,6},{4,0},{6,2},{1,5},{3,7},{5,1},{7,3},{8,12},{10,14},{12... | collective-permute-start | bytes 589832 | tf_op jit(solution)/shard_map/ppermute | solution.py:433
  78.1 1.1 collective-permute-start.2
  79.2 1.0 collective-permute-done.refs_4_
  80.3 5.1 %collective-permute-done.1.refs_5_ = f32[128,384]{1,0:T(8,128)S(1)} collective-permute-done((f32[128,384]{1,0:T(8,128)S(1)}, f32[128,384]{1,0:T(8,128)S(1)}, u32[]{:S(2)}, u32[]{:S(2)}) %collective-permute-start.1) | collective-permute-done | bytes 196640 | tf_op jit(solution)/shard_map/ppermute | solution.py:433
  85.4 3.0 %weights.2 = (f32[4,8,16,384]{3,2,1,0:T(8,128)S(1)}, f32[4,8,16,384]{3,2,1,0:T(8,128)S(1)}) custom-call(s32[2]{0:T(128)S(1)} %pad_add_fusion.refs_0_, s32[1]{0:T(128)} %bitcast.5.refs_1_, f32[4,2,128,1024]{3,2,1,0:T(8,128)} %bitcast.13, f32[128,384]{1,0:T(8,128)S(1)} %get-tuple-element.51.refs_3_, f32[128,384]{1,0:T(8,128)S(1)} %collective-permute-done.refs_4_, ...), custom_call_target="tpu_custom_call" | custom-call | tf_op jit(solution)/shard_map/weights/pallas_call | solution.py:343
  89.2 2.8 %collective-permute-start.3 = (f32[4,8,16,384]{3,2,1,0:T(8,128)}, f32[4,8,16,384]{3,2,1,0:T(8,128)S(1)}, u32[]{:S(2)}, u32[]{:S(2)}) collective-permute-start(f32[4,8,16,384]{3,2,1,0:T(8,128)} %copy-done.8), channel_id=1, source_target_pairs={{0,1},{1,0},{2,3},{3,2},{4,5},{5,4},{6,7},{7,6},{8,9},{9,8},{10,11... | collective-permute-start | bytes 2359304 | tf_op jit(solution)/shard_map/ppermute | solution.py:438
  92.0 1.0 copy-done.1
  93.0 1.5 backward.1
  95.2 3.6 %all-to-all-start.3 = ((f32[4,128,384]{2,1,0:T(8,128)}), f32[4,128,384]{2,1,0:T(8,128)S(1)}, u32[]{:S(2)}, u32[]{:S(2)}) async-start(f32[4,128,384]{2,1,0:T(8,128)} %get-tuple-element.59), calls=%async_computation.3 | async-start | bytes 1572864 | tf_op jit(solution)/shard_map/all_to_all | solution.py:428
  98.9 1.3 collective-permute-start.4
  100.2 2.4 %collective-permute-start.5 = (f32[8,16,384]{2,1,0:T(8,128)S(1)}, f32[8,16,384]{2,1,0:T(8,128)S(1)}, u32[]{:S(2)}, u32[]{:S(2)}) collective-permute-start(f32[8,16,384]{2,1,0:T(8,128)S(1)} %get-tuple-element.64), channel_id=1, source_target_pairs={{0,16},{8,24},{16,0},{24,8},{1,17},{9,25},{17,1},{25,9},{2,18},{10... | collective-permute-start | bytes 589832 | tf_op jit(solution)/shard_map/ppermute | solution.py:433
  102.6 1.2 collective-permute-start.6
  103.8 7.2 %all-to-all-done.3.refs_3_ = f32[4,128,384]{2,1,0:T(8,128)S(1)} async-done(((f32[4,128,384]{2,1,0:T(8,128)}), f32[4,128,384]{2,1,0:T(8,128)S(1)}, u32[]{:S(2)}, u32[]{:S(2)}) %all-to-all-start.3) | async-done | bytes 786464 | tf_op jit(solution)/shard_map/all_to_all | solution.py:428
  111.6 3.0 %weights.3 = (f32[4,8,16,384]{3,2,1,0:T(8,128)S(1)}, f32[4,8,16,384]{3,2,1,0:T(8,128)S(1)}) custom-call(s32[2]{0:T(128)S(1)} %pad_add_fusion.refs_0_, s32[1]{0:T(128)} %constant.33.clone.1.refs_1_, f32[4,2,128,1024]{3,2,1,0:T(8,128)} %bitcast.14, f32[4,128,384]{2,1,0:T(8,128)S(1)} %all-to-all-done.3.refs_3_), custom_call_target="tpu_custom_call" | custom-call | tf_op jit(solution)/shard_map/weights/pallas_call | solution.py:343
  114.5 1.2 collective-permute-start.7
  115.7 1.9 %collective-permute-done.7 = f32[4,8,16,384]{3,2,1,0:T(8,128)S(1)} collective-permute-done((f32[4,8,16,384]{3,2,1,0:T(8,128)S(1)}, f32[4,8,16,384]{3,2,1,0:T(8,128)S(1)}, u32[]{:S(2)}, u32[]{:S(2)}) %collective-permute-start.7) | collective-permute-done | bytes 786464 | tf_op jit(solution)/shard_map/ppermute | solution.py:438
  117.7 14.9 %all_to_all.35.second_ref = f32[4,8,16,384]{3,2,1,0:T(8,128)S(1)} all-to-all(f32[4,8,16,384]{3,2,1,0:T(8,128)S(1)} %add.8), channel_id=1, replica_groups=mesh['z'=8,'x'=4,'y'=4,'c'=2] {'x'}, dimensions={0} | all-to-all | bytes 1572864 | tf_op jit(solution)/shard_map/all_to_all | solution.py:428
  132.7 17.8 %all_to_all.36.got_ref = f32[8,16,768]{2,1,0:T(8,128)S(1)} all-to-all(f32[8,16,768]{2,1,0:T(8,128)S(1)} %merge.1), channel_id=1, replica_groups=mesh['z'=8,'x'=4,'y'=4,'c'=2] {'z'}, dimensions={0} | all-to-all | bytes 786432 | tf_op jit(solution)/shard_map/all_to_all | solution.py:428
  151.3 8.5 %all-to-all-start.6 = ((f32[8,16,768]{2,1,0:T(8,128)}), f32[8,16,768]{2,1,0:T(8,128)S(1)}, u32[]{:S(2)}, u32[]{:S(2)}) async-start(f32[8,16,768]{2,1,0:T(8,128)} %spread.1), calls=%async_computation.6 | async-start | bytes 786432 | tf_op jit(solution)/shard_map/all_to_all | solution.py:428
  159.9 4.7 %fusion = bf16[1,128,1024]{2,1,0:T(8,128)(2,1)} fusion(bf16[1024,2304]{1,0:T(8,128)(2,1)} %w_hbm.1, bf16[128,1536]{1,0:T(8,128)(2,1)S(1)} %copy-done.3, bf16[128,768]{1,0:T(8,128)(2,1)S(1)} %copy-done.7), kind=kOutput, calls=%fused_computation.1 | convolution fusion | flops 605290496 | bytes 5570560 | tf_op jit(solution)/shard_map/dot_general | solution.py:461
  164.5 3.4 %all-to-all-done.6.got_ref = f32[8,16,768]{2,1,0:T(8,128)S(1)} async-done(((f32[8,16,768]{2,1,0:T(8,128)}), f32[8,16,768]{2,1,0:T(8,128)S(1)}, u32[]{:S(2)}, u32[]{:S(2)}) %all-to-all-start.6) | async-done | bytes 393248 | tf_op jit(solution)/shard_map/all_to_all | solution.py:428
  (30 shorter events, 5.6 us)
Async XLA Ops:
  7.2 78.2 %all-gather.3.cloned.1.call-start = ((), (), s32[]{:S(2)}) async-start(), calls=%async_computation.7 | async-start | bytes 5242880 | tf_op jit(solution)/shard_map/all_gather | solution.py:450
  7.2 1.0 copy-start.4
  8.2 0.9 copy-start.5
  15.1 25.7 %all-to-all-start = ((f32[32,24,128]{2,1,0:T(8,128)}), f32[32,24,128]{2,1,0:T(8,128)S(1)}, u32[]{:S(2)}, u32[]{:S(2)}) async-start(f32[32,24,128]{2,1,0:T(8,128)} %get-tuple-element.39), calls=%async_computation | async-start | bytes 786432 | tf_op jit(solution)/shard_map/all_to_all | solution.py:428
  43.3 20.3 %all-to-all-start.1 = ((f32[32,32,128]{2,1,0:T(8,128)}), f32[32,32,128]{2,1,0:T(8,128)S(1)}, u32[]{:S(2)}, u32[]{:S(2)}) async-start(f32[32,32,128]{2,1,0:T(8,128)} %get-tuple-element.43), calls=%async_computation.1 | async-start | bytes 1048576 | tf_op jit(solution)/shard_map/all_to_all | solution.py:428
  66.5 0.8 copy-start
  67.2 0.7 copy-start.6
  67.9 21.3 %all-to-all-start.2 = ((f32[32,24,128]{2,1,0:T(8,128)}), f32[32,24,128]{2,1,0:T(8,128)S(1)}, u32[]{:S(2)}, u32[]{:S(2)}) async-start(f32[32,24,128]{2,1,0:T(8,128)} %get-tuple-element.49), calls=%async_computation.2 | async-start | bytes 786432 | tf_op jit(solution)/shard_map/all_to_all | solution.py:428
  74.1 6.2 %collective-permute-start = (f32[128,384]{1,0:T(8,128)S(1)}, f32[128,384]{1,0:T(8,128)S(1)}, u32[]{:S(2)}, u32[]{:S(2)}) collective-permute-start(f32[128,384]{1,0:T(8,128)S(1)} %get-tuple-element.52), channel_id=1, source_target_pairs={{0,2},{2,4},{4,6},{6,0},{1,3},{3,5},{5,7},{7,1},{8,10},{10,12},{12... | collective-permute-start | bytes 589832 | tf_op jit(solution)/shard_map/ppermute | solution.py:433
  75.5 9.9 %collective-permute-start.1 = (f32[128,384]{1,0:T(8,128)S(1)}, f32[128,384]{1,0:T(8,128)S(1)}, u32[]{:S(2)}, u32[]{:S(2)}) collective-permute-start(f32[128,384]{1,0:T(8,128)S(1)} %get-tuple-element.53), channel_id=1, source_target_pairs={{0,4},{2,6},{4,0},{6,2},{1,5},{3,7},{5,1},{7,3},{8,12},{10,14},{12... | collective-permute-start | bytes 589832 | tf_op jit(solution)/shard_map/ppermute | solution.py:433
  78.1 7.3 %collective-permute-start.2 = (f32[128,384]{1,0:T(8,128)S(1)}, f32[128,384]{1,0:T(8,128)S(1)}, u32[]{:S(2)}, u32[]{:S(2)}) collective-permute-start(f32[128,384]{1,0:T(8,128)S(1)} %get-tuple-element.54), channel_id=1, source_target_pairs={{0,6},{2,0},{4,2},{6,4},{1,7},{3,1},{5,3},{7,5},{8,14},{10,8},{12,... | collective-permute-start | bytes 589832 | tf_op jit(solution)/shard_map/ppermute | solution.py:433
  88.3 0.9 copy-start.8
  89.2 9.6 %collective-permute-start.3 = (f32[4,8,16,384]{3,2,1,0:T(8,128)}, f32[4,8,16,384]{3,2,1,0:T(8,128)S(1)}, u32[]{:S(2)}, u32[]{:S(2)}) collective-permute-start(f32[4,8,16,384]{3,2,1,0:T(8,128)} %copy-done.8), channel_id=1, source_target_pairs={{0,1},{1,0},{2,3},{3,2},{4,5},{5,4},{6,7},{7,6},{8,9},{9,8},{10,11... | collective-permute-start | bytes 2359304 | tf_op jit(solution)/shard_map/ppermute | solution.py:438
  92.0 1.0 copy-start.1
  94.5 0.7 copy-start.2
  95.2 15.7 %all-to-all-start.3 = ((f32[4,128,384]{2,1,0:T(8,128)}), f32[4,128,384]{2,1,0:T(8,128)S(1)}, u32[]{:S(2)}, u32[]{:S(2)}) async-start(f32[4,128,384]{2,1,0:T(8,128)} %get-tuple-element.59), calls=%async_computation.3 | async-start | bytes 1572864 | tf_op jit(solution)/shard_map/all_to_all | solution.py:428
  98.9 12.1 %collective-permute-start.4 = (f32[8,16,384]{2,1,0:T(8,128)S(1)}, f32[8,16,384]{2,1,0:T(8,128)S(1)}, u32[]{:S(2)}, u32[]{:S(2)}) collective-permute-start(f32[8,16,384]{2,1,0:T(8,128)S(1)} %get-tuple-element.63), channel_id=1, source_target_pairs={{0,8},{8,16},{16,24},{24,0},{1,9},{9,17},{17,25},{25,1},{2,10},{10... | collective-permute-start | bytes 589832 | tf_op jit(solution)/shard_map/ppermute | solution.py:433
  100.2 11.4 %collective-permute-start.5 = (f32[8,16,384]{2,1,0:T(8,128)S(1)}, f32[8,16,384]{2,1,0:T(8,128)S(1)}, u32[]{:S(2)}, u32[]{:S(2)}) collective-permute-start(f32[8,16,384]{2,1,0:T(8,128)S(1)} %get-tuple-element.64), channel_id=1, source_target_pairs={{0,16},{8,24},{16,0},{24,8},{1,17},{9,25},{17,1},{25,9},{2,18},{10... | collective-permute-start | bytes 589832 | tf_op jit(solution)/shard_map/ppermute | solution.py:433
  102.6 9.0 %collective-permute-start.6 = (f32[8,16,384]{2,1,0:T(8,128)S(1)}, f32[8,16,384]{2,1,0:T(8,128)S(1)}, u32[]{:S(2)}, u32[]{:S(2)}) collective-permute-start(f32[8,16,384]{2,1,0:T(8,128)S(1)} %get-tuple-element.65), channel_id=1, source_target_pairs={{0,24},{8,0},{16,8},{24,16},{1,25},{9,1},{17,9},{25,17},{2,26},{10... | collective-permute-start | bytes 589832 | tf_op jit(solution)/shard_map/ppermute | solution.py:433
  114.5 45.3 %copy-start.3 = (bf16[128,1536]{1,0:T(8,128)(2,1)S(1)}, bf16[128,1536]{1,0:T(8,128)(2,1)}, u32[]{:S(2)}) copy-start(bf16[128,1536]{1,0:T(8,128)(2,1)} %copy-done.2) | copy-start | bytes 1179652
  114.5 45.3 %copy-start.7 = (bf16[128,768]{1,0:T(8,128)(2,1)S(1)}, bf16[128,768]{1,0:T(8,128)(2,1)}, u32[]{:S(2)}) copy-start(bf16[128,768]{1,0:T(8,128)(2,1)} %copy-done.6) | copy-start | bytes 589828
  114.5 3.1 %collective-permute-start.7 = (f32[4,8,16,384]{3,2,1,0:T(8,128)S(1)}, f32[4,8,16,384]{3,2,1,0:T(8,128)S(1)}, u32[]{:S(2)}, u32[]{:S(2)}) collective-permute-start(f32[4,8,16,384]{3,2,1,0:T(8,128)S(1)} %get-tuple-element.72), channel_id=1, source_target_pairs={{0,1},{1,0},{2,3},{3,2},{4,5},{5,4},{6,7},{7,6},{8,9},{9,8},{10,11... | collective-permute-start | bytes 2359304 | tf_op jit(solution)/shard_map/ppermute | solution.py:438
  151.3 16.6 %all-to-all-start.6 = ((f32[8,16,768]{2,1,0:T(8,128)}), f32[8,16,768]{2,1,0:T(8,128)S(1)}, u32[]{:S(2)}, u32[]{:S(2)}) async-start(f32[8,16,768]{2,1,0:T(8,128)} %spread.1), calls=%async_computation.6 | async-start | bytes 786432 | tf_op jit(solution)/shard_map/all_to_all | solution.py:428
Sparse Core Ops, SparseCore 0:
  15.2 54.6 all-gather.2

commit v3 on v2

v3 whole, which is shorter than its diff:
```python
import jax
import jax.numpy as jnp
from jax import lax
from jax.experimental import pallas as pl
from jax.experimental.pallas import tpu as pltpu
from jax.sharding import Mesh
from jax.sharding import PartitionSpec as P

HEADS = 12
HEAD = 64
BLOCK = 128
PAIRS = HEADS // 2
INNER = HEADS * HEAD
TM = ("z", "x")
DP = ("y", "c")
F32 = jnp.float32
BF16 = jnp.bfloat16
VMEM_LIMIT = 32 * 1024 * 1024
LARGE_VMEM = 54300 * 1024


def features(a):
    return jnp.where(a > 0, a + 1.0, jnp.exp(jnp.minimum(a, 0.0)))


def slope(a):
    return jnp.where(a > 0, 1.0, jnp.exp(jnp.minimum(a, 0.0)))


def low_lanes(shape):
    return lax.broadcasted_iota(jnp.int32, shape, len(shape) - 1) < HEAD


def split_pair(a):
    low = low_lanes(a.shape)
    zero = jnp.zeros_like(a)
    return jnp.where(low, a, zero), jnp.where(low, zero, a)


def block_diagonal(packed):
    first, second = split_pair(packed)
    return jnp.concatenate([first, second], axis=0)


def diagonal_blocks(m):
    return jnp.where(low_lanes((HEAD, 2 * HEAD)), m[:HEAD], m[HEAD:])


def mm(a, b):
    return lax.dot_general(a, b, (((1,), (0,)), ((), ())), preferred_element_type=F32)


def mm_bt(a, b):
    return lax.dot_general(a, b, (((1,), (1,)), ((), ())), preferred_element_type=F32)


def mm_at(a, b):
    return lax.dot_general(a, b, (((0,), (0,)), ((), ())), preferred_element_type=F32)


def causal():
    rows = lax.broadcasted_iota(jnp.int32, (BLOCK, BLOCK), 0)
    columns = lax.broadcasted_iota(jnp.int32, (BLOCK, BLOCK), 1)
    return columns <= rows


def in_vmem(n):
    return [pl.BlockSpec(memory_space=pltpu.VMEM)] * n


def in_hbm(n):
    return [pl.BlockSpec(memory_space=pltpu.HBM)] * n


def f32(*shape):
    return jax.ShapeDtypeStruct(shape, F32)


def bf16(*shape):
    return jax.ShapeDtypeStruct(shape, BF16)


def call(kernel, args, outs, name, scratch=(), in_specs=None, limit=VMEM_LIMIT):
    return pl.pallas_call(
        kernel,
        in_specs=in_specs or in_vmem(len(args)),
        out_specs=in_vmem(len(outs)),
        out_shape=outs,
        scratch_shapes=list(scratch),
        compiler_params=pltpu.CompilerParams(vmem_limit_bytes=limit),
        name=name,
    )(*args)


def time_index():
    return lax.axis_index("z") * 4 + lax.axis_index("x")


def project_kernel(
    x_hbm, dy_hbm, w_hbm, wo_hbm, q_ref, k_ref, v_ref, g_ref, send_ref, xdy_ref,
    x_ref, dy_ref, w_ref, wo_ref, frame_sem, weight_sem,
):
    frames = [
        pltpu.make_async_copy(x_hbm, x_ref, frame_sem.at[0]),
        pltpu.make_async_copy(dy_hbm, dy_ref, frame_sem.at[1]),
    ]
    for copy in frames:
        copy.start()

    def fetch(step):
        copies = []
        for kind, first in enumerate((INNER, 2 * INNER, 0)):
            columns = pl.ds(first + 256 * step, 256)
            sem = weight_sem.at[step, kind]
            copies.append(pltpu.make_async_copy(w_hbm.at[:, columns], w_ref.at[:, columns], sem))
        lanes = pl.ds(256 * step, 256)
        copies.append(pltpu.make_async_copy(wo_hbm.at[:, lanes], wo_ref.at[:, lanes], weight_sem.at[step, 3]))
        for copy in copies:
            copy.start()
        return copies

    copies = fetch(0)
    send_ref[24:32, 0:16, :] = jnp.zeros((8, 16, 128), F32)
    send_ref[:, 22:24, :] = jnp.zeros((32, 2, 128), F32)
    for copy in frames:
        copy.wait()
    x = x_ref[...]
    dy = dy_ref[...]
    xdy_ref[0] = x.astype(F32)
    xdy_ref[1] = dy.astype(F32)
    for step in range(3):
        lanes = slice(256 * step, 256 * step + 256)
        for copy in copies:
            copy.wait()
        if step < 2:
            copies = fetch(step + 1)
        k = mm(x, w_ref[:, slice(INNER + 256 * step, INNER + 256 * step + 256)]).astype(BF16)
        k_ref[:, lanes] = k
        v = mm(x, w_ref[:, slice(2 * INNER + 256 * step, 2 * INNER + 256 * step + 256)]).astype(BF16)
        v_ref[:, lanes] = v
        fk = features(k.astype(F32)).astype(BF16)
        for i in range(2):
            part = slice(128 * i, 128 * i + 128)
            state = diagonal_blocks(mm_at(fk[:, part], v[:, part]))
            norm = jnp.sum(fk[:, part].astype(F32), axis=0, keepdims=True)
            pair = 2 * step + i
            send_ref[4 * pair : 4 * pair + 4, 0:16, :] = state.reshape(4, 16, 128)
            for t in range(32):
                send_ref[t, 16 + pair : 17 + pair, :] = norm
        q_ref[:, lanes] = mm(x, w_ref[:, lanes]).astype(BF16)
        g_ref[:, lanes] = mm(dy, wo_ref[:, lanes]).astype(BF16)


def project(x, dy, w_qkv, w_out):
    rows, width = x.shape
    scratch = [pltpu.VMEM(a.shape, BF16) for a in (x, dy, w_qkv, w_out)]
    scratch += [pltpu.SemaphoreType.DMA((2,)), pltpu.SemaphoreType.DMA((3, 4))]
    outs = [bf16(rows, INNER)] * 4 + [f32(32, 24, 128), f32(2, rows, width)]
    return call(
        project_kernel, (x, dy, w_qkv, w_out), outs, "project", scratch, in_hbm(4), LARGE_VMEM
    )


def denominators_kernel(got_ref, q_ref, k_ref, g_ref, send_ref, den_ref, norm_ref, w_ref):
    me = time_index()
    carry = jnp.zeros((16, 128), F32)
    norms = jnp.zeros((8, 128), F32)
    for t in range(32):
        send_ref[t, 0:16, :] = carry
        carry = carry + got_ref[t, 0:16, :]
        norms = norms + jnp.where(t < me, got_ref[t, 16:24, :], 0.0)
    norm_ref[...] = norms
    mask = causal()
    for p in range(PAIRS):
        lanes = slice(128 * p, 128 * p + 128)
        fq32 = features(q_ref[:, lanes].astype(F32))
        fq = fq32.astype(BF16)
        fk = features(k_ref[:, lanes].astype(F32)).astype(BF16)
        fq_norm = fq.astype(F32) * norms[p : p + 1, :]
        sums = []
        for half, (rows, extra) in enumerate(zip(split_pair(fq), split_pair(fq_norm))):
            scores = jnp.where(mask, mm_bt(rows, fk), 0.0)
            w_ref[p, :, 128 * half : 128 * half + 128] = scores.astype(BF16)
            sums.append(jnp.sum(scores + extra, axis=1, keepdims=True))
        den = jnp.where(low_lanes((BLOCK, 128)), sums[0], sums[1])
        den_ref[:, lanes] = den
        dnum = (g_ref[:, lanes].astype(F32) / den).astype(BF16)
        dstate = diagonal_blocks(mm_at(fq, dnum))
        send_ref[4 * p : 4 * p + 4, 16:32, :] = dstate.reshape(4, 16, 128)
    send_ref[24:32, 16:32, :] = jnp.zeros((8, 16, 128), F32)


def denominators(*args):
    outs = [f32(32, 32, 128), f32(BLOCK, INNER), f32(8, 128), bf16(PAIRS, BLOCK, 256)]
    return call(denominators_kernel, args, outs, "denominators")


def forward_kernel(
    got_ref, q_ref, k_ref, v_ref, g_ref, den_ref, norm_ref, w_ref,
    send_ref, dq_ref, ds_ref, b0_ref, b1_ref, b2_ref, b3_ref, out_ref,
):
    carry = jnp.zeros((16, 128), F32)
    for t in reversed(range(32)):
        send_ref[t, 0:16, :] = carry
        carry = carry + got_ref[t, 16:32, :]
    mask = causal()
    low = low_lanes((BLOCK, 128))
    dnorms = []
    for p in range(PAIRS):
        lanes = slice(128 * p, 128 * p + 128)
        block, part = p // 3, slice(128 * (p % 3), 128 * (p % 3) + 128)
        q = q_ref[:, lanes].astype(F32)
        fq = features(q).astype(BF16)
        fk = features(k_ref[:, lanes].astype(F32)).astype(BF16)
        v = v_ref[:, lanes]
        g = g_ref[:, lanes].astype(F32)
        inverse = 1.0 / den_ref[:, lanes]
        state = block_diagonal(got_ref[4 * p : 4 * p + 4, 0:16, :].reshape(64, 128).astype(BF16))
        v_halves = jnp.concatenate(split_pair(v), axis=0)
        ratio = (mm(w_ref[p], v_halves) + mm(fq, state)) * inverse
        out_ref[2 + block, :, part] = ratio.astype(BF16).astype(F32)
        dnum = (g * inverse).astype(BF16)
        sums = [jnp.sum(a, axis=1, keepdims=True) for a in split_pair(g * ratio)]
        dden = -jnp.where(low, sums[0], sums[1]) * inverse
        ddens = (dden[:, 0:1], dden[:, 127:128])
        dnorms.append(jnp.sum(dden * fq.astype(F32), axis=0, keepdims=True))
        ds = [
            jnp.where(mask, mm_bt(rows, v) + column, 0.0).astype(BF16)
            for rows, column in zip(split_pair(dnum), ddens)
        ]
        ds_ref[p] = jnp.concatenate(ds, axis=0)
        dfq = (
            mm(jnp.concatenate(ds, axis=1), jnp.concatenate(split_pair(fk), axis=0))
            + mm_bt(dnum, state)
            + dden * norm_ref[p : p + 1, :]
        )
        dq = (dfq * slope(q)).astype(BF16)
        dq_ref[:, lanes] = dq
        out_ref[block, :, part] = dq.astype(F32)
    dnorm = jnp.concatenate(dnorms + [jnp.zeros((2, 128), F32)], axis=0)
    for t in range(32):
        send_ref[t, 16:24, :] = dnorm
    y = lax.axis_index("y")
    for i, ref in enumerate((b0_ref, b1_ref, b2_ref, b3_ref)):
        ref[...] = out_ref[lax.rem(y + i, 4)]


def forward(*args):
    outs = [f32(32, 24, 128), bf16(BLOCK, INNER), bf16(PAIRS, 256, 128)] + [f32(BLOCK, 384)] * 4
    return call(forward_kernel, args, outs, "forward", [pltpu.VMEM((4, BLOCK, 384), F32)])


def backward_kernel(
    got_ref, q_ref, k_ref, v_ref, g_ref, den_ref, w_ref, ds_ref, out_ref, dkv_ref
):
    me = time_index()
    dnorms = jnp.zeros((8, 128), F32)
    for t in range(32):
        dnorms = dnorms + jnp.where(t > me, got_ref[t, 16:24, :], 0.0)
    for p in range(PAIRS):
        lanes = slice(128 * p, 128 * p + 128)
        block, part = p // 3, slice(128 * (p % 3), 128 * (p % 3) + 128)
        fq = features(q_ref[:, lanes].astype(F32)).astype(BF16)
        k = k_ref[:, lanes].astype(F32)
        fk = features(k).astype(BF16)
        v = v_ref[:, lanes]
        dnum = (g_ref[:, lanes].astype(F32) * (1.0 / den_ref[:, lanes])).astype(BF16)
        dstate = block_diagonal(got_ref[4 * p : 4 * p + 4, 0:16, :].reshape(64, 128).astype(BF16))
        dfk = (
            mm_at(ds_ref[p], jnp.concatenate(split_pair(fq), axis=0))
            + mm_bt(v, dstate)
            + dnorms[p : p + 1, :]
        )
        dk = (dfk * slope(k)).astype(BF16)
        w = jnp.concatenate([w_ref[p, :, 0:128], w_ref[p, :, 128:256]], axis=0)
        dv = (mm_at(w, jnp.concatenate(split_pair(dnum), axis=0)) + mm(fk, dstate)).astype(BF16)
        out_ref[block, :, part] = dk.astype(F32)
        out_ref[2 + block, :, part] = dv.astype(F32)
        dkv_ref[:, lanes] = dk
        dkv_ref[:, slice(INNER + 128 * p, INNER + 128 * p + 128)] = dv


def backward(*args):
    return call(backward_kernel, args, [f32(4, BLOCK, 384), bf16(BLOCK, 2 * INNER)], "backward")


def stage_kernel(xdy_ref, x_ref, chosen_ref):
    y = lax.axis_index("y")
    sources = [lax.rem(y + 4 - i, 4) for i in range(4)]
    for j in range(8):
        lanes = slice(128 * j, 128 * j + 128)
        x = jnp.concatenate([xdy_ref[i, 0, :, lanes] for i in sources], axis=0)
        dy = jnp.concatenate([xdy_ref[i, 1, :, lanes] for i in sources], axis=0)
        x_ref[lanes, :] = x.T.astype(BF16)
        chosen_ref[lanes, :] = jnp.where(y < 2, x, dy).T.astype(BF16)


def weights_kernel(x_ref, chosen_ref, b0_ref, b1_ref, b2_ref, b3_ref, got_ref, keep_ref, give_ref):
    y, c = lax.axis_index("y"), lax.axis_index("c")
    first = [b0_ref[...], b1_ref[...], b2_ref[...], b3_ref[...]]
    second = [got_ref[lax.rem(y + s, 4)] for s in (0, 3, 2, 1)]
    for frames_ref, blocks, lanes in (
        (chosen_ref, first, slice(0, 384)),
        (x_ref, second, slice(384, 768)),
    ):
        blocks = jnp.concatenate(blocks, axis=0).astype(BF16)
        for j in range(4):
            part = mm(frames_ref[256 * j : 256 * j + 256, :], blocks).reshape(2, 4, 2, 16, 384)
            for i in range(4):
                one, two = part[:, i, 0], part[:, i, 1]
                keep_ref[i, 2 * j : 2 * j + 2, :, lanes] = jnp.where(c == 0, one, two)
                give_ref[i, 2 * j : 2 * j + 2, :, lanes] = jnp.where(c == 0, two, one)


def core_sum_kernel(keep_ref, got_ref, out_ref):
    out_ref[...] = keep_ref[...] + got_ref[...]


def row_sum_kernel(got_ref, out_ref):
    out_ref[...] = (got_ref[0] + got_ref[1]) + (got_ref[2] + got_ref[3])


def spread_kernel(got_ref, out_ref):
    total = got_ref[0]
    for i in range(1, 8):
        total = total + got_ref[i]
    for i in range(8):
        out_ref[i] = total


def frame_gradient_kernel(dq_ref, dkv_ref, w_ref, out_ref):
    for j in range(4):
        rows = slice(256 * j, 256 * j + 256)
        dx = mm_bt(dq_ref[...], w_ref[rows, 0:INNER]) + mm_bt(dkv_ref[...], w_ref[rows, INNER:])
        out_ref[:, rows] = dx.astype(BF16)


def assemble_kernel(got_ref, qkv_ref, out_ref):
    for y in range(4):
        for c in range(2):
            rows = slice(16 * c, 16 * c + 16)
            piece = got_ref[2 * y + c]
            target = qkv_ref if y < 2 else out_ref
            target[rows, 384 * (y % 2) : 384 * (y % 2) + 384] = piece[:, 0:384]
            qkv_ref[rows, INNER + 384 * y : INNER + 384 * y + 384] = piece[:, 384:768]


def swap(a, axes):
    return lax.all_to_all(a, axes, 0, 0, tiled=True)


def shift(a, axis, s):
    n = lax.axis_size(axis)
    return lax.ppermute(a, axis, [(i, (i + s) % n) for i in range(n)])


def together(*values):
    return lax.optimization_barrier(values)


def per_device(frames, grad_frames, w_qkv, w_out):
    q, k, v, g, send, xdy = project(frames[0], grad_frames[0], w_qkv, w_out)
    xdy = lax.all_gather(xdy, "y")
    send, den, norm, w = denominators(swap(send, TM), q, k, g)
    send, dq, ds, *first = forward(swap(send, TM), q, k, v, g, den, norm, w)
    first = [first[0]] + [shift(a, "y", s) for s, a in enumerate(first) if s]
    x, chosen = call(stage_kernel, (xdy,), [bf16(1024, 512)] * 2, "stage", limit=LARGE_VMEM)
    got, first, x, chosen = together(swap(send, TM), first, x, chosen)
    second, dkv = backward(got, q, k, v, g, den, w, ds)
    second = swap(second, "y")
    out = [f32(4, 8, 16, 768)] * 2
    keep, give = call(weights_kernel, (x, chosen, *first, second), out, "weights")
    (part,) = call(core_sum_kernel, (keep, shift(give, "c", 1)), out[:1], "core_sum")
    (part,) = call(row_sum_kernel, (swap(part, "x"),), [f32(8, 16, 768)], "row_sum")
    (part,) = call(spread_kernel, (swap(part, "z"),), [f32(8, 16, 768)], "spread")
    part = swap(part, DP)
    (dx,) = call(frame_gradient_kernel, (dq, dkv, w_qkv), [bf16(BLOCK, 1024)], "frame_gradient", limit=LARGE_VMEM)
    grad_qkv, grad_out = call(assemble_kernel, (part,), [f32(32, 3 * INNER), f32(32, INNER)], "assemble")
    return dx[None], grad_qkv, grad_out


def solution(mesh):
    torus = Mesh(mesh.devices.reshape(8, 4, 4, 2), TM + DP)
    rows = P(DP, TM, None)
    return jax.shard_map(
        per_device,
        mesh=torus,
        in_specs=(rows, rows, P(), P()),
        out_specs=(rows, P(TM, None), P(TM, None)),
        check_vma=False,
    )
```

time: 176 us -> 170 us (0.966)
  blocking collectives: 32.7 us -> 98.6 us
  waiting for transfers between devices: 48.3 us -> 9.51 us
  starting transfers between devices: 49.1 us -> 23.6 us
  local copies, waits for them, and re-layouts: 5.97 us -> 0.69 us
  matrix products: 4.67 us -> 0 us
  Pallas kernels: 20.4 us -> 23.3 us
    all_to_all x2 -> x5, blocking collectives: 32.7 us -> 98.6 us  [swap(): return lax.all_to_all(a, axes, 0, 0, tiled=True)]
    all_to_all x5 -> x2, waiting for transfers between devices: 39.6 us -> 4.18 us  [swap(): return lax.all_to_all(a, axes, 0, 0, tiled=True)]
    all_to_all x5 -> x2, starting transfers between devices: 35.2 us -> 13.6 us  [swap(): return lax.all_to_all(a, axes, 0, 0, tiled=True)]
    unnamed x18 -> x8, local copies, waits for them, and re-layouts: 5.97 us -> 0.69 us
    dot_general x1 -> x0, matrix products: 4.67 us -> none  [per_device(): lax.dot_general(dqkv, w_qkv, (((1,), (1,)), ((), ())), preferred_element_...]
    ppermute x8 -> x4, starting transfers between devices: 13.9 us -> 9.96 us  [shift(): return lax.ppermute(a, axis, [(i, (i + s) % n) for i in range(n)])]
    ppermute x8 -> x4, waiting for transfers between devices: 8.64 us -> 5.31 us  [shift(): return lax.ppermute(a, axis, [(i, (i + s) % n) for i in range(n)])]
    pallas_call x10 -> x11, Pallas kernels: 20.4 us -> 23.3 us  [call(): pl.pallas_call(kernel, in_specs=in_specs or in_vmem(len(args)), out_specs...]
  transfers between devices with their start and end apart: 14 -> 7, of which waited for: 8 -> 4; matrix products, arithmetic and copies ran while one was open for 3% -> 0% of each run, Pallas kernels for 6% -> 8%
where the time goes in v3:
time: 170 us
  blocking collectives  98.6 us (58%)
  starting transfers between devices  23.6 us (14%)
  Pallas kernels  23.3 us (14%)
  between operations  14.1 us (8%)
  waiting for transfers between devices  9.51 us (6%)
    all_to_all x5, blocking collectives, swap(): return lax.all_to_all(a, axes, 0, 0, tiled=True)  98.6 us
    pallas_call x11, Pallas kernels, call(): pl.pallas_call(kernel, in_specs=in_specs or in_vmem(len(args)), out_specs...  23.3 us
    all_to_all x2, starting transfers between devices, swap(): return lax.all_to_all(a, axes, 0, 0, tiled=True)  13.6 us
    ppermute x4, starting transfers between devices, shift(): return lax.ppermute(a, axis, [(i, (i + s) % n) for i in range(n)])  9.96 us
    ppermute x4, waiting for transfers between devices, shift(): return lax.ppermute(a, axis, [(i, (i + s) % n) for i in range(n)])  5.31 us
    all_to_all x2, waiting for transfers between devices, swap(): return lax.all_to_all(a, axes, 0, 0, tiled=True)  4.18 us
  transfers between devices with their start and end apart: 7, of which 4 were waited for; matrix products, arithmetic and copies ran while one was open for 0% of the time, Pallas kernels for 8%

profile of v3, /device:TPU:1, one launch (start us, length us, event | category | flops | bytes accessed | tf_op | source)
XLA Modules:
  0.0 169.8 jit_solution(6360801131331040170)
XLA Ops:
  7.2 0.0 all-gather.3.cloned.1.call-start
  7.2 6.2 %project.1 = (bf16[128,768]{1,0:T(8,128)(2,1)S(1)}, bf16[128,768]{1,0:T(8,128)(2,1)S(1)}, bf16[128,768]{1,0:T(8,128)(2,1)S(1)}, bf16[128,768]{1,0:T(8,128)(2,1)S...) custom-call(bf16[128,1024]{1,0:T(8,128)(2,1)} %bitcast.6, bf16[128,1024]{1,0:T(8,128)(2,1)} %bitcast.7, ...), custom_call_target="tpu_custom_call" | custom-call | tf_op jit(solution)/shard_map/project/pallas_call | solution.py:84
  13.4 0.0 all-gather.3.cloned.1.call-update
  13.4 25.7 %all_to_all.35.got_ref = f32[32,24,128]{2,1,0:T(8,128)S(1)} all-to-all(f32[32,24,128]{2,1,0:T(8,128)} %get-tuple-element.35), channel_id=1, replica_groups=mesh['z'=8,'x'=4,'y'=4,'c'=2] {'z','x'}, dimensions={0} | all-to-all | bytes 786432 | tf_op jit(solution)/shard_map/all_to_all | solution.py:349
  39.1 1.7 %denominators.1 = (f32[32,32,128]{2,1,0:T(8,128)S(1)}, f32[128,768]{1,0:T(8,128)S(1)}, f32[8,128]{1,0:T(8,128)S(1)}, bf16[6,128,256]{2,1,0:T(8,128)(2,1)S(1)}) custom-call(f32[32,24,128]{2,1,0:T(8,128)S(1)} %all_to_all.35.got_ref, bf16[128,768]{1,0:T(8,128)(2,1)S(1)} %get-tuple-element.36.q_ref, bf16[128,768]{1,0:T(8,128)(2,1)S(1)} %get-tuple-element.37.k_ref, ...), custom_call_target="tpu_custom_call" | custom-call | tf_op jit(solution)/shard_map/denominators/pallas_call | solution.py:84
  40.9 20.1 %all_to_all.36.got_ref = f32[32,32,128]{2,1,0:T(8,128)S(1)} all-to-all(f32[32,32,128]{2,1,0:T(8,128)S(1)} %get-tuple-element.39), channel_id=1, replica_groups=mesh['z'=8,'x'=4,'y'=4,'c'=2] {'z','x'}, dimensions={0} | all-to-all | bytes 1048576 | tf_op jit(solution)/shard_map/all_to_all | solution.py:349
  60.9 3.0 %forward.1 = (f32[32,24,128]{2,1,0:T(8,128)}, bf16[128,768]{1,0:T(8,128)(2,1)S(1)}, bf16[6,256,128]{2,1,0:T(8,128)(2,1)S(1)}, f32[128,384]{1,0:T(8,128)S(1)}, f3...) custom-call(f32[32,32,128]{2,1,0:T(8,128)S(1)} %all_to_all.36.got_ref, ...), custom_call_target="tpu_custom_call" | custom-call | tf_op jit(solution)/shard_map/forward/pallas_call | solution.py:84
  63.9 6.2 %all-to-all-start.2 = ((f32[32,24,128]{2,1,0:T(8,128)}), f32[32,24,128]{2,1,0:T(8,128)S(1)}, u32[]{:S(2)}, u32[]{:S(2)}) async-start(f32[32,24,128]{2,1,0:T(8,128)} %get-tuple-element.45), calls=%async_computation.2 | async-start | bytes 786432 | tf_op jit(solution)/shard_map/all_to_all | solution.py:349
  70.1 1.4 collective-permute-start
  71.5 2.6 %collective-permute-start.1 = (f32[128,384]{1,0:T(8,128)}, f32[128,384]{1,0:T(8,128)S(1)}, u32[]{:S(2)}, u32[]{:S(2)}) collective-permute-start(f32[128,384]{1,0:T(8,128)} %get-tuple-element.48), channel_id=1, source_target_pairs={{0,4},{2,6},{4,0},{6,2},{1,5},{3,7},{5,1},{7,3},{8,12},{10,14},{12... | collective-permute-start | bytes 589832 | tf_op jit(solution)/shard_map/ppermute | solution.py:354
  74.1 1.1 collective-permute-start.2
  75.2 4.1 %stage.1 = (bf16[1024,512]{1,0:T(8,128)(2,1)}, bf16[1024,512]{1,0:T(8,128)(2,1)}) custom-call(f32[4,2,128,1024]{3,2,1,0:T(8,128)} %bitcast.4), custom_call_target="tpu_custom_call" | custom-call | tf_op jit(solution)/shard_map/stage/pallas_call | solution.py:84
  79.3 0.0 collective-permute-done.b1_ref
  79.3 2.3 %collective-permute-done.1.b2_ref = f32[128,384]{1,0:T(8,128)S(1)} collective-permute-done((f32[128,384]{1,0:T(8,128)}, f32[128,384]{1,0:T(8,128)S(1)}, u32[]{:S(2)}, u32[]{:S(2)}) %collective-permute-start.1) | collective-permute-done | bytes 196640 | tf_op jit(solution)/shard_map/ppermute | solution.py:354
  81.6 0.0 collective-permute-done.2.b3_ref
  81.6 0.7 copy-done.2
  82.3 0.8 all-to-all-done.2.got_ref
  83.0 0.6 backward.1
  83.6 12.5 %all_to_all.37.got_ref = f32[4,128,384]{2,1,0:T(8,128)S(1)} all-to-all(f32[4,128,384]{2,1,0:T(8,128)S(1)} %get-tuple-element.62), channel_id=1, replica_groups=mesh['z'=8,'x'=4,'y'=4,'c'=2] {'y'}, dimensions={0} | all-to-all | bytes 1572864 | tf_op jit(solution)/shard_map/all_to_all | solution.py:349
  96.2 0.0 copy-done.3
  96.2 1.3 weights.1
  97.4 4.9 %collective-permute-start.3 = (f32[4,8,16,768]{3,2,1,0:T(8,128)S(1)}, f32[4,8,16,768]{3,2,1,0:T(8,128)S(1)}, u32[]{:S(2)}, u32[]{:S(2)}) collective-permute-start(f32[4,8,16,768]{3,2,1,0:T(8,128)S(1)} %get-tuple-element.64), channel_id=1, source_target_pairs={{0,1},{1,0},{2,3},{3,2},{4,5},{5,4},{6,7},{7,6},{8,9},{9,8},{10,11... | collective-permute-start | bytes 4718600 | tf_op jit(solution)/shard_map/ppermute | solution.py:354
  102.3 3.0 %collective-permute-done.3.got_ref = f32[4,8,16,768]{3,2,1,0:T(8,128)S(1)} collective-permute-done((f32[4,8,16,768]{3,2,1,0:T(8,128)S(1)}, f32[4,8,16,768]{3,2,1,0:T(8,128)S(1)}, u32[]{:S(2)}, u32[]{:S(2)}) %collective-permute-start.3) | collective-permute-done | bytes 1572896 | tf_op jit(solution)/shard_map/ppermute | solution.py:354
  105.4 0.2 core_sum.1
  105.5 22.8 %all_to_all.38.got_ref = f32[4,8,16,768]{3,2,1,0:T(8,128)S(1)} all-to-all(f32[4,8,16,768]{3,2,1,0:T(8,128)S(1)} %core_sum.1), channel_id=1, replica_groups=mesh['z'=8,'x'=4,'y'=4,'c'=2] {'x'}, dimensions={0} | all-to-all | bytes 3145728 | tf_op jit(solution)/shard_map/all_to_all | solution.py:349
  128.3 0.1 row_sum.1
  128.4 17.5 %all_to_all.39.got_ref = f32[8,16,768]{2,1,0:T(8,128)S(1)} all-to-all(f32[8,16,768]{2,1,0:T(8,128)S(1)} %row_sum.1), channel_id=1, replica_groups=mesh['z'=8,'x'=4,'y'=4,'c'=2] {'z'}, dimensions={0} | all-to-all | bytes 786432 | tf_op jit(solution)/shard_map/all_to_all | solution.py:349
  145.9 0.8 spread.1
  146.7 7.4 %all-to-all-start.6 = ((f32[8,16,768]{2,1,0:T(8,128)}), f32[8,16,768]{2,1,0:T(8,128)S(1)}, u32[]{:S(2)}, u32[]{:S(2)}) async-start(f32[8,16,768]{2,1,0:T(8,128)} %spread.1), calls=%async_computation.6 | async-start | bytes 786432 | tf_op jit(solution)/shard_map/all_to_all | solution.py:349
  154.1 4.7 %frame_gradient.1 = bf16[128,1024]{1,0:T(8,128)(2,1)} custom-call(bf16[128,768]{1,0:T(8,128)(2,1)S(1)} %get-tuple-element.44.dq_ref, bf16[128,1536]{1,0:T(8,128)(2,1)S(1)} %get-tuple-element.55.dkv_ref, bf16[1024,2304]{1,0:T(8,128)(2,1)} %w_ref.1), custom_call_target="tpu_custom_call" | custom-call | tf_op jit(solution)/shard_map/frame_gradient/pallas_call | solution.py:84
  158.7 3.4 %all-to-all-done.6.got_ref = f32[8,16,768]{2,1,0:T(8,128)S(1)} async-done(((f32[8,16,768]{2,1,0:T(8,128)}), f32[8,16,768]{2,1,0:T(8,128)S(1)}, u32[]{:S(2)}, u32[]{:S(2)}) %all-to-all-start.6) | async-done | bytes 393248 | tf_op jit(solution)/shard_map/all_to_all | solution.py:349
  162.2 0.8 assemble.1
  (7 shorter events, 0.0 us)
Async XLA Ops:
  7.2 68.0 %all-gather.3.cloned.1.call-start = ((), (), s32[]{:S(2)}) async-start(), calls=%async_computation.7 | async-start | bytes 5242880 | tf_op jit(solution)/shard_map/all_gather | solution.py:363
  63.9 19.1 %all-to-all-start.2 = ((f32[32,24,128]{2,1,0:T(8,128)}), f32[32,24,128]{2,1,0:T(8,128)S(1)}, u32[]{:S(2)}, u32[]{:S(2)}) async-start(f32[32,24,128]{2,1,0:T(8,128)} %get-tuple-element.45), calls=%async_computation.2 | async-start | bytes 786432 | tf_op jit(solution)/shard_map/all_to_all | solution.py:349
  70.1 9.2 %collective-permute-start = (f32[128,384]{1,0:T(8,128)}, f32[128,384]{1,0:T(8,128)S(1)}, u32[]{:S(2)}, u32[]{:S(2)}) collective-permute-start(f32[128,384]{1,0:T(8,128)} %get-tuple-element.47), channel_id=1, source_target_pairs={{0,2},{2,4},{4,6},{6,0},{1,3},{3,5},{5,7},{7,1},{8,10},{10,12},{12... | collective-permute-start | bytes 589832 | tf_op jit(solution)/shard_map/ppermute | solution.py:354
  71.5 10.1 %collective-permute-start.1 = (f32[128,384]{1,0:T(8,128)}, f32[128,384]{1,0:T(8,128)S(1)}, u32[]{:S(2)}, u32[]{:S(2)}) collective-permute-start(f32[128,384]{1,0:T(8,128)} %get-tuple-element.48), channel_id=1, source_target_pairs={{0,4},{2,6},{4,0},{6,2},{1,5},{3,7},{5,1},{7,3},{8,12},{10,14},{12... | collective-permute-start | bytes 589832 | tf_op jit(solution)/shard_map/ppermute | solution.py:354
  74.1 7.5 %collective-permute-start.2 = (f32[128,384]{1,0:T(8,128)S(1)}, f32[128,384]{1,0:T(8,128)S(1)}, u32[]{:S(2)}, u32[]{:S(2)}) collective-permute-start(f32[128,384]{1,0:T(8,128)S(1)} %get-tuple-element.49), channel_id=1, source_target_pairs={{0,6},{2,0},{4,2},{6,4},{1,7},{3,1},{5,3},{7,5},{8,14},{10,8},{12,... | collective-permute-start | bytes 589832 | tf_op jit(solution)/shard_map/ppermute | solution.py:354
  81.6 0.7 copy-start.2
  83.0 13.1 %copy-start = (bf16[1024,512]{1,0:T(8,128)(2,1)S(1)}, bf16[1024,512]{1,0:T(8,128)(2,1)}, u32[]{:S(2)}) copy-start(bf16[1024,512]{1,0:T(8,128)(2,1)} %get-tuple-element.56.x_ref) | copy-start | bytes 3145732
  83.0 13.1 %copy-start.1 = (bf16[1024,512]{1,0:T(8,128)(2,1)S(1)}, bf16[1024,512]{1,0:T(8,128)(2,1)}, u32[]{:S(2)}) copy-start(bf16[1024,512]{1,0:T(8,128)(2,1)} %get-tuple-element.57.chosen_ref) | copy-start | bytes 3145732
  83.0 13.1 %copy-start.3 = (f32[128,384]{1,0:T(8,128)S(1)}, f32[128,384]{1,0:T(8,128)}, u32[]{:S(2)}) copy-start(f32[128,384]{1,0:T(8,128)} %copy-done.2) | copy-start | bytes 589828
  97.4 7.9 %collective-permute-start.3 = (f32[4,8,16,768]{3,2,1,0:T(8,128)S(1)}, f32[4,8,16,768]{3,2,1,0:T(8,128)S(1)}, u32[]{:S(2)}, u32[]{:S(2)}) collective-permute-start(f32[4,8,16,768]{3,2,1,0:T(8,128)S(1)} %get-tuple-element.64), channel_id=1, source_target_pairs={{0,1},{1,0},{2,3},{3,2},{4,5},{5,4},{6,7},{7,6},{8,9},{9,8},{10,11... | collective-permute-start | bytes 4718600 | tf_op jit(solution)/shard_map/ppermute | solution.py:354
  146.7 15.4 %all-to-all-start.6 = ((f32[8,16,768]{2,1,0:T(8,128)}), f32[8,16,768]{2,1,0:T(8,128)S(1)}, u32[]{:S(2)}, u32[]{:S(2)}) async-start(f32[8,16,768]{2,1,0:T(8,128)} %spread.1), calls=%async_computation.6 | async-start | bytes 786432 | tf_op jit(solution)/shard_map/all_to_all | solution.py:349
Sparse Core Ops, SparseCore 0:
  13.6 54.6 all-gather.2

commit v4 on v3

--- a/solution.py
+++ b/solution.py
@@ -17,6 +17,7 @@
 BF16 = jnp.bfloat16
 VMEM_LIMIT = 32 * 1024 * 1024
 LARGE_VMEM = 54300 * 1024
+KEYS_VMEM = 54600 * 1024
 
 
 def features(a):
@@ -96,72 +97,101 @@
     return lax.axis_index("z") * 4 + lax.axis_index("x")
 
 
-def project_kernel(
-    x_hbm, dy_hbm, w_hbm, wo_hbm, q_ref, k_ref, v_ref, g_ref, send_ref, xdy_ref,
-    x_ref, dy_ref, w_ref, wo_ref, frame_sem, weight_sem,
+def keys_kernel(
+    x_hbm, dy_hbm, w_hbm, k_ref, v_ref, send_ref, xdy_ref, x_ref, dy_ref, w_ref, sum_ref, frame_sem, weight_sem
 ):
-    frames = [
-        pltpu.make_async_copy(x_hbm, x_ref, frame_sem.at[0]),
-        pltpu.make_async_copy(dy_hbm, dy_ref, frame_sem.at[1]),
-    ]
-    for copy in frames:
-        copy.start()
-
-    def fetch(step):
-        copies = []
-        for kind, first in enumerate((INNER, 2 * INNER, 0)):
-            columns = pl.ds(first + 256 * step, 256)
-            sem = weight_sem.at[step, kind]
-            copies.append(pltpu.make_async_copy(w_hbm.at[:, columns], w_ref.at[:, columns], sem))
-        lanes = pl.ds(256 * step, 256)
-        copies.append(pltpu.make_async_copy(wo_hbm.at[:, lanes], wo_ref.at[:, lanes], weight_sem.at[step, 3]))
-        for copy in copies:
-            copy.start()
-        return copies
-
-    copies = fetch(0)
+    x_copy = pltpu.make_async_copy(x_hbm, x_ref, frame_sem.at[0])
+    dy_copy = pltpu.make_async_copy(dy_hbm, dy_ref, frame_sem.at[1])
+    x_copy.start()
+    copies = []
+    for i in range(4):
+        rows = pl.ds(256 * i, 256)
+        source = w_hbm.at[rows, pl.ds(INNER, 2 * INNER)]
+        copies.append(pltpu.make_async_copy(source, w_ref.at[rows], weight_sem.at[i]))
+        copies[-1].start()
+    dy_copy.start()
     send_ref[24:32, 0:16, :] = jnp.zeros((8, 16, 128), F32)
-    send_ref[:, 22:24, :] = jnp.zeros((32, 2, 128), F32)
-    for copy in frames:
-        copy.wait()
+    x_copy.wait()
     x = x_ref[...]
-    dy = dy_ref[...]
     xdy_ref[0] = x.astype(F32)
-    xdy_ref[1] = dy.astype(F32)
-    for step in range(3):
-        lanes = slice(256 * step, 256 * step + 256)
-        for copy in copies:
-            copy.wait()
-        if step < 2:
-            copies = fetch(step + 1)
-        k = mm(x, w_ref[:, slice(INNER + 256 * step, INNER + 256 * step + 256)]).astype(BF16)
+    for i in range(4):
+        rows = slice(256 * i, 256 * i + 256)
+        copies[i].wait()
+        part = mm(x[:, rows], w_ref[rows, :])
+        sum_ref[...] = part if i == 0 else sum_ref[...] + part
+    norms = []
+    for p in range(PAIRS):
+        lanes = slice(128 * p, 128 * p + 128)
+        k = sum_ref[:, lanes].astype(BF16)
+        v = sum_ref[:, slice(INNER + 128 * p, INNER + 128 * p + 128)].astype(BF16)
         k_ref[:, lanes] = k
-        v = mm(x, w_ref[:, slice(2 * INNER + 256 * step, 2 * INNER + 256 * step + 256)]).astype(BF16)
         v_ref[:, lanes] = v
         fk = features(k.astype(F32)).astype(BF16)
-        for i in range(2):
-            part = slice(128 * i, 128 * i + 128)
-            state = diagonal_blocks(mm_at(fk[:, part], v[:, part]))
-            norm = jnp.sum(fk[:, part].astype(F32), axis=0, keepdims=True)
-            pair = 2 * step + i
-            send_ref[4 * pair : 4 * pair + 4, 0:16, :] = state.reshape(4, 16, 128)
-            for t in range(32):
-                send_ref[t, 16 + pair : 17 + pair, :] = norm
-        q_ref[:, lanes] = mm(x, w_ref[:, lanes]).astype(BF16)
-        g_ref[:, lanes] = mm(dy, wo_ref[:, lanes]).astype(BF16)
-
-
-def project(x, dy, w_qkv, w_out):
+        state = diagonal_blocks(mm_at(fk, v))
+        send_ref[4 * p : 4 * p + 4, 0:16, :] = state.reshape(4, 16, 128)
+        norms.append(jnp.sum(fk.astype(F32), axis=0, keepdims=True))
+    norm = jnp.concatenate(norms + [jnp.zeros((2, 128), F32)], axis=0)
+    for t in range(32):
+        send_ref[t, 16:24, :] = norm
+    dy_copy.wait()
+    xdy_ref[1] = dy_ref[...].astype(F32)
+
+
+def keys(x, dy, w_qkv):
     rows, width = x.shape
-    scratch = [pltpu.VMEM(a.shape, BF16) for a in (x, dy, w_qkv, w_out)]
-    scratch += [pltpu.SemaphoreType.DMA((2,)), pltpu.SemaphoreType.DMA((3, 4))]
-    outs = [bf16(rows, INNER)] * 4 + [f32(32, 24, 128), f32(2, rows, width)]
-    return call(
-        project_kernel, (x, dy, w_qkv, w_out), outs, "project", scratch, in_hbm(4), LARGE_VMEM
-    )
-
-
-def denominators_kernel(got_ref, q_ref, k_ref, g_ref, send_ref, den_ref, norm_ref, w_ref):
+    scratch = [pltpu.VMEM((rows, width), BF16)] * 2 + [pltpu.VMEM((width, 2 * INNER), BF16)]
+    scratch += [pltpu.VMEM((rows, 2 * INNER), F32)]
+    scratch += [pltpu.SemaphoreType.DMA((2,)), pltpu.SemaphoreType.DMA((4,))]
+    outs = [bf16(rows, INNER)] * 2 + [f32(32, 24, 128), f32(2, rows, width)]
+    return call(keys_kernel, (x, dy, w_qkv), outs, "keys", scratch, in_hbm(3), KEYS_VMEM)
+
+
+def queries_kernel(
+    x_hbm, dy_hbm, w_hbm, wo_hbm, k_ref, q_ref, g_ref, w_ref, sums_ref,
+    x_ref, dy_ref, wq_ref, wo_ref, sems,
+):
+    copies = [
+        pltpu.make_async_copy(x_hbm, x_ref, sems.at[0]),
+        pltpu.make_async_copy(w_hbm.at[:, pl.ds(0, INNER)], wq_ref, sems.at[1]),
+        pltpu.make_async_copy(dy_hbm, dy_ref, sems.at[2]),
+        pltpu.make_async_copy(wo_hbm, wo_ref, sems.at[3]),
+    ]
+    for copy in copies:
+        copy.start()
+    copies[0].wait()
+    copies[1].wait()
+    mask = causal()
+    lane = lax.broadcasted_iota(jnp.int32, (BLOCK, 128), 1)
+    packed = jnp.zeros((BLOCK, 128), F32)
+    for step in range(3):
+        wide = slice(256 * step, 256 * step + 256)
+        q_ref[:, wide] = mm(x_ref[...], wq_ref[:, wide]).astype(BF16)
+        for p in (2 * step, 2 * step + 1):
+            lanes = slice(128 * p, 128 * p + 128)
+            fq = features(q_ref[:, lanes].astype(F32)).astype(BF16)
+            fk = features(k_ref[:, lanes].astype(F32)).astype(BF16)
+            for half, rows in enumerate(split_pair(fq)):
+                scores = jnp.where(mask, mm_bt(rows, fk), 0.0)
+                w_ref[p, :, 128 * half : 128 * half + 128] = scores.astype(BF16)
+                packed = jnp.where(lane == 2 * p + half, jnp.sum(scores, axis=1, keepdims=True), packed)
+    sums_ref[...] = packed
+    copies[2].wait()
+    copies[3].wait()
+    for step in range(3):
+        wide = slice(256 * step, 256 * step + 256)
+        g_ref[:, wide] = mm(dy_ref[...], wo_ref[:, wide]).astype(BF16)
+
+
+def queries(x, dy, w_qkv, w_out, k):
+    rows, width = x.shape
+    scratch = [pltpu.VMEM((rows, width), BF16)] * 2 + [pltpu.VMEM((width, INNER), BF16)] * 2
+    scratch += [pltpu.SemaphoreType.DMA((4,))]
+    outs = [bf16(rows, INNER)] * 2 + [bf16(PAIRS, BLOCK, 256), f32(BLOCK, 128)]
+    specs = in_hbm(4) + in_vmem(1)
+    return call(queries_kernel, (x, dy, w_qkv, w_out, k), outs, "queries", scratch, specs, LARGE_VMEM)
+
+
+def denominators_kernel(got_ref, q_ref, g_ref, sums_ref, send_ref, inverse_ref, dnum_ref, norm_ref):
     me = time_index()
     carry = jnp.zeros((16, 128), F32)
     norms = jnp.zeros((8, 128), F32)
@@ -170,33 +200,33 @@
         carry = carry + got_ref[t, 0:16, :]
         norms = norms + jnp.where(t < me, got_ref[t, 16:24, :], 0.0)
     norm_ref[...] = norms
-    mask = causal()
+    lane = lax.broadcasted_iota(jnp.int32, (BLOCK, 128), 1)
+    packed = jnp.ones((BLOCK, 128), F32)
     for p in range(PAIRS):
         lanes = slice(128 * p, 128 * p + 128)
-        fq32 = features(q_ref[:, lanes].astype(F32))
-        fq = fq32.astype(BF16)
-        fk = features(k_ref[:, lanes].astype(F32)).astype(BF16)
-        fq_norm = fq.astype(F32) * norms[p : p + 1, :]
-        sums = []
-        for half, (rows, extra) in enumerate(zip(split_pair(fq), split_pair(fq_norm))):
-            scores = jnp.where(mask, mm_bt(rows, fk), 0.0)
-            w_ref[p, :, 128 * half : 128 * half + 128] = scores.astype(BF16)
-            sums.append(jnp.sum(scores + extra, axis=1, keepdims=True))
-        den = jnp.where(low_lanes((BLOCK, 128)), sums[0], sums[1])
-        den_ref[:, lanes] = den
+        fq = features(q_ref[:, lanes].astype(F32)).astype(BF16)
+        dots = [
+            jnp.sum(a, axis=1, keepdims=True) + sums_ref[:, 2 * p + half : 2 * p + half + 1]
+            for half, a in enumerate(split_pair(fq.astype(F32) * norms[p : p + 1, :]))
+        ]
+        for half in range(2):
+            packed = jnp.where(lane == 2 * p + half, dots[half], packed)
+        den = jnp.where(low_lanes((BLOCK, 128)), dots[0], dots[1])
         dnum = (g_ref[:, lanes].astype(F32) / den).astype(BF16)
+        dnum_ref[:, lanes] = dnum
         dstate = diagonal_blocks(mm_at(fq, dnum))
         send_ref[4 * p : 4 * p + 4, 16:32, :] = dstate.reshape(4, 16, 128)
+    inverse_ref[...] = 1.0 / packed
     send_ref[24:32, 16:32, :] = jnp.zeros((8, 16, 128), F32)
 
 
 def denominators(*args):
-    outs = [f32(32, 32, 128), f32(BLOCK, INNER), f32(8, 128), bf16(PAIRS, BLOCK, 256)]
+    outs = [f32(32, 32, 128), f32(BLOCK, 128), bf16(BLOCK, INNER), f32(8, 128)]
     return call(denominators_kernel, args, outs, "denominators")
 
 
 def forward_kernel(
-    got_ref, q_ref, k_ref, v_ref, g_ref, den_ref, norm_ref, w_ref,
+    got_ref, q_ref, k_ref, v_ref, g_ref, inverse_ref, dnum_ref, norm_ref, w_ref,
     send_ref, dq_ref, ds_ref, b0_ref, b1_ref, b2_ref, b3_ref, out_ref,
 ):
     carry = jnp.zeros((16, 128), F32)
@@ -214,12 +244,14 @@
         fk = features(k_ref[:, lanes].astype(F32)).astype(BF16)
         v = v_ref[:, lanes]
         g = g_ref[:, lanes].astype(F32)
-        inverse = 1.0 / den_ref[:, lanes]
+        inverse = jnp.where(
+            low, inverse_ref[:, 2 * p : 2 * p + 1], inverse_ref[:, 2 * p + 1 : 2 * p + 2]
+        )
         state = block_diagonal(got_ref[4 * p : 4 * p + 4, 0:16, :].reshape(64, 128).astype(BF16))
         v_halves = jnp.concatenate(split_pair(v), axis=0)
         ratio = (mm(w_ref[p], v_halves) + mm(fq, state)) * inverse
         out_ref[2 + block, :, part] = ratio.astype(BF16).astype(F32)
-        dnum = (g * inverse).astype(BF16)
+        dnum = dnum_ref[:, lanes]
         sums = [jnp.sum(a, axis=1, keepdims=True) for a in split_pair(g * ratio)]
         dden = -jnp.where(low, sums[0], sums[1]) * inverse
         ddens = (dden[:, 0:1], dden[:, 127:128])
@@ -251,7 +283,7 @@
 
 
 def backward_kernel(
-    got_ref, q_ref, k_ref, v_ref, g_ref, den_ref, w_ref, ds_ref, out_ref, dkv_ref
+    got_ref, q_ref, k_ref, v_ref, dnum_ref, w_ref, ds_ref, out_ref, dkv_ref
 ):
     me = time_index()
     dnorms = jnp.zeros((8, 128), F32)
@@ -264,7 +296,7 @@
         k = k_ref[:, lanes].astype(F32)
         fk = features(k).astype(BF16)
         v = v_ref[:, lanes]
-        dnum = (g_ref[:, lanes].astype(F32) * (1.0 / den_ref[:, lanes])).astype(BF16)
+        dnum = dnum_ref[:, lanes]
         dstate = block_diagonal(got_ref[4 * p : 4 * p + 4, 0:16, :].reshape(64, 128).astype(BF16))
         dfk = (
             mm_at(ds_ref[p], jnp.concatenate(split_pair(fq), axis=0))
@@ -359,14 +391,16 @@
 
 
 def per_device(frames, grad_frames, w_qkv, w_out):
-    q, k, v, g, send, xdy = project(frames[0], grad_frames[0], w_qkv, w_out)
+    k, v, send, xdy = keys(frames[0], grad_frames[0], w_qkv)
     xdy = lax.all_gather(xdy, "y")
-    send, den, norm, w = denominators(swap(send, TM), q, k, g)
-    send, dq, ds, *first = forward(swap(send, TM), q, k, v, g, den, norm, w)
+    q, g, w, sums = queries(frames[0], grad_frames[0], w_qkv, w_out, k)
+    got, q, g, w, sums = together(swap(send, TM), q, g, w, sums)
+    send, inverse, dnum, norm = denominators(got, q, g, sums)
+    send, dq, ds, *first = forward(swap(send, TM), q, k, v, g, inverse, dnum, norm, w)
     first = [first[0]] + [shift(a, "y", s) for s, a in enumerate(first) if s]
     x, chosen = call(stage_kernel, (xdy,), [bf16(1024, 512)] * 2, "stage", limit=LARGE_VMEM)
     got, first, x, chosen = together(swap(send, TM), first, x, chosen)
-    second, dkv = backward(got, q, k, v, g, den, w, ds)
+    second, dkv = backward(got, q, k, v, dnum, w, ds)
     second = swap(second, "y")
     out = [f32(4, 8, 16, 768)] * 2
     keep, give = call(weights_kernel, (x, chosen, *first, second), out, "weights")

time: 170 us -> 166 us (0.976)
  blocking collectives: 98.6 us -> 71.9 us
  starting transfers between devices: 23.6 us -> 35.6 us
  waiting for transfers between devices: 9.51 us -> 20.9 us
    all_to_all x5 -> x4, blocking collectives: 98.6 us -> 71.9 us  [swap(): return lax.all_to_all(a, axes, 0, 0, tiled=True)]
    all_to_all x2 -> x3, starting transfers between devices: 13.6 us -> 25.6 us  [swap(): return lax.all_to_all(a, axes, 0, 0, tiled=True)]
    all_to_all x2 -> x3, waiting for transfers between devices: 4.18 us -> 15.8 us  [swap(): return lax.all_to_all(a, axes, 0, 0, tiled=True)]
    pallas_call x11 -> x12, Pallas kernels: 23.3 us -> 23.1 us  [call(): pl.pallas_call(kernel, in_specs=in_specs or in_vmem(len(args)), out_specs...]
  transfers between devices with their start and end apart: 7 -> 8, of which waited for: 4 -> 5; matrix products, arithmetic and copies ran while one was open for 0% -> 0% of each run, Pallas kernels for 8% -> 10%
where the time goes in v4:
time: 166 us
  blocking collectives  71.9 us (43%)
  starting transfers between devices  35.6 us (21%)
  Pallas kernels  23.1 us (14%)
  waiting for transfers between devices  20.9 us (13%)
  between operations  14.1 us (8%)
    all_to_all x4, blocking collectives, swap(): return lax.all_to_all(a, axes, 0, 0, tiled=True)  71.9 us
    all_to_all x3, starting transfers between devices, swap(): return lax.all_to_all(a, axes, 0, 0, tiled=True)  25.6 us
    pallas_call x12, Pallas kernels, call(): pl.pallas_call(kernel, in_specs=in_specs or in_vmem(len(args)), out_specs...  23.1 us
    all_to_all x3, waiting for transfers between devices, swap(): return lax.all_to_all(a, axes, 0, 0, tiled=True)  15.8 us
    ppermute x4, starting transfers between devices, shift(): return lax.ppermute(a, axis, [(i, (i + s) % n) for i in range(n)])  9.97 us
    ppermute x4, waiting for transfers between devices, shift(): return lax.ppermute(a, axis, [(i, (i + s) % n) for i in range(n)])  5.11 us
  transfers between devices with their start and end apart: 8, of which 5 were waited for; matrix products, arithmetic and copies ran while one was open for 0% of the time, Pallas kernels for 10%

profile of v4, /device:TPU:1, one launch (start us, length us, event | category | flops | bytes accessed | tf_op | source)
XLA Modules:
  0.0 165.6 jit_solution(603825917438514857)
XLA Ops:
  7.2 0.0 all-gather.3.cloned.1.call-start
  7.2 3.7 %keys.1 = (bf16[128,768]{1,0:T(8,128)(2,1)S(1)}, bf16[128,768]{1,0:T(8,128)(2,1)S(1)}, f32[32,24,128]{2,1,0:T(8,128)}, f32[2,128,1024]{2,1,0:T(8,128)}) custom-call(bf16[128,1024]{1,0:T(8,128)(2,1)} %bitcast.4, bf16[128,1024]{1,0:T(8,128)(2,1)} %bitcast.7, bf16[1024,2304]{1,0:T(8,128)(2,1)} %w_ref.1), custom_call_target="tpu_custom_call" | custom-call | tf_op jit(solution)/shard_map/keys/pallas_call | solution.py:85
  10.9 0.0 copy-start.3
  10.9 0.0 all-gather.3.cloned.1.call-update
  10.9 12.0 %all-to-all-start = ((f32[32,24,128]{2,1,0:T(8,128)}), f32[32,24,128]{2,1,0:T(8,128)S(1)}, u32[]{:S(2)}, u32[]{:S(2)}) async-start(f32[32,24,128]{2,1,0:T(8,128)} %get-tuple-element.42), calls=%async_computation | async-start | bytes 786432 | tf_op jit(solution)/shard_map/all_to_all | solution.py:381
  22.9 3.1 %queries.1 = (bf16[128,768]{1,0:T(8,128)(2,1)S(1)}, bf16[128,768]{1,0:T(8,128)(2,1)S(1)}, bf16[6,128,256]{2,1,0:T(8,128)(2,1)}, f32[128,128]{1,0:T(8,128)S(1)}) custom-call(bf16[128,1024]{1,0:T(8,128)(2,1)S(1)} %bitcast.5, bf16[128,1024]{1,0:T(8,128)(2,1)} %bitcast.8, bf16[1024,2304]{1,0:T(8,128)(2,1)} %w_ref.1, bf16[1024,768]{1,0:T(8,128)(2,1)} %wo_hbm.1, ...), custom_call_target="tpu_custom_call" | custom-call | tf_op jit(solution)/shard_map/queries/pallas_call | solution.py:85
  26.0 10.7 %all-to-all-done.got_ref = f32[32,24,128]{2,1,0:T(8,128)S(1)} async-done(((f32[32,24,128]{2,1,0:T(8,128)}), f32[32,24,128]{2,1,0:T(8,128)S(1)}, u32[]{:S(2)}, u32[]{:S(2)}) %all-to-all-start) | async-done | bytes 393248 | tf_op jit(solution)/shard_map/all_to_all | solution.py:381
  36.7 1.1 denominators.1
  37.8 20.1 %all_to_all.35.got_ref = f32[32,32,128]{2,1,0:T(8,128)S(1)} all-to-all(f32[32,32,128]{2,1,0:T(8,128)S(1)} %get-tuple-element.52), channel_id=1, replica_groups=mesh['z'=8,'x'=4,'y'=4,'c'=2] {'z','x'}, dimensions={0} | all-to-all | bytes 1048576 | tf_op jit(solution)/shard_map/all_to_all | solution.py:381
  57.9 2.9 %forward.1 = (f32[32,24,128]{2,1,0:T(8,128)}, bf16[128,768]{1,0:T(8,128)(2,1)S(1)}, bf16[6,256,128]{2,1,0:T(8,128)(2,1)S(1)}, f32[128,384]{1,0:T(8,128)S(1)}, f3...) custom-call(f32[32,32,128]{2,1,0:T(8,128)S(1)} %all_to_all.35.got_ref, ...), custom_call_target="tpu_custom_call" | custom-call | tf_op jit(solution)/shard_map/forward/pallas_call | solution.py:85
  60.8 6.2 %all-to-all-start.2 = ((f32[32,24,128]{2,1,0:T(8,128)}), f32[32,24,128]{2,1,0:T(8,128)S(1)}, u32[]{:S(2)}, u32[]{:S(2)}) async-start(f32[32,24,128]{2,1,0:T(8,128)} %get-tuple-element.59), calls=%async_computation.2 | async-start | bytes 786432 | tf_op jit(solution)/shard_map/all_to_all | solution.py:381
  67.0 1.4 collective-permute-start
  68.4 2.6 %collective-permute-start.1 = (f32[128,384]{1,0:T(8,128)S(1)}, f32[128,384]{1,0:T(8,128)S(1)}, u32[]{:S(2)}, u32[]{:S(2)}) collective-permute-start(f32[128,384]{1,0:T(8,128)S(1)} %get-tuple-element.62), channel_id=1, source_target_pairs={{0,4},{2,6},{4,0},{6,2},{1,5},{3,7},{5,1},{7,3},{8,12},{10,14},{12... | collective-permute-start | bytes 589832 | tf_op jit(solution)/shard_map/ppermute | solution.py:386
  71.0 1.1 collective-permute-start.2
  72.1 4.1 %stage.1 = (bf16[1024,512]{1,0:T(8,128)(2,1)}, bf16[1024,512]{1,0:T(8,128)(2,1)}) custom-call(f32[4,2,128,1024]{3,2,1,0:T(8,128)} %bitcast.6), custom_call_target="tpu_custom_call" | custom-call | tf_op jit(solution)/shard_map/stage/pallas_call | solution.py:85
  76.2 2.1 %collective-permute-done.1.b2_ref = f32[128,384]{1,0:T(8,128)S(1)} collective-permute-done((f32[128,384]{1,0:T(8,128)S(1)}, f32[128,384]{1,0:T(8,128)S(1)}, u32[]{:S(2)}, u32[]{:S(2)}) %collective-permute-start.1) | collective-permute-done | bytes 196640 | tf_op jit(solution)/shard_map/ppermute | solution.py:386
  78.3 0.0 collective-permute-done.2.b3_ref
  78.3 1.6 all-to-all-done.2.got_ref
  79.9 0.6 backward.1
  80.5 12.5 %all_to_all.36.got_ref = f32[4,128,384]{2,1,0:T(8,128)S(1)} all-to-all(f32[4,128,384]{2,1,0:T(8,128)S(1)} %get-tuple-element.76), channel_id=1, replica_groups=mesh['z'=8,'x'=4,'y'=4,'c'=2] {'y'}, dimensions={0} | all-to-all | bytes 1572864 | tf_op jit(solution)/shard_map/all_to_all | solution.py:381
  93.0 1.2 weights.1
  94.3 4.9 %collective-permute-start.3 = (f32[4,8,16,768]{3,2,1,0:T(8,128)S(1)}, f32[4,8,16,768]{3,2,1,0:T(8,128)S(1)}, u32[]{:S(2)}, u32[]{:S(2)}) collective-permute-start(f32[4,8,16,768]{3,2,1,0:T(8,128)S(1)} %get-tuple-element.78), channel_id=1, source_target_pairs={{0,1},{1,0},{2,3},{3,2},{4,5},{5,4},{6,7},{7,6},{8,9},{9,8},{10,11... | collective-permute-start | bytes 4718600 | tf_op jit(solution)/shard_map/ppermute | solution.py:386
  99.2 3.0 %collective-permute-done.3.got_ref = f32[4,8,16,768]{3,2,1,0:T(8,128)S(1)} collective-permute-done((f32[4,8,16,768]{3,2,1,0:T(8,128)S(1)}, f32[4,8,16,768]{3,2,1,0:T(8,128)S(1)}, u32[]{:S(2)}, u32[]{:S(2)}) %collective-permute-start.3) | collective-permute-done | bytes 1572896 | tf_op jit(solution)/shard_map/ppermute | solution.py:386
  102.2 0.2 core_sum.1
  102.4 22.8 %all_to_all.37.got_ref = f32[4,8,16,768]{3,2,1,0:T(8,128)S(1)} all-to-all(f32[4,8,16,768]{3,2,1,0:T(8,128)S(1)} %core_sum.1), channel_id=1, replica_groups=mesh['z'=8,'x'=4,'y'=4,'c'=2] {'x'}, dimensions={0} | all-to-all | bytes 3145728 | tf_op jit(solution)/shard_map/all_to_all | solution.py:381
  125.2 0.1 row_sum.1
  125.3 16.5 %all_to_all.38.got_ref = f32[8,16,768]{2,1,0:T(8,128)S(1)} all-to-all(f32[8,16,768]{2,1,0:T(8,128)S(1)} %row_sum.1), channel_id=1, replica_groups=mesh['z'=8,'x'=4,'y'=4,'c'=2] {'z'}, dimensions={0} | all-to-all | bytes 786432 | tf_op jit(solution)/shard_map/all_to_all | solution.py:381
  141.8 0.8 spread.1
  142.6 7.4 %all-to-all-start.6 = ((f32[8,16,768]{2,1,0:T(8,128)}), f32[8,16,768]{2,1,0:T(8,128)S(1)}, u32[]{:S(2)}, u32[]{:S(2)}) async-start(f32[8,16,768]{2,1,0:T(8,128)} %spread.1), calls=%async_computation.6 | async-start | bytes 786432 | tf_op jit(solution)/shard_map/all_to_all | solution.py:381
  149.9 4.7 %frame_gradient.1 = bf16[128,1024]{1,0:T(8,128)(2,1)} custom-call(bf16[128,768]{1,0:T(8,128)(2,1)S(1)} %get-tuple-element.58.dq_ref, bf16[128,1536]{1,0:T(8,128)(2,1)S(1)} %get-tuple-element.69.dkv_ref, bf16[1024,2304]{1,0:T(8,128)(2,1)} %w_ref.1), custom_call_target="tpu_custom_call" | custom-call | tf_op jit(solution)/shard_map/frame_gradient/pallas_call | solution.py:85
  154.6 3.4 %all-to-all-done.6.got_ref = f32[8,16,768]{2,1,0:T(8,128)S(1)} async-done(((f32[8,16,768]{2,1,0:T(8,128)}), f32[8,16,768]{2,1,0:T(8,128)S(1)}, u32[]{:S(2)}, u32[]{:S(2)}) %all-to-all-start.6) | async-done | bytes 393248 | tf_op jit(solution)/shard_map/all_to_all | solution.py:381
  158.0 0.8 assemble.1
  (9 shorter events, 0.0 us)
Async XLA Ops:
  7.2 64.9 %all-gather.3.cloned.1.call-start = ((), (), s32[]{:S(2)}) async-start(), calls=%async_computation.7 | async-start | bytes 5242880 | tf_op jit(solution)/shard_map/all_gather | solution.py:395
  10.9 12.1 %copy-start.3 = (bf16[1,128,1024]{2,1,0:T(8,128)(2,1)S(1)}, bf16[1,128,1024]{2,1,0:T(8,128)(2,1)}, u32[]{:S(2)}) copy-start(bf16[1,128,1024]{2,1,0:T(8,128)(2,1)} %param.4) | copy-start | bytes 786436
  10.9 25.8 %all-to-all-start = ((f32[32,24,128]{2,1,0:T(8,128)}), f32[32,24,128]{2,1,0:T(8,128)S(1)}, u32[]{:S(2)}, u32[]{:S(2)}) async-start(f32[32,24,128]{2,1,0:T(8,128)} %get-tuple-element.42), calls=%async_computation | async-start | bytes 786432 | tf_op jit(solution)/shard_map/all_to_all | solution.py:381
  26.0 31.9 %copy-start = (bf16[6,128,256]{2,1,0:T(8,128)(2,1)S(1)}, bf16[6,128,256]{2,1,0:T(8,128)(2,1)}, u32[]{:S(2)}) copy-start(bf16[6,128,256]{2,1,0:T(8,128)(2,1)} %get-tuple-element.57.w_ref) | copy-start | bytes 1179652
  60.8 19.1 %all-to-all-start.2 = ((f32[32,24,128]{2,1,0:T(8,128)}), f32[32,24,128]{2,1,0:T(8,128)S(1)}, u32[]{:S(2)}, u32[]{:S(2)}) async-start(f32[32,24,128]{2,1,0:T(8,128)} %get-tuple-element.59), calls=%async_computation.2 | async-start | bytes 786432 | tf_op jit(solution)/shard_map/all_to_all | solution.py:381
  67.0 9.2 %collective-permute-start = (f32[128,384]{1,0:T(8,128)S(1)}, f32[128,384]{1,0:T(8,128)S(1)}, u32[]{:S(2)}, u32[]{:S(2)}) collective-permute-start(f32[128,384]{1,0:T(8,128)S(1)} %get-tuple-element.61), channel_id=1, source_target_pairs={{0,2},{2,4},{4,6},{6,0},{1,3},{3,5},{5,7},{7,1},{8,10},{10,12},{12... | collective-permute-start | bytes 589832 | tf_op jit(solution)/shard_map/ppermute | solution.py:386
  68.4 9.9 %collective-permute-start.1 = (f32[128,384]{1,0:T(8,128)S(1)}, f32[128,384]{1,0:T(8,128)S(1)}, u32[]{:S(2)}, u32[]{:S(2)}) collective-permute-start(f32[128,384]{1,0:T(8,128)S(1)} %get-tuple-element.62), channel_id=1, source_target_pairs={{0,4},{2,6},{4,0},{6,2},{1,5},{3,7},{5,1},{7,3},{8,12},{10,14},{12... | collective-permute-start | bytes 589832 | tf_op jit(solution)/shard_map/ppermute | solution.py:386
  71.0 7.3 %collective-permute-start.2 = (f32[128,384]{1,0:T(8,128)S(1)}, f32[128,384]{1,0:T(8,128)S(1)}, u32[]{:S(2)}, u32[]{:S(2)}) collective-permute-start(f32[128,384]{1,0:T(8,128)S(1)} %get-tuple-element.63), channel_id=1, source_target_pairs={{0,6},{2,0},{4,2},{6,4},{1,7},{3,1},{5,3},{7,5},{8,14},{10,8},{12,... | collective-permute-start | bytes 589832 | tf_op jit(solution)/shard_map/ppermute | solution.py:386
  79.9 13.1 %copy-start.1 = (bf16[1024,512]{1,0:T(8,128)(2,1)S(1)}, bf16[1024,512]{1,0:T(8,128)(2,1)}, u32[]{:S(2)}) copy-start(bf16[1024,512]{1,0:T(8,128)(2,1)} %get-tuple-element.70.x_ref) | copy-start | bytes 3145732
  79.9 13.1 %copy-start.2 = (bf16[1024,512]{1,0:T(8,128)(2,1)S(1)}, bf16[1024,512]{1,0:T(8,128)(2,1)}, u32[]{:S(2)}) copy-start(bf16[1024,512]{1,0:T(8,128)(2,1)} %get-tuple-element.71.chosen_ref) | copy-start | bytes 3145732
  94.3 7.9 %collective-permute-start.3 = (f32[4,8,16,768]{3,2,1,0:T(8,128)S(1)}, f32[4,8,16,768]{3,2,1,0:T(8,128)S(1)}, u32[]{:S(2)}, u32[]{:S(2)}) collective-permute-start(f32[4,8,16,768]{3,2,1,0:T(8,128)S(1)} %get-tuple-element.78), channel_id=1, source_target_pairs={{0,1},{1,0},{2,3},{3,2},{4,5},{5,4},{6,7},{7,6},{8,9},{9,8},{10,11... | collective-permute-start | bytes 4718600 | tf_op jit(solution)/shard_map/ppermute | solution.py:386
  142.6 15.4 %all-to-all-start.6 = ((f32[8,16,768]{2,1,0:T(8,128)}), f32[8,16,768]{2,1,0:T(8,128)S(1)}, u32[]{:S(2)}, u32[]{:S(2)}) async-start(f32[8,16,768]{2,1,0:T(8,128)} %spread.1), calls=%async_computation.6 | async-start | bytes 786432 | tf_op jit(solution)/shard_map/all_to_all | solution.py:381
Sparse Core Ops, SparseCore 0:
  11.0 54.7 all-gather.2

commit v5 on v4

--- a/solution.py
+++ b/solution.py
@@ -93,12 +93,25 @@
     )(*args)
 
 
+def scatter_rows(state_ref, send_ref, first):
+    for t in range(32):
+        send_ref[t, first : first + 12, :] = state_ref[12 * t : 12 * t + 12, :]
+
+
+def gather_rows(got_ref, state_ref):
+    for t in range(32):
+        state_ref[12 * t : 12 * t + 12, :] = got_ref[t, 0:12, :]
+
+
+STATE = pltpu.VMEM((384, 128), F32)
+
+
 def time_index():
     return lax.axis_index("z") * 4 + lax.axis_index("x")
 
 
 def keys_kernel(
-    x_hbm, dy_hbm, w_hbm, k_ref, v_ref, send_ref, xdy_ref, x_ref, dy_ref, w_ref, sum_ref, frame_sem, weight_sem
+    x_hbm, dy_hbm, w_hbm, k_ref, v_ref, send_ref, xdy_ref, x_ref, dy_ref, w_ref, sum_ref, state_ref, frame_sem, weight_sem
 ):
     x_copy = pltpu.make_async_copy(x_hbm, x_ref, frame_sem.at[0])
     dy_copy = pltpu.make_async_copy(dy_hbm, dy_ref, frame_sem.at[1])
@@ -110,7 +123,6 @@
         copies.append(pltpu.make_async_copy(source, w_ref.at[rows], weight_sem.at[i]))
         copies[-1].start()
     dy_copy.start()
-    send_ref[24:32, 0:16, :] = jnp.zeros((8, 16, 128), F32)
     x_copy.wait()
     x = x_ref[...]
     xdy_ref[0] = x.astype(F32)
@@ -128,11 +140,12 @@
         v_ref[:, lanes] = v
         fk = features(k.astype(F32)).astype(BF16)
         state = diagonal_blocks(mm_at(fk, v))
-        send_ref[4 * p : 4 * p + 4, 0:16, :] = state.reshape(4, 16, 128)
+        state_ref[64 * p : 64 * p + 64, :] = state
         norms.append(jnp.sum(fk.astype(F32), axis=0, keepdims=True))
-    norm = jnp.concatenate(norms + [jnp.zeros((2, 128), F32)], axis=0)
-    for t in range(32):
-        send_ref[t, 16:24, :] = norm
+    scatter_rows(state_ref, send_ref, 0)
+    norm = jnp.concatenate(norms + [jnp.zeros((6, 128), F32)], axis=0)
+    for t in range(32):
+        send_ref[t, 12:24, :] = norm
     dy_copy.wait()
     xdy_ref[1] = dy_ref[...].astype(F32)
 
@@ -140,7 +153,7 @@
 def keys(x, dy, w_qkv):
     rows, width = x.shape
     scratch = [pltpu.VMEM((rows, width), BF16)] * 2 + [pltpu.VMEM((width, 2 * INNER), BF16)]
-    scratch += [pltpu.VMEM((rows, 2 * INNER), F32)]
+    scratch += [pltpu.VMEM((rows, 2 * INNER), F32), STATE]
     scratch += [pltpu.SemaphoreType.DMA((2,)), pltpu.SemaphoreType.DMA((4,))]
     outs = [bf16(rows, INNER)] * 2 + [f32(32, 24, 128), f32(2, rows, width)]
     return call(keys_kernel, (x, dy, w_qkv), outs, "keys", scratch, in_hbm(3), KEYS_VMEM)
@@ -191,14 +204,14 @@
     return call(queries_kernel, (x, dy, w_qkv, w_out, k), outs, "queries", scratch, specs, LARGE_VMEM)
 
 
-def denominators_kernel(got_ref, q_ref, g_ref, sums_ref, send_ref, inverse_ref, dnum_ref, norm_ref):
+def denominators_kernel(got_ref, q_ref, g_ref, sums_ref, send_ref, inverse_ref, dnum_ref, norm_ref, state_ref):
     me = time_index()
-    carry = jnp.zeros((16, 128), F32)
+    carry = jnp.zeros((12, 128), F32)
     norms = jnp.zeros((8, 128), F32)
     for t in range(32):
-        send_ref[t, 0:16, :] = carry
-        carry = carry + got_ref[t, 0:16, :]
-        norms = norms + jnp.where(t < me, got_ref[t, 16:24, :], 0.0)
+        send_ref[t, 0:12, :] = carry
+        carry = carry + got_ref[t, 0:12, :]
+        norms = norms + jnp.where(t < me, got_ref[t, 12:20, :], 0.0)
     norm_ref[...] = norms
     lane = lax.broadcasted_iota(jnp.int32, (BLOCK, 128), 1)
     packed = jnp.ones((BLOCK, 128), F32)
@@ -215,24 +228,25 @@
         dnum = (g_ref[:, lanes].astype(F32) / den).astype(BF16)
         dnum_ref[:, lanes] = dnum
         dstate = diagonal_blocks(mm_at(fq, dnum))
-        send_ref[4 * p : 4 * p + 4, 16:32, :] = dstate.reshape(4, 16, 128)
+        state_ref[64 * p : 64 * p + 64, :] = dstate
     inverse_ref[...] = 1.0 / packed
-    send_ref[24:32, 16:32, :] = jnp.zeros((8, 16, 128), F32)
+    scatter_rows(state_ref, send_ref, 12)
 
 
 def denominators(*args):
-    outs = [f32(32, 32, 128), f32(BLOCK, 128), bf16(BLOCK, INNER), f32(8, 128)]
-    return call(denominators_kernel, args, outs, "denominators")
+    outs = [f32(32, 24, 128), f32(BLOCK, 128), bf16(BLOCK, INNER), f32(8, 128)]
+    return call(denominators_kernel, args, outs, "denominators", [STATE])
 
 
 def forward_kernel(
     got_ref, q_ref, k_ref, v_ref, g_ref, inverse_ref, dnum_ref, norm_ref, w_ref,
-    send_ref, dq_ref, ds_ref, b0_ref, b1_ref, b2_ref, b3_ref, out_ref,
+    send_ref, dq_ref, ds_ref, b0_ref, b1_ref, b2_ref, b3_ref, out_ref, state_ref,
 ):
-    carry = jnp.zeros((16, 128), F32)
+    gather_rows(got_ref, state_ref)
+    carry = jnp.zeros((12, 128), F32)
     for t in reversed(range(32)):
-        send_ref[t, 0:16, :] = carry
-        carry = carry + got_ref[t, 16:32, :]
+        send_ref[t, 0:12, :] = carry
+        carry = carry + got_ref[t, 12:24, :]
     mask = causal()
     low = low_lanes((BLOCK, 128))
     dnorms = []
@@ -247,7 +261,7 @@
         inverse = jnp.where(
             low, inverse_ref[:, 2 * p : 2 * p + 1], inverse_ref[:, 2 * p + 1 : 2 * p + 2]
         )
-        state = block_diagonal(got_ref[4 * p : 4 * p + 4, 0:16, :].reshape(64, 128).astype(BF16))
+        state = block_diagonal(state_ref[64 * p : 64 * p + 64, :].astype(BF16))
         v_halves = jnp.concatenate(split_pair(v), axis=0)
         ratio = (mm(w_ref[p], v_halves) + mm(fq, state)) * inverse
         out_ref[2 + block, :, part] = ratio.astype(BF16).astype(F32)
@@ -269,9 +283,9 @@
         dq = (dfq * slope(q)).astype(BF16)
         dq_ref[:, lanes] = dq
         out_ref[block, :, part] = dq.astype(F32)
-    dnorm = jnp.concatenate(dnorms + [jnp.zeros((2, 128), F32)], axis=0)
-    for t in range(32):
-        send_ref[t, 16:24, :] = dnorm
+    dnorm = jnp.concatenate(dnorms + [jnp.zeros((6, 128), F32)], axis=0)
+    for t in range(32):
+        send_ref[t, 12:24, :] = dnorm
     y = lax.axis_index("y")
     for i, ref in enumerate((b0_ref, b1_ref, b2_ref, b3_ref)):
         ref[...] = out_ref[lax.rem(y + i, 4)]
@@ -279,16 +293,17 @@
 
 def forward(*args):
     outs = [f32(32, 24, 128), bf16(BLOCK, INNER), bf16(PAIRS, 256, 128)] + [f32(BLOCK, 384)] * 4
-    return call(forward_kernel, args, outs, "forward", [pltpu.VMEM((4, BLOCK, 384), F32)])
+    return call(forward_kernel, args, outs, "forward", [pltpu.VMEM((4, BLOCK, 384), F32), STATE])
 
 
 def backward_kernel(
-    got_ref, q_ref, k_ref, v_ref, dnum_ref, w_ref, ds_ref, out_ref, dkv_ref
+    got_ref, q_ref, k_ref, v_ref, dnum_ref, w_ref, ds_ref, out_ref, dkv_ref, state_ref
 ):
     me = time_index()
     dnorms = jnp.zeros((8, 128), F32)
     for t in range(32):
-        dnorms = dnorms + jnp.where(t > me, got_ref[t, 16:24, :], 0.0)
+        dnorms = dnorms + jnp.where(t > me, got_ref[t, 12:20, :], 0.0)
+    gather_rows(got_ref, state_ref)
     for p in range(PAIRS):
         lanes = slice(128 * p, 128 * p + 128)
         block, part = p // 3, slice(128 * (p % 3), 128 * (p % 3) + 128)
@@ -297,7 +312,7 @@
         fk = features(k).astype(BF16)
         v = v_ref[:, lanes]
         dnum = dnum_ref[:, lanes]
-        dstate = block_diagonal(got_ref[4 * p : 4 * p + 4, 0:16, :].reshape(64, 128).astype(BF16))
+        dstate = block_diagonal(state_ref[64 * p : 64 * p + 64, :].astype(BF16))
         dfk = (
             mm_at(ds_ref[p], jnp.concatenate(split_pair(fq), axis=0))
             + mm_bt(v, dstate)
@@ -313,7 +328,7 @@
 
 
 def backward(*args):
-    return call(backward_kernel, args, [f32(4, BLOCK, 384), bf16(BLOCK, 2 * INNER)], "backward")
+    return call(backward_kernel, args, [f32(4, BLOCK, 384), bf16(BLOCK, 2 * INNER)], "backward", [STATE])
 
 
 def stage_kernel(xdy_ref, x_ref, chosen_ref):

time: 166 us -> 163 us (0.982)
  blocking collectives: 71.9 us -> 69.5 us
    all_to_all x4, blocking collectives: 71.9 us -> 69.5 us  [swap(): return lax.all_to_all(a, axes, 0, 0, tiled=True)]
where the time goes in v5:
time: 163 us
  blocking collectives  69.5 us (43%)
  starting transfers between devices  35.2 us (22%)
  Pallas kernels  23.2 us (14%)
  waiting for transfers between devices  20.6 us (13%)
  between operations  14.1 us (9%)
    all_to_all x4, blocking collectives, swap(): return lax.all_to_all(a, axes, 0, 0, tiled=True)  69.5 us
    all_to_all x3, starting transfers between devices, swap(): return lax.all_to_all(a, axes, 0, 0, tiled=True)  25 us
    pallas_call x12, Pallas kernels, call(): pl.pallas_call(kernel, in_specs=in_specs or in_vmem(len(args)), out_specs...  23.2 us
    all_to_all x3, waiting for transfers between devices, swap(): return lax.all_to_all(a, axes, 0, 0, tiled=True)  15.4 us
    ppermute x4, starting transfers between devices, shift(): return lax.ppermute(a, axis, [(i, (i + s) % n) for i in range(n)])  10.2 us
    ppermute x4, waiting for transfers between devices, shift(): return lax.ppermute(a, axis, [(i, (i + s) % n) for i in range(n)])  5.18 us
  transfers between devices with their start and end apart: 8, of which 5 were waited for; matrix products, arithmetic and copies ran while one was open for 0% of the time, Pallas kernels for 10%

profile of v5, /device:TPU:1, one launch (start us, length us, event | category | flops | bytes accessed | tf_op | source)
XLA Modules:
  0.0 162.6 jit_solution(17765352938680007931)
XLA Ops:
  7.2 0.0 all-gather.3.cloned.1.call-start
  7.2 3.7 %keys.1 = (bf16[128,768]{1,0:T(8,128)(2,1)S(1)}, bf16[128,768]{1,0:T(8,128)(2,1)S(1)}, f32[32,24,128]{2,1,0:T(8,128)}, f32[2,128,1024]{2,1,0:T(8,128)}) custom-call(bf16[128,1024]{1,0:T(8,128)(2,1)} %bitcast.4, bf16[128,1024]{1,0:T(8,128)(2,1)} %bitcast.7, bf16[1024,2304]{1,0:T(8,128)(2,1)} %w_ref.1), custom_call_target="tpu_custom_call" | custom-call | tf_op jit(solution)/shard_map/keys/pallas_call | solution.py:85
  10.9 0.0 copy-start.3
  10.9 0.0 all-gather.3.cloned.1.call-update
  10.9 12.0 %all-to-all-start = ((f32[32,24,128]{2,1,0:T(8,128)}), f32[32,24,128]{2,1,0:T(8,128)S(1)}, u32[]{:S(2)}, u32[]{:S(2)}) async-start(f32[32,24,128]{2,1,0:T(8,128)} %get-tuple-element.42), calls=%async_computation | async-start | bytes 786432 | tf_op jit(solution)/shard_map/all_to_all | solution.py:396
  22.9 3.1 %queries.1 = (bf16[128,768]{1,0:T(8,128)(2,1)S(1)}, bf16[128,768]{1,0:T(8,128)(2,1)S(1)}, bf16[6,128,256]{2,1,0:T(8,128)(2,1)}, f32[128,128]{1,0:T(8,128)S(1)}) custom-call(bf16[128,1024]{1,0:T(8,128)(2,1)S(1)} %bitcast.5, bf16[128,1024]{1,0:T(8,128)(2,1)} %bitcast.8, bf16[1024,2304]{1,0:T(8,128)(2,1)} %w_ref.1, bf16[1024,768]{1,0:T(8,128)(2,1)} %wo_hbm.1, ...), custom_call_target="tpu_custom_call" | custom-call | tf_op jit(solution)/shard_map/queries/pallas_call | solution.py:85
  26.0 10.7 %all-to-all-done.got_ref = f32[32,24,128]{2,1,0:T(8,128)S(1)} async-done(((f32[32,24,128]{2,1,0:T(8,128)}), f32[32,24,128]{2,1,0:T(8,128)S(1)}, u32[]{:S(2)}, u32[]{:S(2)}) %all-to-all-start) | async-done | bytes 393248 | tf_op jit(solution)/shard_map/all_to_all | solution.py:396
  36.7 1.1 denominators.1
  37.8 17.7 %all_to_all.35.got_ref = f32[32,24,128]{2,1,0:T(8,128)S(1)} all-to-all(f32[32,24,128]{2,1,0:T(8,128)S(1)} %get-tuple-element.52), channel_id=1, replica_groups=mesh['z'=8,'x'=4,'y'=4,'c'=2] {'z','x'}, dimensions={0} | all-to-all | bytes 786432 | tf_op jit(solution)/shard_map/all_to_all | solution.py:396
  55.5 3.0 %forward.1 = (f32[32,24,128]{2,1,0:T(8,128)}, bf16[128,768]{1,0:T(8,128)(2,1)S(1)}, bf16[6,256,128]{2,1,0:T(8,128)(2,1)S(1)}, f32[128,384]{1,0:T(8,128)S(1)}, f3...) custom-call(f32[32,24,128]{2,1,0:T(8,128)S(1)} %all_to_all.35.got_ref, ...), custom_call_target="tpu_custom_call" | custom-call | tf_op jit(solution)/shard_map/forward/pallas_call | solution.py:85
  58.5 5.6 %all-to-all-start.2 = ((f32[32,24,128]{2,1,0:T(8,128)}), f32[32,24,128]{2,1,0:T(8,128)S(1)}, u32[]{:S(2)}, u32[]{:S(2)}) async-start(f32[32,24,128]{2,1,0:T(8,128)} %get-tuple-element.59), calls=%async_computation.2 | async-start | bytes 786432 | tf_op jit(solution)/shard_map/all_to_all | solution.py:396
  64.1 1.4 collective-permute-start
  65.5 2.6 %collective-permute-start.1 = (f32[128,384]{1,0:T(8,128)S(1)}, f32[128,384]{1,0:T(8,128)S(1)}, u32[]{:S(2)}, u32[]{:S(2)}) collective-permute-start(f32[128,384]{1,0:T(8,128)S(1)} %get-tuple-element.62), channel_id=1, source_target_pairs={{0,4},{2,6},{4,0},{6,2},{1,5},{3,7},{5,1},{7,3},{8,12},{10,14},{12... | collective-permute-start | bytes 589832 | tf_op jit(solution)/shard_map/ppermute | solution.py:401
  68.1 1.1 collective-permute-start.2
  69.2 4.1 %stage.1 = (bf16[1024,512]{1,0:T(8,128)(2,1)}, bf16[1024,512]{1,0:T(8,128)(2,1)}) custom-call(f32[4,2,128,1024]{3,2,1,0:T(8,128)} %bitcast.6), custom_call_target="tpu_custom_call" | custom-call | tf_op jit(solution)/shard_map/stage/pallas_call | solution.py:85
  73.3 0.0 collective-permute-done.b1_ref
  73.3 2.1 %collective-permute-done.1.b2_ref = f32[128,384]{1,0:T(8,128)S(1)} collective-permute-done((f32[128,384]{1,0:T(8,128)S(1)}, f32[128,384]{1,0:T(8,128)S(1)}, u32[]{:S(2)}, u32[]{:S(2)}) %collective-permute-start.1) | collective-permute-done | bytes 196640 | tf_op jit(solution)/shard_map/ppermute | solution.py:401
  75.5 1.3 all-to-all-done.2.got_ref
  76.7 0.6 backward.1
  77.3 12.5 %all_to_all.36.got_ref = f32[4,128,384]{2,1,0:T(8,128)S(1)} all-to-all(f32[4,128,384]{2,1,0:T(8,128)S(1)} %get-tuple-element.76), channel_id=1, replica_groups=mesh['z'=8,'x'=4,'y'=4,'c'=2] {'y'}, dimensions={0} | all-to-all | bytes 1572864 | tf_op jit(solution)/shard_map/all_to_all | solution.py:396
  89.8 1.2 weights.1
  91.0 5.1 %collective-permute-start.3 = (f32[4,8,16,768]{3,2,1,0:T(8,128)S(1)}, f32[4,8,16,768]{3,2,1,0:T(8,128)S(1)}, u32[]{:S(2)}, u32[]{:S(2)}) collective-permute-start(f32[4,8,16,768]{3,2,1,0:T(8,128)S(1)} %get-tuple-element.78), channel_id=1, source_target_pairs={{0,1},{1,0},{2,3},{3,2},{4,5},{5,4},{6,7},{7,6},{8,9},{9,8},{10,11... | collective-permute-start | bytes 4718600 | tf_op jit(solution)/shard_map/ppermute | solution.py:401
  96.2 3.0 %collective-permute-done.3.got_ref = f32[4,8,16,768]{3,2,1,0:T(8,128)S(1)} collective-permute-done((f32[4,8,16,768]{3,2,1,0:T(8,128)S(1)}, f32[4,8,16,768]{3,2,1,0:T(8,128)S(1)}, u32[]{:S(2)}, u32[]{:S(2)}) %collective-permute-start.3) | collective-permute-done | bytes 1572896 | tf_op jit(solution)/shard_map/ppermute | solution.py:401
  99.2 0.2 core_sum.1
  99.4 22.9 %all_to_all.37.got_ref = f32[4,8,16,768]{3,2,1,0:T(8,128)S(1)} all-to-all(f32[4,8,16,768]{3,2,1,0:T(8,128)S(1)} %core_sum.1), channel_id=1, replica_groups=mesh['z'=8,'x'=4,'y'=4,'c'=2] {'x'}, dimensions={0} | all-to-all | bytes 3145728 | tf_op jit(solution)/shard_map/all_to_all | solution.py:396
  122.3 0.1 row_sum.1
  122.4 16.4 %all_to_all.38.got_ref = f32[8,16,768]{2,1,0:T(8,128)S(1)} all-to-all(f32[8,16,768]{2,1,0:T(8,128)S(1)} %row_sum.1), channel_id=1, replica_groups=mesh['z'=8,'x'=4,'y'=4,'c'=2] {'z'}, dimensions={0} | all-to-all | bytes 786432 | tf_op jit(solution)/shard_map/all_to_all | solution.py:396
  138.8 0.8 spread.1
  139.6 7.4 %all-to-all-start.6 = ((f32[8,16,768]{2,1,0:T(8,128)}), f32[8,16,768]{2,1,0:T(8,128)S(1)}, u32[]{:S(2)}, u32[]{:S(2)}) async-start(f32[8,16,768]{2,1,0:T(8,128)} %spread.1), calls=%async_computation.6 | async-start | bytes 786432 | tf_op jit(solution)/shard_map/all_to_all | solution.py:396
  146.9 4.7 %frame_gradient.1 = bf16[128,1024]{1,0:T(8,128)(2,1)} custom-call(bf16[128,768]{1,0:T(8,128)(2,1)S(1)} %get-tuple-element.58.dq_ref, bf16[128,1536]{1,0:T(8,128)(2,1)S(1)} %get-tuple-element.69.dkv_ref, bf16[1024,2304]{1,0:T(8,128)(2,1)} %w_ref.1), custom_call_target="tpu_custom_call" | custom-call | tf_op jit(solution)/shard_map/frame_gradient/pallas_call | solution.py:85
  151.6 3.4 %all-to-all-done.6.got_ref = f32[8,16,768]{2,1,0:T(8,128)S(1)} async-done(((f32[8,16,768]{2,1,0:T(8,128)}), f32[8,16,768]{2,1,0:T(8,128)S(1)}, u32[]{:S(2)}, u32[]{:S(2)}) %all-to-all-start.6) | async-done | bytes 393248 | tf_op jit(solution)/shard_map/all_to_all | solution.py:396
  155.0 0.8 assemble.1
  (9 shorter events, 0.0 us)
Async XLA Ops:
  7.2 62.0 %all-gather.3.cloned.1.call-start = ((), (), s32[]{:S(2)}) async-start(), calls=%async_computation.7 | async-start | bytes 5242880 | tf_op jit(solution)/shard_map/all_gather | solution.py:410
  10.9 12.1 %copy-start.3 = (bf16[1,128,1024]{2,1,0:T(8,128)(2,1)S(1)}, bf16[1,128,1024]{2,1,0:T(8,128)(2,1)}, u32[]{:S(2)}) copy-start(bf16[1,128,1024]{2,1,0:T(8,128)(2,1)} %param.4) | copy-start | bytes 786436
  10.9 25.8 %all-to-all-start = ((f32[32,24,128]{2,1,0:T(8,128)}), f32[32,24,128]{2,1,0:T(8,128)S(1)}, u32[]{:S(2)}, u32[]{:S(2)}) async-start(f32[32,24,128]{2,1,0:T(8,128)} %get-tuple-element.42), calls=%async_computation | async-start | bytes 786432 | tf_op jit(solution)/shard_map/all_to_all | solution.py:396
  26.0 29.5 %copy-start = (bf16[6,128,256]{2,1,0:T(8,128)(2,1)S(1)}, bf16[6,128,256]{2,1,0:T(8,128)(2,1)}, u32[]{:S(2)}) copy-start(bf16[6,128,256]{2,1,0:T(8,128)(2,1)} %get-tuple-element.57.w_ref) | copy-start | bytes 1179652
  58.5 18.2 %all-to-all-start.2 = ((f32[32,24,128]{2,1,0:T(8,128)}), f32[32,24,128]{2,1,0:T(8,128)S(1)}, u32[]{:S(2)}, u32[]{:S(2)}) async-start(f32[32,24,128]{2,1,0:T(8,128)} %get-tuple-element.59), calls=%async_computation.2 | async-start | bytes 786432 | tf_op jit(solution)/shard_map/all_to_all | solution.py:396
  64.1 9.2 %collective-permute-start = (f32[128,384]{1,0:T(8,128)}, f32[128,384]{1,0:T(8,128)S(1)}, u32[]{:S(2)}, u32[]{:S(2)}) collective-permute-start(f32[128,384]{1,0:T(8,128)} %get-tuple-element.61), channel_id=1, source_target_pairs={{0,2},{2,4},{4,6},{6,0},{1,3},{3,5},{5,7},{7,1},{8,10},{10,12},{12... | collective-permute-start | bytes 589832 | tf_op jit(solution)/shard_map/ppermute | solution.py:401
  65.5 10.0 %collective-permute-start.1 = (f32[128,384]{1,0:T(8,128)S(1)}, f32[128,384]{1,0:T(8,128)S(1)}, u32[]{:S(2)}, u32[]{:S(2)}) collective-permute-start(f32[128,384]{1,0:T(8,128)S(1)} %get-tuple-element.62), channel_id=1, source_target_pairs={{0,4},{2,6},{4,0},{6,2},{1,5},{3,7},{5,1},{7,3},{8,12},{10,14},{12... | collective-permute-start | bytes 589832 | tf_op jit(solution)/shard_map/ppermute | solution.py:401
  68.1 7.3 %collective-permute-start.2 = (f32[128,384]{1,0:T(8,128)S(1)}, f32[128,384]{1,0:T(8,128)S(1)}, u32[]{:S(2)}, u32[]{:S(2)}) collective-permute-start(f32[128,384]{1,0:T(8,128)S(1)} %get-tuple-element.63), channel_id=1, source_target_pairs={{0,6},{2,0},{4,2},{6,4},{1,7},{3,1},{5,3},{7,5},{8,14},{10,8},{12,... | collective-permute-start | bytes 589832 | tf_op jit(solution)/shard_map/ppermute | solution.py:401
  76.7 13.1 %copy-start.1 = (bf16[1024,512]{1,0:T(8,128)(2,1)S(1)}, bf16[1024,512]{1,0:T(8,128)(2,1)}, u32[]{:S(2)}) copy-start(bf16[1024,512]{1,0:T(8,128)(2,1)} %get-tuple-element.70.x_ref) | copy-start | bytes 3145732
  76.7 13.1 %copy-start.2 = (bf16[1024,512]{1,0:T(8,128)(2,1)S(1)}, bf16[1024,512]{1,0:T(8,128)(2,1)}, u32[]{:S(2)}) copy-start(bf16[1024,512]{1,0:T(8,128)(2,1)} %get-tuple-element.71.chosen_ref) | copy-start | bytes 3145732
  91.0 8.2 %collective-permute-start.3 = (f32[4,8,16,768]{3,2,1,0:T(8,128)S(1)}, f32[4,8,16,768]{3,2,1,0:T(8,128)S(1)}, u32[]{:S(2)}, u32[]{:S(2)}) collective-permute-start(f32[4,8,16,768]{3,2,1,0:T(8,128)S(1)} %get-tuple-element.78), channel_id=1, source_target_pairs={{0,1},{1,0},{2,3},{3,2},{4,5},{5,4},{6,7},{7,6},{8,9},{9,8},{10,11... | collective-permute-start | bytes 4718600 | tf_op jit(solution)/shard_map/ppermute | solution.py:401
  139.6 15.4 %all-to-all-start.6 = ((f32[8,16,768]{2,1,0:T(8,128)}), f32[8,16,768]{2,1,0:T(8,128)S(1)}, u32[]{:S(2)}, u32[]{:S(2)}) async-start(f32[8,16,768]{2,1,0:T(8,128)} %spread.1), calls=%async_computation.6 | async-start | bytes 786432 | tf_op jit(solution)/shard_map/all_to_all | solution.py:396
Sparse Core Ops, SparseCore 0:
  11.0 54.7 all-gather.2

commit v6 on v5

--- a/solution.py
+++ b/solution.py
@@ -103,6 +103,19 @@
         state_ref[12 * t : 12 * t + 12, :] = got_ref[t, 0:12, :]
 
 
+def narrow(rows_ref, send_ref):
+    for t in range(32):
+        for i in range(9):
+            send_ref[t, i] = rows_ref[t, 2 * i : 2 * i + 2, :]
+
+
+def widen(got_ref, rows_ref):
+    for t in range(32):
+        for i in range(9):
+            rows_ref[t, 2 * i : 2 * i + 2, :] = got_ref[t, i]
+
+
+ROWS = pltpu.VMEM((32, 24, 128), F32)
 STATE = pltpu.VMEM((384, 128), F32)
 
 
@@ -111,7 +124,7 @@
 
 
 def keys_kernel(
-    x_hbm, dy_hbm, w_hbm, k_ref, v_ref, send_ref, xdy_ref, x_ref, dy_ref, w_ref, sum_ref, state_ref, frame_sem, weight_sem
+    x_hbm, dy_hbm, w_hbm, k_ref, v_ref, out_ref, xdy_ref, x_ref, dy_ref, w_ref, sum_ref, state_ref, send_ref, frame_sem, weight_sem
 ):
     x_copy = pltpu.make_async_copy(x_hbm, x_ref, frame_sem.at[0])
     dy_copy = pltpu.make_async_copy(dy_hbm, dy_ref, frame_sem.at[1])
@@ -146,6 +159,7 @@
     norm = jnp.concatenate(norms + [jnp.zeros((6, 128), F32)], axis=0)
     for t in range(32):
         send_ref[t, 12:24, :] = norm
+    narrow(send_ref, out_ref)
     dy_copy.wait()
     xdy_ref[1] = dy_ref[...].astype(F32)
 
@@ -153,9 +167,9 @@
 def keys(x, dy, w_qkv):
     rows, width = x.shape
     scratch = [pltpu.VMEM((rows, width), BF16)] * 2 + [pltpu.VMEM((width, 2 * INNER), BF16)]
-    scratch += [pltpu.VMEM((rows, 2 * INNER), F32), STATE]
+    scratch += [pltpu.VMEM((rows, 2 * INNER), F32), STATE, ROWS]
     scratch += [pltpu.SemaphoreType.DMA((2,)), pltpu.SemaphoreType.DMA((4,))]
-    outs = [bf16(rows, INNER)] * 2 + [f32(32, 24, 128), f32(2, rows, width)]
+    outs = [bf16(rows, INNER)] * 2 + [f32(32, 9, 2, 128), f32(2, rows, width)]
     return call(keys_kernel, (x, dy, w_qkv), outs, "keys", scratch, in_hbm(3), KEYS_VMEM)
 
 
@@ -204,15 +218,16 @@
     return call(queries_kernel, (x, dy, w_qkv, w_out, k), outs, "queries", scratch, specs, LARGE_VMEM)
 
 
-def denominators_kernel(got_ref, q_ref, g_ref, sums_ref, send_ref, inverse_ref, dnum_ref, norm_ref, state_ref):
+def denominators_kernel(in_ref, q_ref, g_ref, sums_ref, send_ref, inverse_ref, dnum_ref, norm_ref, state_ref, got_ref):
+    widen(in_ref, got_ref)
     me = time_index()
     carry = jnp.zeros((12, 128), F32)
-    norms = jnp.zeros((8, 128), F32)
+    norms = jnp.zeros((6, 128), F32)
     for t in range(32):
         send_ref[t, 0:12, :] = carry
         carry = carry + got_ref[t, 0:12, :]
-        norms = norms + jnp.where(t < me, got_ref[t, 12:20, :], 0.0)
-    norm_ref[...] = norms
+        norms = norms + jnp.where(t < me, got_ref[t, 12:18, :], 0.0)
+    norm_ref[...] = jnp.concatenate([norms, jnp.zeros((2, 128), F32)], axis=0)
     lane = lax.broadcasted_iota(jnp.int32, (BLOCK, 128), 1)
     packed = jnp.ones((BLOCK, 128), F32)
     for p in range(PAIRS):
@@ -235,12 +250,12 @@
 
 def denominators(*args):
     outs = [f32(32, 24, 128), f32(BLOCK, 128), bf16(BLOCK, INNER), f32(8, 128)]
-    return call(denominators_kernel, args, outs, "denominators", [STATE])
+    return call(denominators_kernel, args, outs, "denominators", [STATE, ROWS])
 
 
 def forward_kernel(
     got_ref, q_ref, k_ref, v_ref, g_ref, inverse_ref, dnum_ref, norm_ref, w_ref,
-    send_ref, dq_ref, ds_ref, b0_ref, b1_ref, b2_ref, b3_ref, out_ref, state_ref,
+    narrow_ref, dq_ref, ds_ref, b0_ref, b1_ref, b2_ref, b3_ref, out_ref, state_ref, send_ref,
 ):
     gather_rows(got_ref, state_ref)
     carry = jnp.zeros((12, 128), F32)
@@ -286,23 +301,25 @@
     dnorm = jnp.concatenate(dnorms + [jnp.zeros((6, 128), F32)], axis=0)
     for t in range(32):
         send_ref[t, 12:24, :] = dnorm
+    narrow(send_ref, narrow_ref)
     y = lax.axis_index("y")
     for i, ref in enumerate((b0_ref, b1_ref, b2_ref, b3_ref)):
         ref[...] = out_ref[lax.rem(y + i, 4)]
 
 
 def forward(*args):
-    outs = [f32(32, 24, 128), bf16(BLOCK, INNER), bf16(PAIRS, 256, 128)] + [f32(BLOCK, 384)] * 4
-    return call(forward_kernel, args, outs, "forward", [pltpu.VMEM((4, BLOCK, 384), F32), STATE])
+    outs = [f32(32, 9, 2, 128), bf16(BLOCK, INNER), bf16(PAIRS, 256, 128)] + [f32(BLOCK, 384)] * 4
+    return call(forward_kernel, args, outs, "forward", [pltpu.VMEM((4, BLOCK, 384), F32), STATE, ROWS])
 
 
 def backward_kernel(
-    got_ref, q_ref, k_ref, v_ref, dnum_ref, w_ref, ds_ref, out_ref, dkv_ref, state_ref
+    in_ref, q_ref, k_ref, v_ref, dnum_ref, w_ref, ds_ref, out_ref, dkv_ref, state_ref, got_ref
 ):
+    widen(in_ref, got_ref)
     me = time_index()
-    dnorms = jnp.zeros((8, 128), F32)
-    for t in range(32):
-        dnorms = dnorms + jnp.where(t > me, got_ref[t, 12:20, :], 0.0)
+    dnorms = jnp.zeros((6, 128), F32)
+    for t in range(32):
+        dnorms = dnorms + jnp.where(t > me, got_ref[t, 12:18, :], 0.0)
     gather_rows(got_ref, state_ref)
     for p in range(PAIRS):
         lanes = slice(128 * p, 128 * p + 128)
@@ -328,7 +345,7 @@
 
 
 def backward(*args):
-    return call(backward_kernel, args, [f32(4, BLOCK, 384), bf16(BLOCK, 2 * INNER)], "backward", [STATE])
+    return call(backward_kernel, args, [f32(4, BLOCK, 384), bf16(BLOCK, 2 * INNER)], "backward", [STATE, ROWS])
 
 
 def stage_kernel(xdy_ref, x_ref, chosen_ref):

time: 163 us -> 161 us (0.988)
  waiting for transfers between devices: 20.6 us -> 17.3 us
    all_to_all x3, waiting for transfers between devices: 15.4 us -> 12.3 us  [swap(): return lax.all_to_all(a, axes, 0, 0, tiled=True)]
  transfers between devices with their start and end apart: 8 -> 8, of which waited for: 5 -> 4; matrix products, arithmetic and copies ran while one was open for 0% -> 0% of each run, Pallas kernels for 10% -> 10%
where the time goes in v6:
time: 161 us; the launch traced here: 160 us
  blocking collectives  70.1 us (44%)
  starting transfers between devices  35.5 us (22%)
  Pallas kernels  23.2 us (14%)
  waiting for transfers between devices  17.3 us (11%)
  between operations  14.1 us (9%)
    all_to_all x4, blocking collectives, swap(): return lax.all_to_all(a, axes, 0, 0, tiled=True)  70.1 us
    all_to_all x3, starting transfers between devices, swap(): return lax.all_to_all(a, axes, 0, 0, tiled=True)  25 us
    pallas_call x12, Pallas kernels, call(): pl.pallas_call(kernel, in_specs=in_specs or in_vmem(len(args)), out_specs...  23.2 us
    all_to_all x3, waiting for transfers between devices, swap(): return lax.all_to_all(a, axes, 0, 0, tiled=True)  12.3 us
    ppermute x4, starting transfers between devices, shift(): return lax.ppermute(a, axis, [(i, (i + s) % n) for i in range(n)])  10.5 us
    ppermute x4, waiting for transfers between devices, shift(): return lax.ppermute(a, axis, [(i, (i + s) % n) for i in range(n)])  4.93 us
  transfers between devices with their start and end apart: 8, of which 4 were waited for; matrix products, arithmetic and copies ran while one was open for 0% of the time, Pallas kernels for 10%

profile of v6, /device:TPU:1, one launch (start us, length us, event | category | flops | bytes accessed | tf_op | source)
XLA Modules:
  0.0 160.3 jit_solution(534236917429090985)
XLA Ops:
  7.2 0.0 all-gather.3.cloned.1.call-start
  7.2 3.6 %keys.1 = (bf16[128,768]{1,0:T(8,128)(2,1)S(1)}, bf16[128,768]{1,0:T(8,128)(2,1)S(1)}, f32[32,9,2,128]{3,2,1,0:T(2,128)}, f32[2,128,1024]{2,1,0:T(8,128)}) custom-call(bf16[128,1024]{1,0:T(8,128)(2,1)} %bitcast.4, bf16[128,1024]{1,0:T(8,128)(2,1)} %bitcast.7, bf16[1024,2304]{1,0:T(8,128)(2,1)} %w_ref.1), custom_call_target="tpu_custom_call" | custom-call | tf_op jit(solution)/shard_map/keys/pallas_call | solution.py:85
  10.9 0.0 copy-start.3
  10.9 0.0 all-gather.3.cloned.1.call-update
  10.9 12.0 %all-to-all-start = ((f32[32,9,2,128]{3,2,1,0:T(2,128)}), f32[32,9,2,128]{3,2,1,0:T(2,128)S(1)}, u32[]{:S(2)}, u32[]{:S(2)}) async-start(f32[32,9,2,128]{3,2,1,0:T(2,128)} %get-tuple-element.42), calls=%async_computation | async-start | bytes 589824 | tf_op jit(solution)/shard_map/all_to_all | solution.py:413
  22.9 3.1 %queries.1 = (bf16[128,768]{1,0:T(8,128)(2,1)S(1)}, bf16[128,768]{1,0:T(8,128)(2,1)S(1)}, bf16[6,128,256]{2,1,0:T(8,128)(2,1)}, f32[128,128]{1,0:T(8,128)S(1)}) custom-call(bf16[128,1024]{1,0:T(8,128)(2,1)S(1)} %bitcast.5, bf16[128,1024]{1,0:T(8,128)(2,1)} %bitcast.8, bf16[1024,2304]{1,0:T(8,128)(2,1)} %w_ref.1, bf16[1024,768]{1,0:T(8,128)(2,1)} %wo_hbm.1, ...), custom_call_target="tpu_custom_call" | custom-call | tf_op jit(solution)/shard_map/queries/pallas_call | solution.py:85
  26.1 8.9 %all-to-all-done.in_ref = f32[32,9,2,128]{3,2,1,0:T(2,128)S(1)} async-done(((f32[32,9,2,128]{3,2,1,0:T(2,128)}), f32[32,9,2,128]{3,2,1,0:T(2,128)S(1)}, u32[]{:S(2)}, u32[]{:S(2)}) %all-to-all-start) | async-done | bytes 294944 | tf_op jit(solution)/shard_map/all_to_all | solution.py:413
  35.0 1.1 denominators.1
  36.1 17.3 %all_to_all.35.got_ref = f32[32,24,128]{2,1,0:T(8,128)S(1)} all-to-all(f32[32,24,128]{2,1,0:T(8,128)S(1)} %get-tuple-element.52), channel_id=1, replica_groups=mesh['z'=8,'x'=4,'y'=4,'c'=2] {'z','x'}, dimensions={0} | all-to-all | bytes 786432 | tf_op jit(solution)/shard_map/all_to_all | solution.py:413
  53.4 2.9 %forward.1 = (f32[32,9,2,128]{3,2,1,0:T(2,128)}, bf16[128,768]{1,0:T(8,128)(2,1)S(1)}, bf16[6,256,128]{2,1,0:T(8,128)(2,1)S(1)}, f32[128,384]{1,0:T(8,128)S(1)},...) custom-call(f32[32,24,128]{2,1,0:T(8,128)S(1)} %all_to_all.35.got_ref, ...), custom_call_target="tpu_custom_call" | custom-call | tf_op jit(solution)/shard_map/forward/pallas_call | solution.py:85
  56.3 5.6 %all-to-all-start.2 = ((f32[32,9,2,128]{3,2,1,0:T(2,128)}), f32[32,9,2,128]{3,2,1,0:T(2,128)S(1)}, u32[]{:S(2)}, u32[]{:S(2)}) async-start(f32[32,9,2,128]{3,2,1,0:T(2,128)} %get-tuple-element.59), calls=%async_computation.2 | async-start | bytes 589824 | tf_op jit(solution)/shard_map/all_to_all | solution.py:413
  61.9 1.4 collective-permute-start
  63.3 2.6 %collective-permute-start.1 = (f32[128,384]{1,0:T(8,128)S(1)}, f32[128,384]{1,0:T(8,128)S(1)}, u32[]{:S(2)}, u32[]{:S(2)}) collective-permute-start(f32[128,384]{1,0:T(8,128)S(1)} %get-tuple-element.62), channel_id=1, source_target_pairs={{0,4},{2,6},{4,0},{6,2},{1,5},{3,7},{5,1},{7,3},{8,12},{10,14},{12... | collective-permute-start | bytes 589832 | tf_op jit(solution)/shard_map/ppermute | solution.py:418
  65.9 1.1 collective-permute-start.2
  66.9 4.1 %stage.1 = (bf16[1024,512]{1,0:T(8,128)(2,1)}, bf16[1024,512]{1,0:T(8,128)(2,1)}) custom-call(f32[4,2,128,1024]{3,2,1,0:T(8,128)} %bitcast.6), custom_call_target="tpu_custom_call" | custom-call | tf_op jit(solution)/shard_map/stage/pallas_call | solution.py:85
  71.1 0.0 collective-permute-done.b1_ref
  71.1 1.9 %collective-permute-done.1.b2_ref = f32[128,384]{1,0:T(8,128)S(1)} collective-permute-done((f32[128,384]{1,0:T(8,128)S(1)}, f32[128,384]{1,0:T(8,128)S(1)}, u32[]{:S(2)}, u32[]{:S(2)}) %collective-permute-start.1) | collective-permute-done | bytes 196640 | tf_op jit(solution)/shard_map/ppermute | solution.py:418
  73.0 0.0 collective-permute-done.2.b3_ref
  73.0 0.7 backward.1
  73.6 12.1 %all_to_all.36.got_ref = f32[4,128,384]{2,1,0:T(8,128)S(1)} all-to-all(f32[4,128,384]{2,1,0:T(8,128)S(1)} %get-tuple-element.76), channel_id=1, replica_groups=mesh['z'=8,'x'=4,'y'=4,'c'=2] {'y'}, dimensions={0} | all-to-all | bytes 1572864 | tf_op jit(solution)/shard_map/all_to_all | solution.py:413
  85.7 1.2 weights.1
  87.0 5.5 %collective-permute-start.3 = (f32[4,8,16,768]{3,2,1,0:T(8,128)S(1)}, f32[4,8,16,768]{3,2,1,0:T(8,128)S(1)}, u32[]{:S(2)}, u32[]{:S(2)}) collective-permute-start(f32[4,8,16,768]{3,2,1,0:T(8,128)S(1)} %get-tuple-element.78), channel_id=1, source_target_pairs={{0,1},{1,0},{2,3},{3,2},{4,5},{5,4},{6,7},{7,6},{8,9},{9,8},{10,11... | collective-permute-start | bytes 4718600 | tf_op jit(solution)/shard_map/ppermute | solution.py:418
  92.4 3.0 %collective-permute-done.3.got_ref = f32[4,8,16,768]{3,2,1,0:T(8,128)S(1)} collective-permute-done((f32[4,8,16,768]{3,2,1,0:T(8,128)S(1)}, f32[4,8,16,768]{3,2,1,0:T(8,128)S(1)}, u32[]{:S(2)}, u32[]{:S(2)}) %collective-permute-start.3) | collective-permute-done | bytes 1572896 | tf_op jit(solution)/shard_map/ppermute | solution.py:418
  95.5 0.2 core_sum.1
  95.6 22.9 %all_to_all.37.got_ref = f32[4,8,16,768]{3,2,1,0:T(8,128)S(1)} all-to-all(f32[4,8,16,768]{3,2,1,0:T(8,128)S(1)} %core_sum.1), channel_id=1, replica_groups=mesh['z'=8,'x'=4,'y'=4,'c'=2] {'x'}, dimensions={0} | all-to-all | bytes 3145728 | tf_op jit(solution)/shard_map/all_to_all | solution.py:413
  118.5 0.1 row_sum.1
  118.6 17.8 %all_to_all.38.got_ref = f32[8,16,768]{2,1,0:T(8,128)S(1)} all-to-all(f32[8,16,768]{2,1,0:T(8,128)S(1)} %row_sum.1), channel_id=1, replica_groups=mesh['z'=8,'x'=4,'y'=4,'c'=2] {'z'}, dimensions={0} | all-to-all | bytes 786432 | tf_op jit(solution)/shard_map/all_to_all | solution.py:413
  136.4 0.8 spread.1
  137.2 7.4 %all-to-all-start.6 = ((f32[8,16,768]{2,1,0:T(8,128)}), f32[8,16,768]{2,1,0:T(8,128)S(1)}, u32[]{:S(2)}, u32[]{:S(2)}) async-start(f32[8,16,768]{2,1,0:T(8,128)} %spread.1), calls=%async_computation.6 | async-start | bytes 786432 | tf_op jit(solution)/shard_map/all_to_all | solution.py:413
  144.6 4.7 %frame_gradient.1 = bf16[128,1024]{1,0:T(8,128)(2,1)} custom-call(bf16[128,768]{1,0:T(8,128)(2,1)S(1)} %get-tuple-element.58.dq_ref, bf16[128,1536]{1,0:T(8,128)(2,1)S(1)} %get-tuple-element.69.dkv_ref, bf16[1024,2304]{1,0:T(8,128)(2,1)} %w_ref.1), custom_call_target="tpu_custom_call" | custom-call | tf_op jit(solution)/shard_map/frame_gradient/pallas_call | solution.py:85
  149.2 3.4 %all-to-all-done.6.got_ref = f32[8,16,768]{2,1,0:T(8,128)S(1)} async-done(((f32[8,16,768]{2,1,0:T(8,128)}), f32[8,16,768]{2,1,0:T(8,128)S(1)}, u32[]{:S(2)}, u32[]{:S(2)}) %all-to-all-start.6) | async-done | bytes 393248 | tf_op jit(solution)/shard_map/all_to_all | solution.py:413
  152.6 0.8 assemble.1
  (9 shorter events, 0.0 us)
Async XLA Ops:
  7.2 59.8 %all-gather.3.cloned.1.call-start = ((), (), s32[]{:S(2)}) async-start(), calls=%async_computation.7 | async-start | bytes 5242880 | tf_op jit(solution)/shard_map/all_gather | solution.py:427
  10.9 12.1 %copy-start.3 = (bf16[1,128,1024]{2,1,0:T(8,128)(2,1)S(1)}, bf16[1,128,1024]{2,1,0:T(8,128)(2,1)}, u32[]{:S(2)}) copy-start(bf16[1,128,1024]{2,1,0:T(8,128)(2,1)} %param.4) | copy-start | bytes 786436
  10.9 24.1 %all-to-all-start = ((f32[32,9,2,128]{3,2,1,0:T(2,128)}), f32[32,9,2,128]{3,2,1,0:T(2,128)S(1)}, u32[]{:S(2)}, u32[]{:S(2)}) async-start(f32[32,9,2,128]{3,2,1,0:T(2,128)} %get-tuple-element.42), calls=%async_computation | async-start | bytes 589824 | tf_op jit(solution)/shard_map/all_to_all | solution.py:413
  26.0 27.4 %copy-start = (bf16[6,128,256]{2,1,0:T(8,128)(2,1)S(1)}, bf16[6,128,256]{2,1,0:T(8,128)(2,1)}, u32[]{:S(2)}) copy-start(bf16[6,128,256]{2,1,0:T(8,128)(2,1)} %get-tuple-element.57.w_ref) | copy-start | bytes 1179652
  56.3 16.7 %all-to-all-start.2 = ((f32[32,9,2,128]{3,2,1,0:T(2,128)}), f32[32,9,2,128]{3,2,1,0:T(2,128)S(1)}, u32[]{:S(2)}, u32[]{:S(2)}) async-start(f32[32,9,2,128]{3,2,1,0:T(2,128)} %get-tuple-element.59), calls=%async_computation.2 | async-start | bytes 589824 | tf_op jit(solution)/shard_map/all_to_all | solution.py:413
  61.9 9.2 %collective-permute-start = (f32[128,384]{1,0:T(8,128)S(1)}, f32[128,384]{1,0:T(8,128)S(1)}, u32[]{:S(2)}, u32[]{:S(2)}) collective-permute-start(f32[128,384]{1,0:T(8,128)S(1)} %get-tuple-element.61), channel_id=1, source_target_pairs={{0,2},{2,4},{4,6},{6,0},{1,3},{3,5},{5,7},{7,1},{8,10},{10,12},{12... | collective-permute-start | bytes 589832 | tf_op jit(solution)/shard_map/ppermute | solution.py:418
  63.3 9.7 %collective-permute-start.1 = (f32[128,384]{1,0:T(8,128)S(1)}, f32[128,384]{1,0:T(8,128)S(1)}, u32[]{:S(2)}, u32[]{:S(2)}) collective-permute-start(f32[128,384]{1,0:T(8,128)S(1)} %get-tuple-element.62), channel_id=1, source_target_pairs={{0,4},{2,6},{4,0},{6,2},{1,5},{3,7},{5,1},{7,3},{8,12},{10,14},{12... | collective-permute-start | bytes 589832 | tf_op jit(solution)/shard_map/ppermute | solution.py:418
  65.9 7.1 %collective-permute-start.2 = (f32[128,384]{1,0:T(8,128)S(1)}, f32[128,384]{1,0:T(8,128)S(1)}, u32[]{:S(2)}, u32[]{:S(2)}) collective-permute-start(f32[128,384]{1,0:T(8,128)S(1)} %get-tuple-element.63), channel_id=1, source_target_pairs={{0,6},{2,0},{4,2},{6,4},{1,7},{3,1},{5,3},{7,5},{8,14},{10,8},{12,... | collective-permute-start | bytes 589832 | tf_op jit(solution)/shard_map/ppermute | solution.py:418
  73.0 12.8 %copy-start.1 = (bf16[1024,512]{1,0:T(8,128)(2,1)S(1)}, bf16[1024,512]{1,0:T(8,128)(2,1)}, u32[]{:S(2)}) copy-start(bf16[1024,512]{1,0:T(8,128)(2,1)} %get-tuple-element.70.x_ref) | copy-start | bytes 3145732
  73.0 12.8 %copy-start.2 = (bf16[1024,512]{1,0:T(8,128)(2,1)S(1)}, bf16[1024,512]{1,0:T(8,128)(2,1)}, u32[]{:S(2)}) copy-start(bf16[1024,512]{1,0:T(8,128)(2,1)} %get-tuple-element.71.chosen_ref) | copy-start | bytes 3145732
  87.0 8.5 %collective-permute-start.3 = (f32[4,8,16,768]{3,2,1,0:T(8,128)S(1)}, f32[4,8,16,768]{3,2,1,0:T(8,128)S(1)}, u32[]{:S(2)}, u32[]{:S(2)}) collective-permute-start(f32[4,8,16,768]{3,2,1,0:T(8,128)S(1)} %get-tuple-element.78), channel_id=1, source_target_pairs={{0,1},{1,0},{2,3},{3,2},{4,5},{5,4},{6,7},{7,6},{8,9},{9,8},{10,11... | collective-permute-start | bytes 4718600 | tf_op jit(solution)/shard_map/ppermute | solution.py:418
  137.2 15.4 %all-to-all-start.6 = ((f32[8,16,768]{2,1,0:T(8,128)}), f32[8,16,768]{2,1,0:T(8,128)S(1)}, u32[]{:S(2)}, u32[]{:S(2)}) async-start(f32[8,16,768]{2,1,0:T(8,128)} %spread.1), calls=%async_computation.6 | async-start | bytes 786432 | tf_op jit(solution)/shard_map/all_to_all | solution.py:413
Sparse Core Ops, SparseCore 0:
  11.0 54.7 all-gather.2

commit v7 on v6

--- a/solution.py
+++ b/solution.py
@@ -438,9 +438,10 @@
     keep, give = call(weights_kernel, (x, chosen, *first, second), out, "weights")
     (part,) = call(core_sum_kernel, (keep, shift(give, "c", 1)), out[:1], "core_sum")
     (part,) = call(row_sum_kernel, (swap(part, "x"),), [f32(8, 16, 768)], "row_sum")
-    (part,) = call(spread_kernel, (swap(part, "z"),), [f32(8, 16, 768)], "spread")
+    (dx,) = call(frame_gradient_kernel, (dq, dkv, w_qkv), [bf16(BLOCK, 1024)], "frame_gradient", limit=LARGE_VMEM)
+    part, dx = together(swap(part, "z"), dx)
+    (part,) = call(spread_kernel, (part,), [f32(8, 16, 768)], "spread")
     part = swap(part, DP)
-    (dx,) = call(frame_gradient_kernel, (dq, dkv, w_qkv), [bf16(BLOCK, 1024)], "frame_gradient", limit=LARGE_VMEM)
     grad_qkv, grad_out = call(assemble_kernel, (part,), [f32(32, 3 * INNER), f32(32, INNER)], "assemble")
     return dx[None], grad_qkv, grad_out
 

time: 161 us -> 160 us (level)
  waiting for transfers between devices: 17.3 us -> 21.4 us
  blocking collectives: 70.1 us -> 66.2 us
    all_to_all x3, waiting for transfers between devices: 12.3 us -> 16.4 us  [swap(): return lax.all_to_all(a, axes, 0, 0, tiled=True)]
    all_to_all x4, blocking collectives: 70.1 us -> 66.2 us  [swap(): return lax.all_to_all(a, axes, 0, 0, tiled=True)]
where the time goes in v7:
time: 160 us; the launch traced here: 159 us
  blocking collectives  66.2 us (41%)
  starting transfers between devices  34.5 us (22%)
  Pallas kernels  23.2 us (14%)
  waiting for transfers between devices  21.4 us (13%)
  between operations  14.1 us (9%)
    all_to_all x4, blocking collectives, swap(): return lax.all_to_all(a, axes, 0, 0, tiled=True)  66.2 us
    all_to_all x3, starting transfers between devices, swap(): return lax.all_to_all(a, axes, 0, 0, tiled=True)  24 us
    pallas_call x12, Pallas kernels, call(): pl.pallas_call(kernel, in_specs=in_specs or in_vmem(len(args)), out_specs...  23.2 us
    all_to_all x3, waiting for transfers between devices, swap(): return lax.all_to_all(a, axes, 0, 0, tiled=True)  16.4 us
    ppermute x4, starting transfers between devices, shift(): return lax.ppermute(a, axis, [(i, (i + s) % n) for i in range(n)])  10.5 us
    ppermute x4, waiting for transfers between devices, shift(): return lax.ppermute(a, axis, [(i, (i + s) % n) for i in range(n)])  4.93 us
  transfers between devices with their start and end apart: 8, of which 4 were waited for; matrix products, arithmetic and copies ran while one was open for 0% of the time, Pallas kernels for 10%

profile of v7, /device:TPU:1, one launch (start us, length us, event | category | flops | bytes accessed | tf_op | source)
XLA Modules:
  0.0 159.5 jit_solution(13162800112035456292)
XLA Ops:
  7.2 0.0 all-gather.3.cloned.1.call-start
  7.2 3.6 %keys.1 = (bf16[128,768]{1,0:T(8,128)(2,1)S(1)}, bf16[128,768]{1,0:T(8,128)(2,1)S(1)}, f32[32,9,2,128]{3,2,1,0:T(2,128)}, f32[2,128,1024]{2,1,0:T(8,128)}) custom-call(bf16[128,1024]{1,0:T(8,128)(2,1)} %bitcast.4, bf16[128,1024]{1,0:T(8,128)(2,1)} %bitcast.7, bf16[1024,2304]{1,0:T(8,128)(2,1)} %w_ref.1), custom_call_target="tpu_custom_call" | custom-call | tf_op jit(solution)/shard_map/keys/pallas_call | solution.py:85
  10.9 0.0 copy-start.3
  10.9 0.0 all-gather.3.cloned.1.call-update
  10.9 12.0 %all-to-all-start = ((f32[32,9,2,128]{3,2,1,0:T(2,128)}), f32[32,9,2,128]{3,2,1,0:T(2,128)S(1)}, u32[]{:S(2)}, u32[]{:S(2)}) async-start(f32[32,9,2,128]{3,2,1,0:T(2,128)} %get-tuple-element.44), calls=%async_computation | async-start | bytes 589824 | tf_op jit(solution)/shard_map/all_to_all | solution.py:413
  22.9 3.1 %queries.1 = (bf16[128,768]{1,0:T(8,128)(2,1)S(1)}, bf16[128,768]{1,0:T(8,128)(2,1)S(1)}, bf16[6,128,256]{2,1,0:T(8,128)(2,1)}, f32[128,128]{1,0:T(8,128)S(1)}) custom-call(bf16[128,1024]{1,0:T(8,128)(2,1)S(1)} %bitcast.5, bf16[128,1024]{1,0:T(8,128)(2,1)} %bitcast.8, bf16[1024,2304]{1,0:T(8,128)(2,1)} %w_ref.1, bf16[1024,768]{1,0:T(8,128)(2,1)} %wo_hbm.1, ...), custom_call_target="tpu_custom_call" | custom-call | tf_op jit(solution)/shard_map/queries/pallas_call | solution.py:85
  26.1 8.9 %all-to-all-done.in_ref = f32[32,9,2,128]{3,2,1,0:T(2,128)S(1)} async-done(((f32[32,9,2,128]{3,2,1,0:T(2,128)}), f32[32,9,2,128]{3,2,1,0:T(2,128)S(1)}, u32[]{:S(2)}, u32[]{:S(2)}) %all-to-all-start) | async-done | bytes 294944 | tf_op jit(solution)/shard_map/all_to_all | solution.py:413
  35.0 1.1 denominators.1
  36.1 17.3 %all_to_all.35.got_ref = f32[32,24,128]{2,1,0:T(8,128)S(1)} all-to-all(f32[32,24,128]{2,1,0:T(8,128)S(1)} %get-tuple-element.54), channel_id=1, replica_groups=mesh['z'=8,'x'=4,'y'=4,'c'=2] {'z','x'}, dimensions={0} | all-to-all | bytes 786432 | tf_op jit(solution)/shard_map/all_to_all | solution.py:413
  53.4 2.9 %forward.1 = (f32[32,9,2,128]{3,2,1,0:T(2,128)}, bf16[128,768]{1,0:T(8,128)(2,1)S(1)}, bf16[6,256,128]{2,1,0:T(8,128)(2,1)S(1)}, f32[128,384]{1,0:T(8,128)S(1)},...) custom-call(f32[32,24,128]{2,1,0:T(8,128)S(1)} %all_to_all.35.got_ref, ...), custom_call_target="tpu_custom_call" | custom-call | tf_op jit(solution)/shard_map/forward/pallas_call | solution.py:85
  56.3 5.6 %all-to-all-start.2 = ((f32[32,9,2,128]{3,2,1,0:T(2,128)}), f32[32,9,2,128]{3,2,1,0:T(2,128)S(1)}, u32[]{:S(2)}, u32[]{:S(2)}) async-start(f32[32,9,2,128]{3,2,1,0:T(2,128)} %get-tuple-element.60), calls=%async_computation.2 | async-start | bytes 589824 | tf_op jit(solution)/shard_map/all_to_all | solution.py:413
  61.9 1.4 collective-permute-start
  63.3 2.6 %collective-permute-start.1 = (f32[128,384]{1,0:T(8,128)S(1)}, f32[128,384]{1,0:T(8,128)S(1)}, u32[]{:S(2)}, u32[]{:S(2)}) collective-permute-start(f32[128,384]{1,0:T(8,128)S(1)} %get-tuple-element.63), channel_id=1, source_target_pairs={{0,4},{2,6},{4,0},{6,2},{1,5},{3,7},{5,1},{7,3},{8,12},{10,14},{12... | collective-permute-start | bytes 589832 | tf_op jit(solution)/shard_map/ppermute | solution.py:418
  65.9 1.1 collective-permute-start.2
  66.9 4.1 %stage.1 = (bf16[1024,512]{1,0:T(8,128)(2,1)}, bf16[1024,512]{1,0:T(8,128)(2,1)}) custom-call(f32[4,2,128,1024]{3,2,1,0:T(8,128)} %bitcast.6), custom_call_target="tpu_custom_call" | custom-call | tf_op jit(solution)/shard_map/stage/pallas_call | solution.py:85
  71.1 0.0 collective-permute-done.b1_ref
  71.1 1.9 %collective-permute-done.1.b2_ref = f32[128,384]{1,0:T(8,128)S(1)} collective-permute-done((f32[128,384]{1,0:T(8,128)S(1)}, f32[128,384]{1,0:T(8,128)S(1)}, u32[]{:S(2)}, u32[]{:S(2)}) %collective-permute-start.1) | collective-permute-done | bytes 196640 | tf_op jit(solution)/shard_map/ppermute | solution.py:418
  73.0 0.0 collective-permute-done.2.b3_ref
  73.0 0.0 all-to-all-done.2.in_ref
  73.0 0.7 backward.1
  73.6 12.1 %all_to_all.36.got_ref = f32[4,128,384]{2,1,0:T(8,128)S(1)} all-to-all(f32[4,128,384]{2,1,0:T(8,128)S(1)} %get-tuple-element.76), channel_id=1, replica_groups=mesh['z'=8,'x'=4,'y'=4,'c'=2] {'y'}, dimensions={0} | all-to-all | bytes 1572864 | tf_op jit(solution)/shard_map/all_to_all | solution.py:413
  85.7 1.2 weights.1
  87.0 5.5 %collective-permute-start.3 = (f32[4,8,16,768]{3,2,1,0:T(8,128)S(1)}, f32[4,8,16,768]{3,2,1,0:T(8,128)S(1)}, u32[]{:S(2)}, u32[]{:S(2)}) collective-permute-start(f32[4,8,16,768]{3,2,1,0:T(8,128)S(1)} %get-tuple-element.78), channel_id=1, source_target_pairs={{0,1},{1,0},{2,3},{3,2},{4,5},{5,4},{6,7},{7,6},{8,9},{9,8},{10,11... | collective-permute-start | bytes 4718600 | tf_op jit(solution)/shard_map/ppermute | solution.py:418
  92.4 3.0 %collective-permute-done.3.got_ref = f32[4,8,16,768]{3,2,1,0:T(8,128)S(1)} collective-permute-done((f32[4,8,16,768]{3,2,1,0:T(8,128)S(1)}, f32[4,8,16,768]{3,2,1,0:T(8,128)S(1)}, u32[]{:S(2)}, u32[]{:S(2)}) %collective-permute-start.3) | collective-permute-done | bytes 1572896 | tf_op jit(solution)/shard_map/ppermute | solution.py:418
  95.5 0.2 core_sum.1
  95.6 22.9 %all_to_all.37.got_ref = f32[4,8,16,768]{3,2,1,0:T(8,128)S(1)} all-to-all(f32[4,8,16,768]{3,2,1,0:T(8,128)S(1)} %core_sum.1), channel_id=1, replica_groups=mesh['z'=8,'x'=4,'y'=4,'c'=2] {'x'}, dimensions={0} | all-to-all | bytes 3145728 | tf_op jit(solution)/shard_map/all_to_all | solution.py:413
  118.5 0.8 row_sum.1
  119.3 6.4 %all-to-all-start.5 = ((f32[8,16,768]{2,1,0:T(8,128)}), f32[8,16,768]{2,1,0:T(8,128)S(1)}, u32[]{:S(2)}, u32[]{:S(2)}) async-start(f32[8,16,768]{2,1,0:T(8,128)} %row_sum.1), calls=%async_computation.5 | async-start | bytes 786432 | tf_op jit(solution)/shard_map/all_to_all | solution.py:413
  125.7 4.7 %frame_gradient.1 = bf16[128,1024]{1,0:T(8,128)(2,1)} custom-call(bf16[128,768]{1,0:T(8,128)(2,1)S(1)} %get-tuple-element.79.dq_ref, bf16[128,1536]{1,0:T(8,128)(2,1)S(1)} %get-tuple-element.80.dkv_ref, bf16[1024,2304]{1,0:T(8,128)(2,1)} %w_ref.1), custom_call_target="tpu_custom_call" | custom-call | tf_op jit(solution)/shard_map/frame_gradient/pallas_call | solution.py:85
  130.4 7.5 %all-to-all-done.5.got_ref = f32[8,16,768]{2,1,0:T(8,128)S(1)} async-done(((f32[8,16,768]{2,1,0:T(8,128)}), f32[8,16,768]{2,1,0:T(8,128)S(1)}, u32[]{:S(2)}, u32[]{:S(2)}) %all-to-all-start.5) | async-done | bytes 393248 | tf_op jit(solution)/shard_map/all_to_all | solution.py:413
  138.0 13.9 %all_to_all.38.got_ref = f32[8,16,768]{2,1,0:T(8,128)S(1)} all-to-all(f32[8,16,768]{2,1,0:T(8,128)S(1)} %spread.1), channel_id=1, replica_groups=mesh['z'=8,'x'=4,'y'=4,'c'=2] {'y','c'}, dimensions={0} | all-to-all | bytes 786432 | tf_op jit(solution)/shard_map/all_to_all | solution.py:413
  151.9 0.8 assemble.1
  (9 shorter events, 0.1 us)
Async XLA Ops:
  7.2 59.8 %all-gather.3.cloned.1.call-start = ((), (), s32[]{:S(2)}) async-start(), calls=%async_computation.7 | async-start | bytes 5242880 | tf_op jit(solution)/shard_map/all_gather | solution.py:427
  10.9 12.1 %copy-start.3 = (bf16[1,128,1024]{2,1,0:T(8,128)(2,1)S(1)}, bf16[1,128,1024]{2,1,0:T(8,128)(2,1)}, u32[]{:S(2)}) copy-start(bf16[1,128,1024]{2,1,0:T(8,128)(2,1)} %param.4) | copy-start | bytes 786436
  10.9 24.1 %all-to-all-start = ((f32[32,9,2,128]{3,2,1,0:T(2,128)}), f32[32,9,2,128]{3,2,1,0:T(2,128)S(1)}, u32[]{:S(2)}, u32[]{:S(2)}) async-start(f32[32,9,2,128]{3,2,1,0:T(2,128)} %get-tuple-element.44), calls=%async_computation | async-start | bytes 589824 | tf_op jit(solution)/shard_map/all_to_all | solution.py:413
  26.0 27.4 %copy-start = (bf16[6,128,256]{2,1,0:T(8,128)(2,1)S(1)}, bf16[6,128,256]{2,1,0:T(8,128)(2,1)}, u32[]{:S(2)}) copy-start(bf16[6,128,256]{2,1,0:T(8,128)(2,1)} %get-tuple-element.59.w_ref) | copy-start | bytes 1179652
  56.3 16.7 %all-to-all-start.2 = ((f32[32,9,2,128]{3,2,1,0:T(2,128)}), f32[32,9,2,128]{3,2,1,0:T(2,128)S(1)}, u32[]{:S(2)}, u32[]{:S(2)}) async-start(f32[32,9,2,128]{3,2,1,0:T(2,128)} %get-tuple-element.60), calls=%async_computation.2 | async-start | bytes 589824 | tf_op jit(solution)/shard_map/all_to_all | solution.py:413
  61.9 9.2 %collective-permute-start = (f32[128,384]{1,0:T(8,128)S(1)}, f32[128,384]{1,0:T(8,128)S(1)}, u32[]{:S(2)}, u32[]{:S(2)}) collective-permute-start(f32[128,384]{1,0:T(8,128)S(1)} %get-tuple-element.62), channel_id=1, source_target_pairs={{0,2},{2,4},{4,6},{6,0},{1,3},{3,5},{5,7},{7,1},{8,10},{10,12},{12... | collective-permute-start | bytes 589832 | tf_op jit(solution)/shard_map/ppermute | solution.py:418
  63.3 9.7 %collective-permute-start.1 = (f32[128,384]{1,0:T(8,128)S(1)}, f32[128,384]{1,0:T(8,128)S(1)}, u32[]{:S(2)}, u32[]{:S(2)}) collective-permute-start(f32[128,384]{1,0:T(8,128)S(1)} %get-tuple-element.63), channel_id=1, source_target_pairs={{0,4},{2,6},{4,0},{6,2},{1,5},{3,7},{5,1},{7,3},{8,12},{10,14},{12... | collective-permute-start | bytes 589832 | tf_op jit(solution)/shard_map/ppermute | solution.py:418
  65.9 7.1 %collective-permute-start.2 = (f32[128,384]{1,0:T(8,128)S(1)}, f32[128,384]{1,0:T(8,128)S(1)}, u32[]{:S(2)}, u32[]{:S(2)}) collective-permute-start(f32[128,384]{1,0:T(8,128)S(1)} %get-tuple-element.64), channel_id=1, source_target_pairs={{0,6},{2,0},{4,2},{6,4},{1,7},{3,1},{5,3},{7,5},{8,14},{10,8},{12,... | collective-permute-start | bytes 589832 | tf_op jit(solution)/shard_map/ppermute | solution.py:418
  73.0 12.8 %copy-start.1 = (bf16[1024,512]{1,0:T(8,128)(2,1)S(1)}, bf16[1024,512]{1,0:T(8,128)(2,1)}, u32[]{:S(2)}) copy-start(bf16[1024,512]{1,0:T(8,128)(2,1)} %get-tuple-element.68.x_ref) | copy-start | bytes 3145732
  73.0 12.8 %copy-start.2 = (bf16[1024,512]{1,0:T(8,128)(2,1)S(1)}, bf16[1024,512]{1,0:T(8,128)(2,1)}, u32[]{:S(2)}) copy-start(bf16[1024,512]{1,0:T(8,128)(2,1)} %get-tuple-element.69.chosen_ref) | copy-start | bytes 3145732
  87.0 8.5 %collective-permute-start.3 = (f32[4,8,16,768]{3,2,1,0:T(8,128)S(1)}, f32[4,8,16,768]{3,2,1,0:T(8,128)S(1)}, u32[]{:S(2)}, u32[]{:S(2)}) collective-permute-start(f32[4,8,16,768]{3,2,1,0:T(8,128)S(1)} %get-tuple-element.78), channel_id=1, source_target_pairs={{0,1},{1,0},{2,3},{3,2},{4,5},{5,4},{6,7},{7,6},{8,9},{9,8},{10,11... | collective-permute-start | bytes 4718600 | tf_op jit(solution)/shard_map/ppermute | solution.py:418
  119.3 18.6 %all-to-all-start.5 = ((f32[8,16,768]{2,1,0:T(8,128)}), f32[8,16,768]{2,1,0:T(8,128)S(1)}, u32[]{:S(2)}, u32[]{:S(2)}) async-start(f32[8,16,768]{2,1,0:T(8,128)} %row_sum.1), calls=%async_computation.5 | async-start | bytes 786432 | tf_op jit(solution)/shard_map/all_to_all | solution.py:413
Sparse Core Ops, SparseCore 0:
  11.0 54.7 all-gather.2
